TPU v7x, 32 devices: a whole 2x2x4 slice. The times are simulated.
32 devices in a mesh: grp: 2 (over x), refl: 16 (over z, y, core).
Axes of the slice: x: 2, y: 2, z: 4, core: 2. Of those that a mesh axis runs over, the one named last changes fastest.
Arguments:
- feed_plane: float32 [4, 2048], P('grp', 'refl'), parts along dimension 0, may hold values from -3 to 3
- feed_height: float32 [4096], P(('grp', 'refl')), parts along dimension 0, may hold values from 20 to 24
- feed_weights: bfloat16 [2048, 256], P('refl', 'grp'), parts along dimension 1, may hold values from -0.125 to 0.125
- point_plane: float32 [4, 4096], P('grp', 'refl'), parts along dimension 0, may hold values from -35 to 35
- point_height: float32 [8192], P(('grp', 'refl')), parts along dimension 0, may hold values from 0 to 4
- patch_factor: float32 [8192], P(('grp', 'refl')), parts along dimension 0, may hold values from 0.3 to 3
- direction_cosines: float32 [2, 2048], P(None, 'refl'), may hold values from -0.3 to 0.3
Outputs:
- pattern: float32 [2048, 256], P('refl', 'grp'), parts along dimension 1
There are 2 independent parts, one for each index of `grp`. A program takes and returns all parts, laid end to end along the dimension named above; an argument that names none is the same for every part. Nothing has to cross between parts.
All inputs are finite; a program needn't handle non-finite values.
Results may differ from a plain program's by a relative error of at most 0.0047.
Values may be sent and summed in bfloat16 or wider, within the bound.
No kernel may reach another device: no remote copies, remote signals or barrier semaphores. Data moves between devices by JAX's collectives and lax.ppermute only.
A program may use at most 64 MiB of HBM per device.

v0:
```python
import math

import jax
import jax.numpy as jnp
from jax import lax
from jax.sharding import PartitionSpec as P

TWO_PI = 2.0 * math.pi
RANGE_REF = 20.0


def rotate(columns):
    half = columns.shape[1] // 2
    return jnp.concatenate([-columns[:, half:], columns[:, :half]], axis=1)


def green_tile(point_plane, point_height, feed_plane, feed_height):
    across = point_plane[0][:, None] - feed_plane[0][None, :]
    along = point_plane[1][:, None] - feed_plane[1][None, :]
    height = feed_height[None, :] - point_height[:, None]
    squared = across * across + along * along + height * height
    distance = jnp.sqrt(squared)
    amplitude = RANGE_REF * height / squared
    turning = TWO_PI * distance
    return (
        (amplitude * jnp.cos(turning)).astype(jnp.bfloat16),
        (-amplitude * jnp.sin(turning)).astype(jnp.bfloat16),
    )


def incident_rows(point_plane, point_height, feed_plane, feed_height, weights, weights_turned):
    in_phase, quadrature = green_tile(point_plane, point_height, feed_plane, feed_height)
    return jnp.dot(in_phase, weights, preferred_element_type=jnp.float32) + jnp.dot(
        quadrature, weights_turned, preferred_element_type=jnp.float32
    )


def far_kernel(cosines, point_plane, point_height):
    normal = jnp.sqrt(1.0 - cosines[0] * cosines[0] - cosines[1] * cosines[1])
    turning = TWO_PI * (
        cosines[0][:, None] * point_plane[0][None, :]
        + cosines[1][:, None] * point_plane[1][None, :]
        + normal[:, None] * point_height[None, :]
    )
    return (jnp.cos(turning).astype(jnp.bfloat16), jnp.sin(turning).astype(jnp.bfloat16))


def radiate_rows(cosines, point_plane, point_height, currents, currents_turned):
    in_phase, quadrature = far_kernel(cosines, point_plane, point_height)
    return jnp.dot(in_phase, currents, preferred_element_type=jnp.float32) + jnp.dot(
        quadrature, currents_turned, preferred_element_type=jnp.float32
    )


def per_device(
    feed_plane,
    feed_height,
    feed_weights,
    point_plane,
    point_height,
    patch_factor,
    direction_cosines,
):
    local_points = point_plane.shape[1]
    source_plane, source_height = (
        lax.all_gather(feed_plane, "refl", axis=1, tiled=True),
        lax.all_gather(feed_height, "refl", axis=0, tiled=True),
    )
    segment = lax.all_gather(feed_weights, "refl", axis=0, tiled=True)
    part_plane = source_plane
    part_height = source_height
    incident = incident_rows(
        point_plane, point_height, part_plane, part_height, segment, rotate(segment)
    )
    norm_scale = 1.0 / math.sqrt(local_points * lax.axis_size("refl"))
    currents = (incident * (patch_factor * norm_scale)[:, None]).astype(jnp.bfloat16)
    radiator_plane, radiator_height = (
        lax.all_gather(point_plane, "refl", axis=1, tiled=True),
        lax.all_gather(point_height, "refl", axis=0, tiled=True),
    )
    segment = lax.all_gather(currents, "refl", axis=0, tiled=True)
    part_plane = radiator_plane
    part_height = radiator_height
    return radiate_rows(direction_cosines, part_plane, part_height, segment, rotate(segment))


def solution(mesh):
    in_specs = (
        P("grp", "refl"),
        P(("grp", "refl")),
        P("refl", "grp"),
        P("grp", "refl"),
        P(("grp", "refl")),
        P(("grp", "refl")),
        P(None, "refl"),
    )
    out_specs = P("refl", "grp")
    return jax.shard_map(
        per_device, mesh=mesh, in_specs=in_specs, out_specs=out_specs, check_vma=False
    )
```

profile of v0, /device:TPU:1, one launch (start us, length us, event | category | flops | bytes accessed | tf_op | source)
XLA Modules:
  0.0 149.4 jit_solution(372851326946409768)
XLA Ops:
  6.5 0.0 all-gather.4.cloned.1.call-start
  6.5 0.7 broadcast_multiply_fusion
  7.2 0.8 fusion.36
  8.0 23.0 %all-gather.1 = f32[16,1,128]{2,1,0:T(1,128)S(1)} all-gather(f32[1,1,128]{2,1,0:T(1,128)} %bitcast.37), channel_id=1, replica_groups=mesh['grp'=2,'refl'=16] {'refl'}, dimensions={0}, use_global_device_ids=true | all-gather | bytes 8704 | tf_op jit(solution)/shard_map/all_gather | solution.py:67
  31.0 17.7 %all_gather.21 = f32[2,2048]{1,0:T(2,128)S(1)} all-gather(f32[2,128]{1,0:T(2,128)} %param.7), channel_id=1, replica_groups=mesh['grp'=2,'refl'=16] {'refl'}, dimensions={1}, use_global_device_ids=true | all-gather | bytes 17408 | tf_op jit(solution)/shard_map/all_gather | solution.py:66
  48.6 20.6 %all_gather.22 = bf16[2048,128]{1,0:T(8,128)(2,1)S(1)} all-gather(bf16[128,128]{1,0:T(8,128)(2,1)} %param.9), channel_id=1, replica_groups=mesh['grp'=2,'refl'=16] {'refl'}, dimensions={0}, use_global_device_ids=true | all-gather | bytes 557056 | tf_op jit(solution)/shard_map/all_gather | solution.py:69
  69.2 0.0 copy-start.2
  69.2 0.2 slice_negate_fusion.1
  69.5 0.4 copy-done.2
  69.9 8.3 %fusion.22 = f32[256,128]{1,0:T(8,128)S(1)} fusion(bf16[2048,128]{1,0:T(8,128)(2,1)S(1)} %all_gather.22, f32[2048]{0:T(1024)S(1)} %bitcast.30, f32[256]{0:T(256)S(1)} %bitcast.35, f32[2048]{0:T(1024)S(1)} %bitcast.28, f32[256]{0:T(256)S(1)} %bitcast.33, f32[256]{0:T(256)S(1)} %copy-done.2, f32[2048]{0:T(1024)S(1)} %bitcast.26), kind=kOutput, calls=%fused_computation.33 | convolution fusion | flops 141033472 | bytes 683008 | tf_op jit(solution)/shard_map/dot_general | solution.py:33
  78.2 0.0 copy-start.1
  78.2 0.0 copy-start.3
  78.2 9.6 %fusion.3 = bf16[256,128]{1,0:T(8,128)(2,1)} fusion(f32[256,128]{1,0:T(8,128)S(1)} %fusion.22, f32[2048]{0:T(1024)S(1)} %bitcast.31, f32[256]{0:T(256)S(1)} %bitcast.36, f32[2048]{0:T(1024)S(1)} %bitcast.29, f32[256]{0:T(256)S(1)} %bitcast.34, f32[256]{0:T(256)S(1)} %copy-done.2, f32[2048]{0:T(1024)S(1)} %bitcast.27, ...), kind=kOutput, calls=%fused_computation.12 | convolution fusion | flops 142704640 | bytes 749568 | tf_op jit(solution)/shard_map/dot_general | solution.py:33
  87.8 0.0 all-gather.4.cloned.1.call-update
  87.8 17.4 %all-gather = f32[16,1,256]{2,1,0:T(1,128)S(1)} all-gather(f32[1,1,256]{2,1,0:T(1,128)S(1)} %bitcast.32), channel_id=1, replica_groups=mesh['grp'=2,'refl'=16] {'refl'}, dimensions={0}, use_global_device_ids=true | all-gather | bytes 17408 | tf_op jit(solution)/shard_map/all_gather | solution.py:79
  105.3 0.0 copy-done.1
  105.3 18.9 %all_gather.18 = f32[2,4096]{1,0:T(2,128)S(1)} all-gather(f32[2,256]{1,0:T(2,128)S(1)} %copy-done.1), channel_id=1, replica_groups=mesh['grp'=2,'refl'=16] {'refl'}, dimensions={1}, use_global_device_ids=true | all-gather | bytes 34816 | tf_op jit(solution)/shard_map/all_gather | solution.py:78
  124.1 0.0 copy-done.3
  124.2 0.0 all-gather.4.cloned.1.call-done
  124.2 0.0 copy-start
  124.2 2.1 %slice_negate_fusion = (bf16[4096,64]{1,0:T(8,128)(2,1)S(1)}, bf16[4096,64]{1,0:T(8,128)(2,1)S(1)}) fusion(bf16[4096,128]{1,0:T(8,128)(2,1)} %all-gather.4.cloned.1.call-done), kind=kLoop, calls=%fused_computation.15 | loop fusion | flops 262144 | bytes 2097152 | tf_op jit(solution)/shard_map/neg | solution.py:14
  126.3 0.0 copy-done
  126.3 7.4 %fusion.4 = f32[128,128]{1,0:T(8,128)S(1)} fusion(bf16[4096,128]{1,0:T(8,128)(2,1)S(1)} %copy-done, f32[4096]{0:T(1024)S(1)} %bitcast.20, f32[128]{0:T(128)S(1)} %subtract_sqrt_fusion, f32[4096]{0:T(1024)S(1)} %bitcast.24, f32[128]{0:T(128)S(1)} %get-tuple-element.16, f32[4096]{0:T(1024)S(1)} %bitcast.22, f32[128]{0:T(128)S(1)} %get-tuple-element.15), kind=kOutput, calls=%fused_computation.14 | convolution fusion | flops 137887744 | bytes 1164800 | tf_op jit(solution)/shard_map/dot_general | solution.py:50
  133.7 8.9 %convolution_add_fusion.1 = f32[128,128]{1,0:T(8,128)} fusion(f32[128,128]{1,0:T(8,128)S(1)} %fusion.4, bf16[4096,64]{1,0:T(8,128)(2,1)S(1)} %get-tuple-element.6, bf16[4096,64]{1,0:T(8,128)(2,1)S(1)} %get-tuple-element.5, f32[4096]{0:T(1024)S(1)} %bitcast.21, f32[128]{0:T(128)S(1)} %subtract_sqrt_fusion, f32[4096]{0:T(1024)S(1)} %bitcast.25, ...), kind=kOutput, calls=%fused_computation.13 | convolution fusion | flops 140001280 | bytes 1230336 | tf_op jit(solution)/shard_map/dot_general | solution.py:50
  (4 shorter events, 0.1 us)
Async XLA Ops:
  6.5 117.7 %all-gather.4.cloned.1.call-start = ((), (), s32[]{:S(2)}) async-start(), calls=%async_computation | async-start | bytes 1114112 | tf_op jit(solution)/shard_map/all_gather | solution.py:81
  69.2 0.7 copy-start.2
  78.2 27.0 %copy-start.1 = (f32[2,256]{1,0:T(2,128)S(1)}, f32[2,256]{1,0:T(2,128)}, u32[]{:S(2)}) copy-start(f32[2,256]{1,0:T(2,128)} %param.10) | copy-start | bytes 6148
  78.2 45.9 %copy-start.3 = (f32[2,128]{1,0:T(2,128)S(1)}, f32[2,128]{1,0:T(2,128)}, u32[]{:S(2)}) copy-start(f32[2,128]{1,0:T(2,128)} %param.13) | copy-start | bytes 3076
  124.2 2.1 %copy-start = (bf16[4096,128]{1,0:T(8,128)(2,1)S(1)}, bf16[4096,128]{1,0:T(8,128)(2,1)}, u32[]{:S(2)}) copy-start(bf16[4096,128]{1,0:T(8,128)(2,1)} %all-gather.4.cloned.1.call-done) | copy-start | bytes 3145732
Sparse Core Ops, SparseCore 0:
  87.9 35.1 all-gather.3
where the time goes:
time: 150 us; the launch traced here: 149 us
  blocking collectives  97.6 us (65%)
  matrix products  34.1 us (23%)
  between operations  13.5 us (9%)
  other arithmetic  2.98 us (2%)
    all_gather x1, blocking collectives, per_device(): lax.all_gather(feed_height, 'refl', axis=0, tiled=True)  23 us
    all_gather x1, blocking collectives, per_device(): segment = lax.all_gather(feed_weights, 'refl', axis=0, tiled=True)  20.6 us
    all_gather x1, blocking collectives, per_device(): lax.all_gather(point_plane, 'refl', axis=1, tiled=True)  18.9 us
    all_gather x1, blocking collectives, per_device(): lax.all_gather(feed_plane, 'refl', axis=1, tiled=True)  17.7 us
    all_gather x1, blocking collectives, per_device(): lax.all_gather(point_height, 'refl', axis=0, tiled=True)  17.4 us
    dot_general x1, matrix products, incident_rows(): jnp.dot(quadrature, weights_turned, preferred_element_type=jnp.float32)  9.56 us
    dot_general x1, matrix products, radiate_rows(): jnp.dot(quadrature, currents_turned, preferred_element_type=jnp.float32)  8.86 us
    dot_general x1, matrix products, incident_rows(): jnp.dot(in_phase, weights, preferred_element_type=jnp.float32)  8.31 us
  transfers between devices with their start and end apart: 1, of which 0 were waited for; matrix products, arithmetic and copies ran while one was open for 0% of the time, Pallas kernels for 0%

commit v1 on v0

v1 whole, which is shorter than its diff:
```python
import math

import jax
import jax.numpy as jnp
from jax import lax
from jax.experimental import pallas as pl
from jax.experimental.pallas import tpu as pltpu
from jax.sharding import PartitionSpec as P

RANGE_REF = 20.0
F32, BF16 = jnp.float32, jnp.bfloat16

SIN_HALF = (3.1415902835895886, -5.167407697719414, 2.544020810735872, -0.5594899090940457)
COS_HALF = (0.9999932952798736, -4.933938014977294, 4.041283824377777, -1.222127057577997)

COORDS = 5
PACK_ROWS = 16


def horner(square, terms, scale):
    total = jnp.float32(terms[-1] * scale)
    for term in terms[-2::-1]:
        total = total * square + jnp.float32(term * scale)
    return total


def circle(turns, gain):
    part = turns - jnp.round(turns)
    square = part * part
    root = math.sqrt(2.0 * abs(gain))
    half_sin = part * horner(square, SIN_HALF, root)
    half_cos = horner(square, COS_HALF, 2.0 * gain / root)
    return abs(gain) - half_sin * half_sin, half_sin * half_cos


def turned(columns):
    half = columns.shape[1] // 2
    return jnp.concatenate([-columns[:, half:], columns[:, :half]], axis=1)


def pack_body(weights, feed_plane, feed_height, cosines, message):
    rows = weights.shape[0]
    message[:rows, :] = weights[...]
    lanes = weights.shape[1]
    exact = jnp.concatenate([feed_plane[...], feed_height[...], cosines[...]], axis=0)
    high = exact.astype(BF16)
    rest = exact - high.astype(F32)
    middle = rest.astype(BF16)
    low = (rest - middle.astype(F32)).astype(BF16)
    pad = jnp.zeros((PACK_ROWS - 3 * COORDS, lanes), F32)
    message[rows:, :] = jnp.concatenate(
        [high.astype(F32), middle.astype(F32), low.astype(F32), pad], axis=0
    ).astype(BF16)


def unpack(tail):
    tail = tail.astype(F32)
    return (tail[:COORDS] + tail[COORDS : 2 * COORDS]) + tail[2 * COORDS : 3 * COORDS]


def fill_point_columns(points, columns, base):
    lanes = points.shape[1]
    up = points[...].T
    for at in range(2):
        columns[base + at * lanes : base + (at + 1) * lanes, :] = jnp.concatenate(
            [up[:, 2 * k + at : 2 * k + at + 1] for k in range(4)], axis=1
        )


def green_body(has_base, *refs):
    own_points, far_points, messages = refs[:3]
    base = refs[3] if has_base else None
    outs = refs[4:-6] if has_base else refs[3:-6]
    columns, rows, weights, weights_turned, green_re, green_im = refs[-6:]
    count, height, lanes = messages.shape
    sources = height - PACK_ROWS
    half = 2 * lanes
    fill_point_columns(own_points, columns, 0)
    fill_point_columns(far_points, columns, half)
    for at in range(count):
        where = slice(at * sources, (at + 1) * sources)
        rows[0:COORDS, where] = unpack(messages[at, sources:, :])
        block = messages[at, :sources, :]
        weights[where, :] = block
        weights_turned[where, :] = turned(block)
    tile = 16

    def one(at, carry):
        here = pl.ds(pl.multiple_of(at * tile, tile), tile)
        across = columns[here, 0:1] - rows[0:1, :]
        along = columns[here, 1:2] - rows[1:2, :]
        height = rows[2:3, :] - columns[here, 2:3]
        squared = across * across + along * along + height * height
        inverse = lax.rsqrt(squared)
        cosine, sine = circle(squared * inverse, -RANGE_REF)
        amplitude = height * (inverse * inverse)
        green_re[here, :] = (amplitude * cosine).astype(BF16)
        green_im[here, :] = (amplitude * sine).astype(BF16)
        return carry

    lax.fori_loop(0, green_re.shape[0] // tile, one, 0, unroll=2)
    total = jnp.dot(green_re[...], weights[...], preferred_element_type=F32) + jnp.dot(
        green_im[...], weights_turned[...], preferred_element_type=F32
    )
    if has_base:
        total = total + base[...]
    for out in outs:
        out[...] = total.astype(out.dtype)


def kernel_body(own_points, far_points, tails, kernel_re, kernel_im, columns, rows):
    count, _, lanes = tails.shape
    half = 2 * lanes
    for at in range(count):
        uv = unpack(tails[at])[3:5]
        normal = jnp.sqrt(1.0 - uv[0:1] * uv[0:1] - uv[1:2] * uv[1:2])
        pad = jnp.zeros((5, lanes), F32)
        columns[at * lanes : (at + 1) * lanes, :] = jnp.concatenate([uv, normal, pad], axis=0).T
    for base, points in ((0, own_points), (half, far_points)):
        for k in range(3):
            for at in range(2):
                rows[k : k + 1, base + at * lanes : base + (at + 1) * lanes] = points[
                    2 * k + at : 2 * k + at + 1, :
                ]
    tile = 16

    def one(at, carry):
        here = pl.ds(pl.multiple_of(at * tile, tile), tile)
        turns = (
            columns[here, 0:1] * rows[0:1, :]
            + columns[here, 1:2] * rows[1:2, :]
            + columns[here, 2:3] * rows[2:3, :]
        )
        cosine, sine = circle(turns, 1.0)
        kernel_re[here, :] = cosine.astype(BF16)
        kernel_im[here, :] = sine.astype(BF16)
        return carry

    lax.fori_loop(0, kernel_re.shape[0] // tile, one, 0, unroll=2)


def currents_body(scale, mine, theirs, own_points, far_points, currents, columns):
    half = mine.shape[0] // 2
    fill_point_columns(own_points, columns, 0)
    fill_point_columns(far_points, columns, half)
    for here, there in ((slice(0, half), slice(half, None)), (slice(half, None), slice(0, half))):
        field = mine[here, :] + theirs[there, :].astype(F32)
        currents[here, :] = (field * (columns[here, 3:4] * scale)).astype(BF16)


def radiate_body(kernel_re, kernel_im, currents, out):
    held = currents[...]
    out[...] = (
        jnp.dot(kernel_re[...], held, preferred_element_type=F32)
        + jnp.dot(kernel_im[...], turned(held), preferred_element_type=F32)
    ).astype(out.dtype)


def fold_body(mine, theirs, kept, sent):
    first = kept.shape[0]
    total = mine[...] + theirs[...].astype(F32)
    kept[...] = total[:first]
    sent[...] = total[first:].astype(BF16)


def finish_body(kept, *refs):
    total = kept[...]
    for ref in refs[:-1]:
        total = total + ref[...].astype(F32)
    refs[-1][...] = total


def call(body, outs, scratch=(), flops=0, trans=0):
    return pl.pallas_call(
        body,
        out_shape=[jax.ShapeDtypeStruct(*out) for out in outs],
        scratch_shapes=list(scratch),
        compiler_params=pltpu.CompilerParams(vmem_limit_bytes=32 * 1024 * 1024),
        cost_estimate=pl.CostEstimate(flops=flops, bytes_accessed=1 << 20, transcendentals=trans),
    )


def per_device(
    feed_plane,
    feed_height,
    feed_weights,
    point_plane,
    point_height,
    patch_factor,
    direction_cosines,
):
    size = lax.axis_size("refl")
    line = size // 4
    sources, lanes = feed_weights.shape
    local_points = point_height.shape[0]
    half_points = 2 * local_points
    directions = direction_cosines.shape[1]

    def pairs(step):
        out = []
        for at in range(size):
            row, place = divmod(at, 4)
            far, near = divmod(step, 4)
            to = (row ^ far) if line & (line - 1) == 0 else (row + far) % line
            out.append((at, to * 4 + (place ^ near)))
        return out

    def swap(x, step, back=False):
        links = pairs(step)
        return lax.ppermute(x, "refl", [(b, a) for a, b in links] if back else links)

    message = call(pack_body, [((sources + PACK_ROWS, lanes), BF16)])(
        feed_weights, feed_plane, feed_height[None, :], direction_cosines
    )[0]
    points = jnp.concatenate(
        [
            point_plane.reshape(4, lanes),
            point_height.reshape(2, lanes),
            patch_factor.reshape(2, lanes),
        ],
        axis=0,
    )
    far_points = swap(points, 2)
    near_messages = jnp.stack([message] + [swap(message, 4 * k) for k in range(1, line)])
    side_messages = swap(near_messages, 1)

    part = line * sources
    elements = half_points * part
    scratch = [
        pltpu.VMEM((half_points, 4), F32),
        pltpu.VMEM((8, part), F32),
        pltpu.VMEM((part, lanes), BF16),
        pltpu.VMEM((part, lanes), BF16),
        pltpu.VMEM((half_points, part), BF16),
        pltpu.VMEM((half_points, part), BF16),
    ]
    first = call(
        lambda *refs: green_body(False, *refs), [((half_points, lanes), F32)], scratch, 40 * elements
    )(points, far_points, near_messages)[0]
    mine, told = call(
        lambda *refs: green_body(True, *refs),
        [((half_points, lanes), F32), ((half_points, lanes), BF16)],
        scratch,
        40 * elements,
    )(points, far_points, side_messages, first)
    theirs = swap(told, 2)

    def kernels(messages):
        count = line * directions
        return call(
            kernel_body,
            [((count, half_points), BF16), ((count, half_points), BF16)],
            [pltpu.VMEM((count, 8), F32), pltpu.VMEM((8, half_points), F32)],
            30 * count * half_points,
        )(points, far_points, messages[:, sources:, :])

    side_re, side_im = kernels(side_messages)
    near_re, near_im = kernels(near_messages)
    scale = 1.0 / math.sqrt(local_points * size)
    currents = call(
        lambda *refs: currents_body(scale, *refs),
        [((half_points, lanes), BF16)],
        [pltpu.VMEM((half_points, 4), F32)],
    )(mine, theirs, points, far_points)[0]

    def radiate(re, im, dtype):
        return call(radiate_body, [((line * directions, lanes), dtype)])(re, im, currents)[0]

    given = swap(radiate(side_re, side_im, BF16), 1)
    kept, sent = call(
        fold_body, [((directions, lanes), F32), (((line - 1) * directions, lanes), BF16)]
    )(radiate(near_re, near_im, F32), given)
    sent = sent.reshape(line - 1, directions, lanes)
    arrived = [swap(sent[k - 1], 4 * k, back=True) for k in range(1, line)]
    return call(finish_body, [((directions, lanes), F32)])(kept, *arrived)[0]


def solution(mesh):
    in_specs = (
        P("grp", "refl"),
        P(("grp", "refl")),
        P("refl", "grp"),
        P("grp", "refl"),
        P(("grp", "refl")),
        P(("grp", "refl")),
        P(None, "refl"),
    )
    out_specs = P("refl", "grp")
    return jax.shard_map(
        per_device, mesh=mesh, in_specs=in_specs, out_specs=out_specs, check_vma=False
    )
```

time: 150 us -> 40.3 us (0.27)
  blocking collectives: 97.6 us -> 0 us
  matrix products: 34.1 us -> 0 us
  starting transfers between devices: 0.01 us -> 15.9 us
  between operations: 13.5 us -> 0.1 us
  Pallas kernels: 0 us -> 12.8 us
  waiting for transfers between devices: 0.04 us -> 7.78 us
  other arithmetic: 2.98 us -> 0.03 us
  local copies, waits for them, and re-layouts: 1.27 us -> 2.84 us
    all_gather x5 -> x0, blocking collectives: 97.6 us -> none  [the longest x1 23 us: per_device(): lax.all_gather(feed_height, 'refl', axis=0, tiled=True)]
    dot_general x4 -> x0, matrix products: 34.1 us -> none  [the longest x1 9.56 us: incident_rows(): jnp.dot(quadrature, weights_turned, preferred_element_type=jnp.float32)]
    ppermute x0 -> x10, starting transfers between devices: none -> 15.9 us  [swap(): lax.ppermute(x, 'refl', [(b, a) for a, b in links] if back else links)]
    pallas_call x0 -> x10, Pallas kernels: none -> 12.8 us  [the longest x2 4.43 us: kernels(): call(kernel_body, [((count, half_points), BF16), ((count, half_points), B...]
    ppermute x0 -> x10, waiting for transfers between devices: none -> 7.78 us  [swap(): lax.ppermute(x, 'refl', [(b, a) for a, b in links] if back else links)]
    unnamed x8 -> x14, local copies, waits for them, and re-layouts: 0.46 us -> 2.81 us
    neg x2 -> x0, other arithmetic: 2.29 us -> none  [rotate(): return jnp.concatenate([-columns[:, half:], columns[:, :half]], axis=1)]
  transfers between devices with their start and end apart: 1 -> 10, of which waited for: 0 -> 7; matrix products, arithmetic and copies ran while one was open for 0% -> 0% of each run, Pallas kernels for 0% -> 20%
where the time goes in v1:
time: 40.3 us; the launch traced here: 39.5 us
  starting transfers between devices  15.9 us (39%)
  Pallas kernels  12.8 us (32%)
  waiting for transfers between devices  7.78 us (19%)
  local copies, waits for them, and re-layouts  2.84 us (7%)
    ppermute x10, starting transfers between devices, swap(): lax.ppermute(x, 'refl', [(b, a) for a, b in links] if back else links)  15.9 us
    ppermute x10, waiting for transfers between devices, swap(): lax.ppermute(x, 'refl', [(b, a) for a, b in links] if back else links)  7.78 us
    pallas_call x2, Pallas kernels, kernels(): call(kernel_body, [((count, half_points), BF16), ((count, half_points), B...  4.43 us
    pallas_call x1, Pallas kernels, per_device(): call(lambda *refs: green_body(True, *refs), [((half_points, lanes), F32),...  3.13 us
    pallas_call x1, Pallas kernels, per_device(): call(lambda *refs: green_body(False, *refs), [((half_points, lanes), F32)...  3.13 us
    unnamed x14, local copies, waits for them, and re-layouts  2.81 us
    pallas_call x2, Pallas kernels, radiate(): call(radiate_body, [((line * directions, lanes), dtype)])(re, im, currents)  0.99 us
  transfers between devices with their start and end apart: 10, of which 7 were waited for; matrix products, arithmetic and copies ran while one was open for 0% of the time, Pallas kernels for 20%

profile of v1, /device:TPU:1, one launch (start us, length us, event | category | flops | bytes accessed | tf_op | source)
XLA Modules:
  0.0 39.5 jit_solution(10277936695767582554)
XLA Ops:
  0.0 0.0 copy-start.3
  0.0 0.0 copy-start.1
  0.0 0.7 %copy-done.3 = f32[128]{0:T(128)S(1)} copy-done((f32[128]{0:T(128)S(1)}, f32[128]{0:T(128)}, u32[]{:S(2)}) %copy-start.3) | copy-done | bytes 536
  0.7 0.0 copy-done.1
  0.7 0.0 copy-start
  0.7 0.8 %copy-done = bf16[128,128]{1,0:T(8,128)(2,1)S(1)} copy-done((bf16[128,128]{1,0:T(8,128)(2,1)S(1)}, bf16[128,128]{1,0:T(8,128)(2,1)}, u32[]{:S(2)}) %copy-start) | copy-done | bytes 32792
  1.5 0.0 copy-start.2
  1.5 0.7 %copy-done.2 = f32[2,128]{1,0:T(2,128)S(1)} copy-done((f32[2,128]{1,0:T(2,128)S(1)}, f32[2,128]{1,0:T(2,128)}, u32[]{:S(2)}) %copy-start.2) | copy-done | bytes 1048
  2.1 4.2 %collective-permute-start.3 = (bf16[144,128]{1,0:T(8,128)(2,1)S(1)}, bf16[144,128]{1,0:T(8,128)(2,1)S(1)}, u32[]{:S(2)}, u32[]{:S(2)}) collective-permute-start(bf16[144,128]{1,0:T(8,128)(2,1)S(1)} %shard_map.73), channel_id=1, source_target_pairs={{0,12},{1,13},{2,14},{3,15},{4,8},{5,9},{6,10},{7,11},{8,4},{9,5},... | collective-permute-start | bytes 110600 | tf_op jit(solution)/shard_map/ppermute | solution.py:210
  6.4 0.0 collective-permute-start.2
  6.4 0.4 collective-permute-start.1
  6.7 1.0 %collective-permute-done.3 = bf16[144,128]{1,0:T(8,128)(2,1)S(1)} collective-permute-done((bf16[144,128]{1,0:T(8,128)(2,1)S(1)}, bf16[144,128]{1,0:T(8,128)(2,1)S(1)}, u32[]{:S(2)}, u32[]{:S(2)}) %collective-permute-start.3) | collective-permute-done | bytes 36896 | tf_op jit(solution)/shard_map/ppermute | solution.py:210
  7.7 2.4 %collective-permute-done.2 = bf16[144,128]{1,0:T(8,128)(2,1)S(1)} collective-permute-done((bf16[144,128]{1,0:T(8,128)(2,1)S(1)}, bf16[144,128]{1,0:T(8,128)(2,1)S(1)}, u32[]{:S(2)}, u32[]{:S(2)}) %collective-permute-start.2) | collective-permute-done | bytes 36896 | tf_op jit(solution)/shard_map/ppermute | solution.py:210
  10.1 0.0 collective-permute-done.1
  10.1 0.0 copy-start.4
  10.1 2.2 %collective-permute-start.4 = (bf16[4,144,128]{2,1,0:T(8,128)(2,1)S(1)}, bf16[4,144,128]{2,1,0:T(8,128)(2,1)S(1)}, u32[]{:S(2)}, u32[]{:S(2)}) collective-permute-start(bf16[4,144,128]{2,1,0:T(8,128)(2,1)S(1)} %pad_maximum_fusion.refs_2_), channel_id=1, source_target_pairs={{0,1},{1,0},{2,3},{3,2},{4,5},{5,4},{6,7},{7,6},{8,9},{9,8},{10,11... | collective-permute-start | bytes 442376 | tf_op jit(solution)/shard_map/ppermute | solution.py:210
  12.3 0.0 copy-done.4
  12.3 0.0 copy-start.6
  12.3 0.0 copy-start.5
  12.3 0.7 %copy-done.6 = f32[256]{0:T(256)S(1)} copy-done((f32[256]{0:T(256)S(1)}, f32[256]{0:T(256)}, u32[]{:S(2)}) %copy-start.6) | copy-done | bytes 1048
  13.0 0.0 copy-done.5
  13.0 1.3 %collective-permute-start = (f32[8,128]{1,0:T(8,128)S(1)}, f32[8,128]{1,0:T(8,128)S(1)}, u32[]{:S(2)}, u32[]{:S(2)}) collective-permute-start(f32[8,128]{1,0:T(8,128)S(1)} %pad_maximum_fusion.1.own_points.refs_0_.refs_2_), channel_id=1, source_target_pairs={{0,2},{1,3},{2,0},{3,1},{4,6},{5,7},{6,4},{7,5},{8,10},{9,11},{10,... | collective-permute-start | bytes 12296 | tf_op jit(solution)/shard_map/ppermute | solution.py:210
  14.3 1.2 %collective-permute-done.far_points.refs_1_.refs_3_ = f32[8,128]{1,0:T(8,128)S(1)} collective-permute-done((f32[8,128]{1,0:T(8,128)S(1)}, f32[8,128]{1,0:T(8,128)S(1)}, u32[]{:S(2)}, u32[]{:S(2)}) %collective-permute-start) | collective-permute-done | bytes 4128 | tf_op jit(solution)/shard_map/ppermute | solution.py:210
  15.5 3.1 %shard_map.75.refs_3_ = f32[512,128]{1,0:T(8,128)S(1)} custom-call(f32[8,128]{1,0:T(8,128)S(1)} %pad_maximum_fusion.1.own_points.refs_0_.refs_2_, f32[8,128]{1,0:T(8,128)S(1)} %collective-permute-done.far_points.refs_1_.refs_3_, bf16[4,144,128]{2,1,0:T(8,128)(2,1)S(1)} %pad_maximum_fusion.refs_2_), custom_call_target="tpu_custom_call" | custom-call | flops 10485760 | bytes 1048576 | tf_op jit(solution)/shard_map/pallas_call | solution.py:237
  18.6 0.0 collective-permute-done.4.refs_2_
  18.6 3.1 %shard_map.76 = (f32[512,128]{1,0:T(8,128)S(1)}, bf16[512,128]{1,0:T(8,128)(2,1)S(1)}) custom-call(f32[8,128]{1,0:T(8,128)S(1)} %pad_maximum_fusion.1.own_points.refs_0_.refs_2_, f32[8,128]{1,0:T(8,128)S(1)} %collective-permute-done.far_points.refs_1_.refs_3_, bf16[4,144,128]{2,1,0:T(8,128)(2,1)S(1)} %collective-permute-done.4.refs_2_, ...), custom_call_target="tpu_custom_call" | custom-call | flops 10485760 | bytes 1048576 | tf_op jit(solution)/shard_map/pallas_call | solution.py:240
  21.8 1.3 %collective-permute-start.5 = (bf16[512,128]{1,0:T(8,128)(2,1)S(1)}, bf16[512,128]{1,0:T(8,128)(2,1)S(1)}, u32[]{:S(2)}, u32[]{:S(2)}) collective-permute-start(bf16[512,128]{1,0:T(8,128)(2,1)S(1)} %get-tuple-element.16), channel_id=1, source_target_pairs={{0,2},{1,3},{2,0},{3,1},{4,6},{5,7},{6,4},{7,5},{8,10},{9,11},{10,... | collective-permute-start | bytes 393224 | tf_op jit(solution)/shard_map/ppermute | solution.py:210
  23.1 2.2 %shard_map.79 = (bf16[512,512]{1,0:T(8,128)(2,1)S(1)}, bf16[512,512]{1,0:T(8,128)(2,1)S(1)}) custom-call(f32[8,128]{1,0:T(8,128)S(1)} %pad_maximum_fusion.1.own_points.refs_0_.refs_2_, f32[8,128]{1,0:T(8,128)S(1)} %collective-permute-done.far_points.refs_1_.refs_3_, bf16[4,16,128]{2,1,0:T(8,128)(2,1)S(1)} %slice.24.tails), custom_call_target="tpu_custom_call" | custom-call | flops 7864320 | bytes 1048576 | tf_op jit(solution)/shard_map/pallas_call | solution.py:250
  25.3 0.4 collective-permute-done.5.refs_1_
  25.7 0.4 %shard_map.77.currents = bf16[512,128]{1,0:T(8,128)(2,1)S(1)} custom-call(f32[512,128]{1,0:T(8,128)S(1)} %get-tuple-element.15.refs_0_, bf16[512,128]{1,0:T(8,128)(2,1)S(1)} %collective-permute-done.5.refs_1_, f32[8,128]{1,0:T(8,128)S(1)} %pad_maximum_fusion.1.own_points.refs_0_.refs_2_, f32[8,128]{1,0:T(8,128)S(1)} %collective-permute-done.far_points.refs_1_.refs_3_), custom_call_target="tpu_custom_call" | custom-call | bytes 1048576 | tf_op jit(solution)/shard_map/pallas_call | solution.py:260
  26.1 0.5 %shard_map.80 = bf16[512,128]{1,0:T(8,128)(2,1)S(1)} custom-call(bf16[512,512]{1,0:T(8,128)(2,1)S(1)} %get-tuple-element.17.kernel_re, bf16[512,512]{1,0:T(8,128)(2,1)S(1)} %get-tuple-element.18.kernel_im, bf16[512,128]{1,0:T(8,128)(2,1)S(1)} %shard_map.77.currents), custom_call_target="tpu_custom_call" | custom-call | bytes 1048576 | tf_op jit(solution)/shard_map/pallas_call | solution.py:267
  26.6 2.9 %collective-permute-start.6 = (bf16[512,128]{1,0:T(8,128)(2,1)S(1)}, bf16[512,128]{1,0:T(8,128)(2,1)S(1)}, u32[]{:S(2)}, u32[]{:S(2)}) collective-permute-start(bf16[512,128]{1,0:T(8,128)(2,1)S(1)} %shard_map.80), channel_id=1, source_target_pairs={{0,1},{1,0},{2,3},{3,2},{4,5},{5,4},{6,7},{7,6},{8,9},{9,8},{10,11... | collective-permute-start | bytes 393224 | tf_op jit(solution)/shard_map/ppermute | solution.py:210
  29.6 2.2 %shard_map.74 = (bf16[512,512]{1,0:T(8,128)(2,1)S(1)}, bf16[512,512]{1,0:T(8,128)(2,1)S(1)}) custom-call(f32[8,128]{1,0:T(8,128)S(1)} %pad_maximum_fusion.1.own_points.refs_0_.refs_2_, f32[8,128]{1,0:T(8,128)S(1)} %collective-permute-done.far_points.refs_1_.refs_3_, bf16[4,16,128]{2,1,0:T(8,128)(2,1)S(1)} %slice.23.tails), custom_call_target="tpu_custom_call" | custom-call | flops 7864320 | bytes 1048576 | tf_op jit(solution)/shard_map/pallas_call | solution.py:250
  31.8 0.5 %shard_map.78.mine = f32[512,128]{1,0:T(8,128)S(1)} custom-call(bf16[512,512]{1,0:T(8,128)(2,1)S(1)} %get-tuple-element.13.kernel_re, bf16[512,512]{1,0:T(8,128)(2,1)S(1)} %get-tuple-element.14.kernel_im, bf16[512,128]{1,0:T(8,128)(2,1)S(1)} %shard_map.77.currents), custom_call_target="tpu_custom_call" | custom-call | bytes 1048576 | tf_op jit(solution)/shard_map/pallas_call | solution.py:267
  32.3 0.0 collective-permute-done.6.theirs
  32.4 1.2 %collective-permute-start.9 = (bf16[128,128]{1,0:T(8,128)(2,1)S(1)}, bf16[128,128]{1,0:T(8,128)(2,1)S(1)}, u32[]{:S(2)}, u32[]{:S(2)}) collective-permute-start(bf16[128,128]{1,0:T(8,128)(2,1)S(1)} %get-tuple-element.21), channel_id=1, source_target_pairs={{12,0},{13,1},{14,2},{15,3},{8,4},{9,5},{10,6},{11,7},{4,8},{5,9},... | collective-permute-start | bytes 98312 | tf_op jit(solution)/shard_map/ppermute | solution.py:210
  33.6 0.6 %collective-permute-start.8 = (bf16[128,128]{1,0:T(8,128)(2,1)S(1)}, bf16[128,128]{1,0:T(8,128)(2,1)S(1)}, u32[]{:S(2)}, u32[]{:S(2)}) collective-permute-start(bf16[128,128]{1,0:T(8,128)(2,1)S(1)} %get-tuple-element.22), channel_id=1, source_target_pairs={{8,0},{9,1},{10,2},{11,3},{12,4},{13,5},{14,6},{15,7},{0,8},{1,9},... | collective-permute-start | bytes 98312 | tf_op jit(solution)/shard_map/ppermute | solution.py:210
  34.2 1.7 %collective-permute-start.7 = (bf16[128,128]{1,0:T(8,128)(2,1)S(1)}, bf16[128,128]{1,0:T(8,128)(2,1)S(1)}, u32[]{:S(2)}, u32[]{:S(2)}) collective-permute-start(bf16[128,128]{1,0:T(8,128)(2,1)S(1)} %get-tuple-element.23), channel_id=1, source_target_pairs={{4,0},{5,1},{6,2},{7,3},{0,4},{1,5},{2,6},{3,7},{12,8},{13,9},{14,... | collective-permute-start | bytes 98312 | tf_op jit(solution)/shard_map/ppermute | solution.py:210
  36.0 1.0 %collective-permute-done.9.refs_2_ = bf16[128,128]{1,0:T(8,128)(2,1)S(1)} collective-permute-done((bf16[128,128]{1,0:T(8,128)(2,1)S(1)}, bf16[128,128]{1,0:T(8,128)(2,1)S(1)}, u32[]{:S(2)}, u32[]{:S(2)}) %collective-permute-start.9) | collective-permute-done | bytes 32800 | tf_op jit(solution)/shard_map/ppermute | solution.py:210
  37.0 1.5 %collective-permute-done.8.refs_1_ = bf16[128,128]{1,0:T(8,128)(2,1)S(1)} collective-permute-done((bf16[128,128]{1,0:T(8,128)(2,1)S(1)}, bf16[128,128]{1,0:T(8,128)(2,1)S(1)}, u32[]{:S(2)}, u32[]{:S(2)}) %collective-permute-start.8) | collective-permute-done | bytes 32800 | tf_op jit(solution)/shard_map/ppermute | solution.py:210
  38.5 0.3 collective-permute-done.7.refs_0_
  38.8 0.6 %shard_map.82 = f32[128,128]{1,0:T(8,128)} custom-call(f32[128,128]{1,0:T(8,128)S(1)} %get-tuple-element.19.kept, bf16[128,128]{1,0:T(8,128)(2,1)S(1)} %collective-permute-done.7.refs_0_, bf16[128,128]{1,0:T(8,128)(2,1)S(1)} %collective-permute-done.8.refs_1_, bf16[128,128]{1,0:T(8,128)(2,1)S(1)} %collective-permute-done.9.refs_2_), custom_call_target="tpu_custom_call" | custom-call | bytes 1048576 | tf_op jit(solution)/shard_map/pallas_call | solution.py:275
  (8 shorter events, 0.1 us)
Async XLA Ops:
  0.0 0.7 %copy-start.3 = (f32[128]{0:T(128)S(1)}, f32[128]{0:T(128)}, u32[]{:S(2)}) copy-start(f32[128]{0:T(128)} %param.8) | copy-start | bytes 1540
  0.0 0.7 %copy-start.1 = (f32[2,128]{1,0:T(2,128)S(1)}, f32[2,128]{1,0:T(2,128)}, u32[]{:S(2)}) copy-start(f32[2,128]{1,0:T(2,128)} %feed_plane.1) | copy-start | bytes 3076
  0.7 0.8 %copy-start = (bf16[128,128]{1,0:T(8,128)(2,1)S(1)}, bf16[128,128]{1,0:T(8,128)(2,1)}, u32[]{:S(2)}) copy-start(bf16[128,128]{1,0:T(8,128)(2,1)} %weights.1) | copy-start | bytes 98308
  1.5 0.7 %copy-start.2 = (f32[2,128]{1,0:T(2,128)S(1)}, f32[2,128]{1,0:T(2,128)}, u32[]{:S(2)}) copy-start(f32[2,128]{1,0:T(2,128)} %cosines.1) | copy-start | bytes 3076
  2.1 5.6 %collective-permute-start.3 = (bf16[144,128]{1,0:T(8,128)(2,1)S(1)}, bf16[144,128]{1,0:T(8,128)(2,1)S(1)}, u32[]{:S(2)}, u32[]{:S(2)}) collective-permute-start(bf16[144,128]{1,0:T(8,128)(2,1)S(1)} %shard_map.73), channel_id=1, source_target_pairs={{0,12},{1,13},{2,14},{3,15},{4,8},{5,9},{6,10},{7,11},{8,4},{9,5},... | collective-permute-start | bytes 110600 | tf_op jit(solution)/shard_map/ppermute | solution.py:210
  6.4 3.7 %collective-permute-start.2 = (bf16[144,128]{1,0:T(8,128)(2,1)S(1)}, bf16[144,128]{1,0:T(8,128)(2,1)S(1)}, u32[]{:S(2)}, u32[]{:S(2)}) collective-permute-start(bf16[144,128]{1,0:T(8,128)(2,1)S(1)} %shard_map.73), channel_id=1, source_target_pairs={{0,8},{1,9},{2,10},{3,11},{4,12},{5,13},{6,14},{7,15},{8,0},{9,1},... | collective-permute-start | bytes 110600 | tf_op jit(solution)/shard_map/ppermute | solution.py:210
  6.4 3.7 %collective-permute-start.1 = (bf16[144,128]{1,0:T(8,128)(2,1)S(1)}, bf16[144,128]{1,0:T(8,128)(2,1)S(1)}, u32[]{:S(2)}, u32[]{:S(2)}) collective-permute-start(bf16[144,128]{1,0:T(8,128)(2,1)S(1)} %shard_map.73), channel_id=1, source_target_pairs={{0,4},{1,5},{2,6},{3,7},{4,0},{5,1},{6,2},{7,3},{8,12},{9,13},{10,... | collective-permute-start | bytes 110600 | tf_op jit(solution)/shard_map/ppermute | solution.py:210
  10.1 2.2 %copy-start.4 = (f32[2,256]{1,0:T(2,128)S(1)}, f32[2,256]{1,0:T(2,128)}, u32[]{:S(2)}) copy-start(f32[2,256]{1,0:T(2,128)} %param.10) | copy-start | bytes 6148
  10.1 8.5 %collective-permute-start.4 = (bf16[4,144,128]{2,1,0:T(8,128)(2,1)S(1)}, bf16[4,144,128]{2,1,0:T(8,128)(2,1)S(1)}, u32[]{:S(2)}, u32[]{:S(2)}) collective-permute-start(bf16[4,144,128]{2,1,0:T(8,128)(2,1)S(1)} %pad_maximum_fusion.refs_2_), channel_id=1, source_target_pairs={{0,1},{1,0},{2,3},{3,2},{4,5},{5,4},{6,7},{7,6},{8,9},{9,8},{10,11... | collective-permute-start | bytes 442376 | tf_op jit(solution)/shard_map/ppermute | solution.py:210
  12.3 0.7 %copy-start.6 = (f32[256]{0:T(256)S(1)}, f32[256]{0:T(256)}, u32[]{:S(2)}) copy-start(f32[256]{0:T(256)} %param.11) | copy-start | bytes 3076
  12.3 0.7 %copy-start.5 = (f32[256]{0:T(256)S(1)}, f32[256]{0:T(256)}, u32[]{:S(2)}) copy-start(f32[256]{0:T(256)} %param.12) | copy-start | bytes 3076
  13.0 2.5 %collective-permute-start = (f32[8,128]{1,0:T(8,128)S(1)}, f32[8,128]{1,0:T(8,128)S(1)}, u32[]{:S(2)}, u32[]{:S(2)}) collective-permute-start(f32[8,128]{1,0:T(8,128)S(1)} %pad_maximum_fusion.1.own_points.refs_0_.refs_2_), channel_id=1, source_target_pairs={{0,2},{1,3},{2,0},{3,1},{4,6},{5,7},{6,4},{7,5},{8,10},{9,11},{10,... | collective-permute-start | bytes 12296 | tf_op jit(solution)/shard_map/ppermute | solution.py:210
  21.8 3.9 %collective-permute-start.5 = (bf16[512,128]{1,0:T(8,128)(2,1)S(1)}, bf16[512,128]{1,0:T(8,128)(2,1)S(1)}, u32[]{:S(2)}, u32[]{:S(2)}) collective-permute-start(bf16[512,128]{1,0:T(8,128)(2,1)S(1)} %get-tuple-element.16), channel_id=1, source_target_pairs={{0,2},{1,3},{2,0},{3,1},{4,6},{5,7},{6,4},{7,5},{8,10},{9,11},{10,... | collective-permute-start | bytes 393224 | tf_op jit(solution)/shard_map/ppermute | solution.py:210
  26.6 5.7 %collective-permute-start.6 = (bf16[512,128]{1,0:T(8,128)(2,1)S(1)}, bf16[512,128]{1,0:T(8,128)(2,1)S(1)}, u32[]{:S(2)}, u32[]{:S(2)}) collective-permute-start(bf16[512,128]{1,0:T(8,128)(2,1)S(1)} %shard_map.80), channel_id=1, source_target_pairs={{0,1},{1,0},{2,3},{3,2},{4,5},{5,4},{6,7},{7,6},{8,9},{9,8},{10,11... | collective-permute-start | bytes 393224 | tf_op jit(solution)/shard_map/ppermute | solution.py:210
  32.4 4.6 %collective-permute-start.9 = (bf16[128,128]{1,0:T(8,128)(2,1)S(1)}, bf16[128,128]{1,0:T(8,128)(2,1)S(1)}, u32[]{:S(2)}, u32[]{:S(2)}) collective-permute-start(bf16[128,128]{1,0:T(8,128)(2,1)S(1)} %get-tuple-element.21), channel_id=1, source_target_pairs={{12,0},{13,1},{14,2},{15,3},{8,4},{9,5},{10,6},{11,7},{4,8},{5,9},... | collective-permute-start | bytes 98312 | tf_op jit(solution)/shard_map/ppermute | solution.py:210
  33.6 4.9 %collective-permute-start.8 = (bf16[128,128]{1,0:T(8,128)(2,1)S(1)}, bf16[128,128]{1,0:T(8,128)(2,1)S(1)}, u32[]{:S(2)}, u32[]{:S(2)}) collective-permute-start(bf16[128,128]{1,0:T(8,128)(2,1)S(1)} %get-tuple-element.22), channel_id=1, source_target_pairs={{8,0},{9,1},{10,2},{11,3},{12,4},{13,5},{14,6},{15,7},{0,8},{1,9},... | collective-permute-start | bytes 98312 | tf_op jit(solution)/shard_map/ppermute | solution.py:210
  34.2 4.6 %collective-permute-start.7 = (bf16[128,128]{1,0:T(8,128)(2,1)S(1)}, bf16[128,128]{1,0:T(8,128)(2,1)S(1)}, u32[]{:S(2)}, u32[]{:S(2)}) collective-permute-start(bf16[128,128]{1,0:T(8,128)(2,1)S(1)} %get-tuple-element.23), channel_id=1, source_target_pairs={{4,0},{5,1},{6,2},{7,3},{0,4},{1,5},{2,6},{3,7},{12,8},{13,9},{14,... | collective-permute-start | bytes 98312 | tf_op jit(solution)/shard_map/ppermute | solution.py:210

commit v2 on v1

v2 whole, which is shorter than its diff:
```python
import functools
import math

import jax
import jax.numpy as jnp
from jax import lax
from jax.experimental import pallas as pl
from jax.experimental.pallas import tpu as pltpu
from jax.sharding import PartitionSpec as P

RANGE_REF = 20.0
F32, BF16 = jnp.float32, jnp.bfloat16

SIN_HALF = (3.1415902835895886, -5.167407697719414, 2.544020810735872, -0.5594899090940457)
COS_HALF = (0.9999932952798736, -4.933938014977294, 4.041283824377777, -1.222127057577997)

ROUNDER = 1.5 * 2.0**23

COORDS = 5
PACK_ROWS = 16


def horner(square, terms, scale):
    total = jnp.float32(terms[-1] * scale)
    for term in terms[-2::-1]:
        total = total * square + jnp.float32(term * scale)
    return total


def circle(turns, gain):
    part = turns - ((turns + ROUNDER) - ROUNDER)
    square = part * part
    root = math.sqrt(2.0 * abs(gain))
    half_sin = part * horner(square, SIN_HALF, root)
    half_cos = horner(square, COS_HALF, 2.0 * gain / root)
    return abs(gain) - half_sin * half_sin, half_sin * half_cos


def turned(columns):
    half = columns.shape[1] // 2
    return jnp.concatenate([-columns[:, half:], columns[:, :half]], axis=1)


def pack_body(weights, feed_plane, feed_height, cosines, message):
    rows, lanes = weights.shape
    message[:rows, :] = weights[...]
    exact = jnp.concatenate([feed_plane[...], feed_height[...], cosines[...]], axis=0)
    high = exact.astype(BF16)
    rest = exact - high.astype(F32)
    middle = rest.astype(BF16)
    low = (rest - middle.astype(F32)).astype(BF16)
    pad = jnp.zeros((PACK_ROWS - 3 * COORDS, lanes), F32)
    message[rows:, :] = jnp.concatenate(
        [high.astype(F32), middle.astype(F32), low.astype(F32), pad], axis=0
    ).astype(BF16)


def points_body(plane, height, patch, points):
    lanes = points.shape[1]
    points[0:2, :] = plane[:, :lanes]
    points[2:4, :] = plane[:, lanes:]
    points[4:6, :] = height[...]
    points[6:8, :] = patch[...]


def unpack(tail):
    tail = tail.astype(F32)
    return (tail[:COORDS] + tail[COORDS : 2 * COORDS]) + tail[2 * COORDS : 3 * COORDS]


def point_rows(points, at):
    return (2 * at, 2 * at + 1, 4 + at, 6 + at)


def fill_point_columns(points, columns, base):
    lanes = points.shape[1]
    up = points[...].T
    for at in range(2):
        columns[base + at * lanes : base + (at + 1) * lanes, :] = jnp.concatenate(
            [up[:, k : k + 1] for k in point_rows(points, at)], axis=1
        )


TILE = 16
LANES = 512


def blocks(total, most):
    return [slice(at, min(at + most, total)) for at in range(0, total, most)]


def green_body(point_sets, bases, scale, *refs):
    points, messages, refs = refs[:point_sets], refs[point_sets], refs[point_sets + 1 :]
    base, outs = refs[:bases], refs[bases:-8]
    columns, rows, weights, weights_turned, even_re, even_im, odd_re, odd_im = refs[-8:]
    count, height, lanes = messages.shape
    sources = height - PACK_ROWS
    total_points = columns.shape[0]
    for at in range(point_sets):
        fill_point_columns(points[at], columns, 2 * lanes * at)
    for at in range(count):
        where = slice(at * sources, (at + 1) * sources)
        rows[0:COORDS, where] = unpack(messages[at, sources:, :])
        block = messages[at, :sources, :]
        weights[where, :] = block
        weights_turned[where, :] = turned(block)
    chunk = even_re.shape[0]

    def fill(start, green_re, green_im):
        for at in range(0, chunk, TILE):
            here = slice(start + at, start + at + TILE)
            x, y, z = columns[here, 0:1], columns[here, 1:2], columns[here, 2:3]
            for part in blocks(count * sources, LANES):
                across = x - rows[0:1, part]
                along = y - rows[1:2, part]
                height = rows[2:3, part] - z
                squared = across * across + along * along + height * height
                inverse = lax.rsqrt(squared)
                cosine, sine = circle(squared * inverse, -RANGE_REF)
                amplitude = height * (inverse * inverse)
                green_re[at : at + TILE, part] = (amplitude * cosine).astype(BF16)
                green_im[at : at + TILE, part] = (amplitude * sine).astype(BF16)

    def add_up(start, green_re, green_im):
        here = slice(start, start + chunk)
        total = jnp.dot(green_re[...], weights[...], preferred_element_type=F32) + jnp.dot(
            green_im[...], weights_turned[...], preferred_element_type=F32
        )
        if base:
            step = base[0].shape[0]
            held = base[start // step][start % step : start % step + chunk, :]
            total = (total + held) * (columns[here, 3:4] * scale)
        for out in outs:
            out[here, :] = total.astype(out.dtype)

    slots = ((even_re, even_im), (odd_re, odd_im))
    turns = total_points // chunk
    for at in range(turns + 1):
        if at < turns:
            fill(at * chunk, *slots[at % 2])
        if at > 0:
            add_up((at - 1) * chunk, *slots[(at - 1) % 2])


def kernel_body(own_points, far_points, *refs):
    groups = refs[:2]
    outs = refs[2:6]
    columns, rows = refs[6:]
    count, height, lanes = groups[0].shape
    sources = height - PACK_ROWS
    size = count * lanes
    for which, messages in enumerate(groups):
        for at in range(count):
            uv = unpack(messages[at, sources:, :])[3:5]
            normal = jnp.sqrt(1.0 - uv[0:1] * uv[0:1] - uv[1:2] * uv[1:2])
            pad = jnp.zeros((5, lanes), F32)
            base = which * size + at * lanes
            columns[base : base + lanes, :] = jnp.concatenate([uv, normal, pad], axis=0).T
    for which, points in enumerate((own_points, far_points)):
        for at in range(2):
            base = (2 * which + at) * lanes
            for k, row in enumerate(point_rows(points, at)[:3]):
                rows[k : k + 1, base : base + lanes] = points[row : row + 1, :]
    for which in range(2):
        kernel_re, kernel_im = outs[2 * which : 2 * which + 2]

        def one(at, carry):
            start = pl.multiple_of(at * TILE, TILE)
            here = pl.ds(start, TILE)
            from_ = pl.ds(pl.multiple_of(which * size + start, TILE), TILE)
            turns = (
                columns[from_, 0:1] * rows[0:1, :]
                + columns[from_, 1:2] * rows[1:2, :]
                + columns[from_, 2:3] * rows[2:3, :]
            )
            cosine, sine = circle(turns, 1.0)
            kernel_re[here, :] = cosine.astype(BF16)
            kernel_im[here, :] = sine.astype(BF16)
            return carry

        lax.fori_loop(0, size // TILE, one, 0, unroll=16)


def radiate(kernel_re, kernel_im, held):
    return jnp.dot(kernel_re[...], held, preferred_element_type=F32) + jnp.dot(
        kernel_im[...], turned(held), preferred_element_type=F32
    )


def side_body(mine, theirs, kernel_re, kernel_im, currents, out):
    half = mine.shape[0] // 2
    for here, there in ((slice(0, half), slice(half, None)), (slice(half, None), slice(0, half))):
        currents[here, :] = (mine[here, :] + theirs[there, :].astype(F32)).astype(BF16)
    out[...] = radiate(kernel_re, kernel_im, currents[...]).astype(out.dtype)


def near_body(currents, kernel_re, kernel_im, out):
    out[...] = radiate(kernel_re, kernel_im, currents[...])


def fold_body(mine, theirs, kept, sent):
    first = kept.shape[0]
    total = mine[...] + theirs[...].astype(F32)
    kept[...] = total[:first]
    sent[...] = total[first:].astype(BF16)


def finish_body(kept, *refs):
    total = kept[...]
    for ref in refs[:-1]:
        total = total + ref[...].astype(F32)
    refs[-1][...] = total


def call(body, outs, scratch=(), flops=0, moved=0):
    return pl.pallas_call(
        body,
        out_shape=[jax.ShapeDtypeStruct(*out) for out in outs],
        scratch_shapes=list(scratch),
        compiler_params=pltpu.CompilerParams(vmem_limit_bytes=32 * 1024 * 1024),
        cost_estimate=pl.CostEstimate(flops=flops, bytes_accessed=moved, transcendentals=0),
    )


def per_device(
    feed_plane,
    feed_height,
    feed_weights,
    point_plane,
    point_height,
    patch_factor,
    direction_cosines,
):
    size = lax.axis_size("refl")
    line = size // 4
    sources, lanes = feed_weights.shape
    local_points = point_height.shape[0]
    half_points = 2 * local_points
    directions = direction_cosines.shape[1]

    def pairs(step):
        out = []
        for at in range(size):
            row, place = divmod(at, 4)
            far, near = divmod(step, 4)
            to = (row ^ far) if line & (line - 1) == 0 else (row + far) % line
            out.append((at, to * 4 + (place ^ near)))
        return out

    def swap(x, step, back=False):
        links = pairs(step)
        return lax.ppermute(x, "refl", [(b, a) for a, b in links] if back else links)

    message = call(pack_body, [((sources + PACK_ROWS, lanes), BF16)])(
        feed_weights, feed_plane, feed_height.reshape(1, lanes), direction_cosines
    )[0]
    points = call(points_body, [((8, lanes), F32)])(
        point_plane, point_height.reshape(2, lanes), patch_factor.reshape(2, lanes)
    )[0]
    arrived = [swap(message, 4 * k + 1) for k in range(1, line)]
    far_points = swap(points, 3)
    near_messages = jnp.stack([message, *arrived])
    side_messages = jnp.stack([swap(x, 1) for x in [message, *arrived]])

    part = line * sources
    chunk = local_points // 2
    scale = 1.0 / math.sqrt(local_points * size)

    def green(points, messages, bases, types):
        rows = len(points) * local_points
        scratch = [
            pltpu.VMEM((rows, 4), F32),
            pltpu.VMEM((8, part), F32),
            pltpu.VMEM((part, lanes), BF16),
            pltpu.VMEM((part, lanes), BF16),
        ] + [pltpu.VMEM((chunk, part), BF16)] * 4
        return call(
            functools.partial(green_body, len(points), len(bases), scale),
            [((rows, lanes), kind) for kind in types],
            scratch,
            0,
        )(*points, messages, *bases)

    bases = [green([which], near_messages, [], [F32])[0] for which in (points, far_points)]
    mine, told = green([points, far_points], side_messages, bases, [F32, BF16])
    theirs = swap(told, 3)

    count = line * directions
    near_re, near_im, side_re, side_im = call(
        kernel_body,
        [((count, half_points), BF16)] * 4,
        [pltpu.VMEM((2 * count, 8), F32), pltpu.VMEM((8, half_points), F32)],
        60 * count * half_points,
    )(points, far_points, near_messages, side_messages)
    currents, told = call(side_body, [((half_points, lanes), BF16), ((count, lanes), BF16)])(
        mine, theirs, side_re, side_im
    )
    given = swap(told, 1)
    near = call(near_body, [((count, lanes), F32)])(currents, near_re, near_im)[0]
    kept, sent = call(
        fold_body, [((directions, lanes), F32), (((line - 1) * directions, lanes), BF16)]
    )(near, given)
    sent = sent.reshape(line - 1, directions, lanes)
    arrived = [swap(sent[k - 1], 4 * k + 1, back=True) for k in range(1, line)]
    return call(finish_body, [((directions, lanes), F32)])(kept, *arrived)[0]


def solution(mesh):
    in_specs = (
        P("grp", "refl"),
        P(("grp", "refl")),
        P("refl", "grp"),
        P("grp", "refl"),
        P(("grp", "refl")),
        P(("grp", "refl")),
        P(None, "refl"),
    )
    out_specs = P("refl", "grp")
    return jax.shard_map(
        per_device, mesh=mesh, in_specs=in_specs, out_specs=out_specs, check_vma=False
    )
```

time: 40.3 us -> 31 us (0.77); the launches traced: 39.5 us -> 30.6 us
  Pallas kernels: 12.8 us -> 7.95 us
  starting transfers between devices: 15.9 us -> 13.4 us
  waiting for transfers between devices: 7.78 us -> 6.31 us
    pallas_call x7, Pallas kernels: 12.1 us -> 7.26 us  [the longest x3 3.94 us: green(): call(functools.partial(green_body, len(points), len(bases), scale), [((ro...]
    ppermute x10 -> x13, starting transfers between devices: 15.9 us -> 13.4 us  [swap(): lax.ppermute(x, 'refl', [(b, a) for a, b in links] if back else links)]
    ppermute x10 -> x13, waiting for transfers between devices: 7.78 us -> 6.31 us  [swap(): lax.ppermute(x, 'refl', [(b, a) for a, b in links] if back else links)]
  transfers between devices with their start and end apart: 10 -> 13, of which waited for: 7 -> 5; matrix products, arithmetic and copies ran while one was open for 0% -> 0% of each run, Pallas kernels for 20% -> 16%
where the time goes in v2:
time: 31 us; the launch traced here: 30.6 us
  starting transfers between devices  13.4 us (43%)
  Pallas kernels  7.95 us (26%)
  waiting for transfers between devices  6.31 us (20%)
  local copies, waits for them, and re-layouts  2.82 us (9%)
    ppermute x13, starting transfers between devices, swap(): lax.ppermute(x, 'refl', [(b, a) for a, b in links] if back else links)  13.4 us
    ppermute x13, waiting for transfers between devices, swap(): lax.ppermute(x, 'refl', [(b, a) for a, b in links] if back else links)  6.31 us
    pallas_call x3, Pallas kernels, green(): call(functools.partial(green_body, len(points), len(bases), scale), [((ro...  3.94 us
    unnamed x14, local copies, waits for them, and re-layouts  2.81 us
    pallas_call x1, Pallas kernels, per_device(): call(kernel_body, [((count, half_points), BF16)] * 4, [pltpu.VMEM((2 * co...  2.31 us
    pallas_call x1, Pallas kernels, per_device(): return call(finish_body, [((directions, lanes), F32)])(kept, *arrived)[0]  0.65 us
  transfers between devices with their start and end apart: 13, of which 5 were waited for; matrix products, arithmetic and copies ran while one was open for 0% of the time, Pallas kernels for 16%

profile of v2, /device:TPU:1, one launch (start us, length us, event | category | flops | bytes accessed | tf_op | source)
XLA Modules:
  0.0 30.6 jit_solution(14152749221172832652)
XLA Ops:
  0.0 0.0 copy-start.6
  0.0 0.0 copy-start.2
  0.0 0.7 %copy-done.6 = f32[128]{0:T(128)S(1)} copy-done((f32[128]{0:T(128)S(1)}, f32[128]{0:T(128)}, u32[]{:S(2)}) %copy-start.6) | copy-done | bytes 536
  0.7 0.0 copy-done.2
  0.7 0.0 copy-start
  0.7 0.8 %copy-done = bf16[128,128]{1,0:T(8,128)(2,1)S(1)} copy-done((bf16[128,128]{1,0:T(8,128)(2,1)S(1)}, bf16[128,128]{1,0:T(8,128)(2,1)}, u32[]{:S(2)}) %copy-start) | copy-done | bytes 32792
  1.5 0.0 copy-start.3
  1.5 0.7 %copy-done.3 = f32[2,128]{1,0:T(2,128)S(1)} copy-done((f32[2,128]{1,0:T(2,128)S(1)}, f32[2,128]{1,0:T(2,128)}, u32[]{:S(2)}) %copy-start.3) | copy-done | bytes 1048
  2.1 0.0 copy-start.5
  2.2 0.0 copy-start.1
  2.2 4.8 %collective-permute-start.6 = (bf16[144,128]{1,0:T(8,128)(2,1)S(1)}, bf16[144,128]{1,0:T(8,128)(2,1)S(1)}, u32[]{:S(2)}, u32[]{:S(2)}) collective-permute-start(bf16[144,128]{1,0:T(8,128)(2,1)S(1)} %shard_map.74), channel_id=1, source_target_pairs={{0,13},{1,12},{2,15},{3,14},{4,9},{5,8},{6,11},{7,10},{8,5},{9,4},... | collective-permute-start | bytes 110600 | tf_op jit(solution)/shard_map/ppermute | solution.py:252
  6.9 0.0 collective-permute-start.4
  6.9 0.1 collective-permute-start.2
  7.0 0.7 %collective-permute-start.1 = (bf16[144,128]{1,0:T(8,128)(2,1)S(1)}, bf16[144,128]{1,0:T(8,128)(2,1)S(1)}, u32[]{:S(2)}, u32[]{:S(2)}) collective-permute-start(bf16[144,128]{1,0:T(8,128)(2,1)S(1)} %shard_map.74), channel_id=1, source_target_pairs={{0,1},{1,0},{2,3},{3,2},{4,5},{5,4},{6,7},{7,6},{8,9},{9,8},{10,11... | collective-permute-start | bytes 110600 | tf_op jit(solution)/shard_map/ppermute | solution.py:252
  7.7 0.0 copy-start.4
  7.7 0.0 copy-done.5
  7.7 0.0 copy-done.1
  7.7 0.7 %copy-done.4 = f32[256]{0:T(256)S(1)} copy-done((f32[256]{0:T(256)S(1)}, f32[256]{0:T(256)}, u32[]{:S(2)}) %copy-start.4) | copy-done | bytes 1048
  8.4 1.4 %collective-permute-start = (f32[8,128]{1,0:T(8,128)S(1)}, f32[8,128]{1,0:T(8,128)S(1)}, u32[]{:S(2)}, u32[]{:S(2)}) collective-permute-start(f32[8,128]{1,0:T(8,128)S(1)} %shard_map.73.refs_0_.own_points), channel_id=1, source_target_pairs={{0,3},{1,2},{2,1},{3,0},{4,7},{5,6},{6,5},{7,4},{8,11},{9,10},{10,... | collective-permute-start | bytes 12296 | tf_op jit(solution)/shard_map/ppermute | solution.py:252
  9.8 0.0 collective-permute-done.6
  9.8 0.3 collective-permute-start.7
  10.0 1.2 %collective-permute-done.4 = bf16[144,128]{1,0:T(8,128)(2,1)S(1)} collective-permute-done((bf16[144,128]{1,0:T(8,128)(2,1)S(1)}, bf16[144,128]{1,0:T(8,128)(2,1)S(1)}, u32[]{:S(2)}, u32[]{:S(2)}) %collective-permute-start.4) | collective-permute-done | bytes 36896 | tf_op jit(solution)/shard_map/ppermute | solution.py:252
  11.2 0.2 collective-permute-start.5
  11.4 0.0 collective-permute-done.2
  11.4 0.3 %collective-permute-start.3 = (bf16[144,128]{1,0:T(8,128)(2,1)S(1)}, bf16[144,128]{1,0:T(8,128)(2,1)S(1)}, u32[]{:S(2)}, u32[]{:S(2)}) collective-permute-start(bf16[144,128]{1,0:T(8,128)(2,1)S(1)} %collective-permute-done.2), channel_id=1, source_target_pairs={{0,1},{1,0},{2,3},{3,2},{4,5},{5,4},{6,7},{7,6},{8,9},{9,8},{10,11... | collective-permute-start | bytes 110600 | tf_op jit(solution)/shard_map/ppermute | solution.py:252
  11.8 1.1 %shard_map.75.refs_3_ = f32[256,128]{1,0:T(8,128)S(1)} custom-call(f32[8,128]{1,0:T(8,128)S(1)} %shard_map.73.refs_0_.own_points, bf16[4,144,128]{2,1,0:T(8,128)(2,1)S(1)} %pad_maximum_fusion.1.refs_1_.refs_0_), custom_call_target="tpu_custom_call" | custom-call | tf_op jit(solution)/shard_map/pallas_call | solution.py:277
  12.8 0.0 collective-permute-done.refs_0_.refs_1_.far_points
  12.8 1.1 %shard_map.76.refs_4_ = f32[256,128]{1,0:T(8,128)S(1)} custom-call(f32[8,128]{1,0:T(8,128)S(1)} %collective-permute-done.refs_0_.refs_1_.far_points, bf16[4,144,128]{2,1,0:T(8,128)(2,1)S(1)} %pad_maximum_fusion.1.refs_1_.refs_0_), custom_call_target="tpu_custom_call" | custom-call | tf_op jit(solution)/shard_map/pallas_call | solution.py:277
  13.9 0.0 collective-permute-done.1
  13.9 0.0 collective-permute-done.7
  13.9 0.0 collective-permute-done.5
  13.9 0.0 collective-permute-done.3
  14.0 1.8 %shard_map.77 = (f32[512,128]{1,0:T(8,128)S(1)}, bf16[512,128]{1,0:T(8,128)(2,1)S(1)}) custom-call(f32[8,128]{1,0:T(8,128)S(1)} %shard_map.73.refs_0_.own_points, f32[8,128]{1,0:T(8,128)S(1)} %collective-permute-done.refs_0_.refs_1_.far_points, bf16[4,144,128]{2,1,0:T(8,128)(2,1)S(1)} %pad_maximum_fusion.refs_2_.refs_1_, f32[256,128]{1,0:T(8,128)S(1)} %shard_map.75.refs_3_, ...), custom_call_target="tpu_custom_call" | custom-call | tf_op jit(solution)/shard_map/pallas_call | solution.py:277
  15.8 1.4 %collective-permute-start.8 = (bf16[512,128]{1,0:T(8,128)(2,1)S(1)}, bf16[512,128]{1,0:T(8,128)(2,1)S(1)}, u32[]{:S(2)}, u32[]{:S(2)}) collective-permute-start(bf16[512,128]{1,0:T(8,128)(2,1)S(1)} %get-tuple-element.16), channel_id=1, source_target_pairs={{0,3},{1,2},{2,1},{3,0},{4,7},{5,6},{6,5},{7,4},{8,11},{9,10},{10,... | collective-permute-start | bytes 393224 | tf_op jit(solution)/shard_map/ppermute | solution.py:252
  17.2 2.3 %shard_map.78 = (bf16[512,512]{1,0:T(8,128)(2,1)S(1)}, bf16[512,512]{1,0:T(8,128)(2,1)S(1)}, bf16[512,512]{1,0:T(8,128)(2,1)S(1)}, bf16[512,512]{1,0:T(8,128)(2,1)S(1)}) custom-call(f32[8,128]{1,0:T(8,128)S(1)} %shard_map.73.refs_0_.own_points, f32[8,128]{1,0:T(8,128)S(1)} %collective-permute-done.refs_0_.refs_1_.far_points, ...), custom_call_target="tpu_custom_call" | custom-call | flops 15728640 | tf_op jit(solution)/shard_map/pallas_call | solution.py:289
  19.5 1.7 %collective-permute-done.8.theirs = bf16[512,128]{1,0:T(8,128)(2,1)S(1)} collective-permute-done((bf16[512,128]{1,0:T(8,128)(2,1)S(1)}, bf16[512,128]{1,0:T(8,128)(2,1)S(1)}, u32[]{:S(2)}, u32[]{:S(2)}) %collective-permute-start.8) | collective-permute-done | bytes 131104 | tf_op jit(solution)/shard_map/ppermute | solution.py:252
  21.2 0.5 %shard_map.79 = (bf16[512,128]{1,0:T(8,128)(2,1)S(1)}, bf16[512,128]{1,0:T(8,128)(2,1)S(1)}) custom-call(f32[512,128]{1,0:T(8,128)S(1)} %get-tuple-element.15.mine, bf16[512,128]{1,0:T(8,128)(2,1)S(1)} %collective-permute-done.8.theirs, bf16[512,512]{1,0:T(8,128)(2,1)S(1)} %get-tuple-element.17.kernel_re, bf16[512,512]{1,0:T(8,128)(2,1)S(1)} %get-tuple-element.18.kernel_im), custom_call_target="tpu_custom_call" | custom-call | tf_op jit(solution)/shard_map/pallas_call | solution.py:295
  21.7 0.3 %collective-permute-start.9 = (bf16[512,128]{1,0:T(8,128)(2,1)S(1)}, bf16[512,128]{1,0:T(8,128)(2,1)S(1)}, u32[]{:S(2)}, u32[]{:S(2)}) collective-permute-start(bf16[512,128]{1,0:T(8,128)(2,1)S(1)} %get-tuple-element.22), channel_id=1, source_target_pairs={{0,1},{1,0},{2,3},{3,2},{4,5},{5,4},{6,7},{7,6},{8,9},{9,8},{10,11... | collective-permute-start | bytes 393224 | tf_op jit(solution)/shard_map/ppermute | solution.py:252
  22.0 0.5 %shard_map.80.mine = f32[512,128]{1,0:T(8,128)S(1)} custom-call(bf16[512,128]{1,0:T(8,128)(2,1)S(1)} %get-tuple-element.19.currents, bf16[512,512]{1,0:T(8,128)(2,1)S(1)} %get-tuple-element.20.kernel_re, bf16[512,512]{1,0:T(8,128)(2,1)S(1)} %get-tuple-element.21.kernel_im), custom_call_target="tpu_custom_call" | custom-call | tf_op jit(solution)/shard_map/pallas_call | solution.py:299
  22.5 0.6 %collective-permute-done.9.theirs = bf16[512,128]{1,0:T(8,128)(2,1)S(1)} collective-permute-done((bf16[512,128]{1,0:T(8,128)(2,1)S(1)}, bf16[512,128]{1,0:T(8,128)(2,1)S(1)}, u32[]{:S(2)}, u32[]{:S(2)}) %collective-permute-start.9) | collective-permute-done | bytes 131104 | tf_op jit(solution)/shard_map/ppermute | solution.py:252
  23.1 2.6 %collective-permute-start.12 = (bf16[128,128]{1,0:T(8,128)(2,1)S(1)}, bf16[128,128]{1,0:T(8,128)(2,1)S(1)}, u32[]{:S(2)}, u32[]{:S(2)}) collective-permute-start(bf16[128,128]{1,0:T(8,128)(2,1)S(1)} %get-tuple-element.25), channel_id=1, source_target_pairs={{13,0},{12,1},{15,2},{14,3},{9,4},{8,5},{11,6},{10,7},{5,8},{4,9},... | collective-permute-start | bytes 98312 | tf_op jit(solution)/shard_map/ppermute | solution.py:252
  25.7 0.0 collective-permute-start.11
  25.7 1.4 %collective-permute-start.10 = (bf16[128,128]{1,0:T(8,128)(2,1)S(1)}, bf16[128,128]{1,0:T(8,128)(2,1)S(1)}, u32[]{:S(2)}, u32[]{:S(2)}) collective-permute-start(bf16[128,128]{1,0:T(8,128)(2,1)S(1)} %get-tuple-element.27), channel_id=1, source_target_pairs={{5,0},{4,1},{7,2},{6,3},{1,4},{0,5},{3,6},{2,7},{13,8},{12,9},{15,... | collective-permute-start | bytes 98312 | tf_op jit(solution)/shard_map/ppermute | solution.py:252
  27.2 1.2 %collective-permute-done.12.refs_2_ = bf16[128,128]{1,0:T(8,128)(2,1)S(1)} collective-permute-done((bf16[128,128]{1,0:T(8,128)(2,1)S(1)}, bf16[128,128]{1,0:T(8,128)(2,1)S(1)}, u32[]{:S(2)}, u32[]{:S(2)}) %collective-permute-start.12) | collective-permute-done | bytes 32800 | tf_op jit(solution)/shard_map/ppermute | solution.py:252
  28.4 1.6 %collective-permute-done.11.refs_1_ = bf16[128,128]{1,0:T(8,128)(2,1)S(1)} collective-permute-done((bf16[128,128]{1,0:T(8,128)(2,1)S(1)}, bf16[128,128]{1,0:T(8,128)(2,1)S(1)}, u32[]{:S(2)}, u32[]{:S(2)}) %collective-permute-start.11) | collective-permute-done | bytes 32800 | tf_op jit(solution)/shard_map/ppermute | solution.py:252
  30.0 0.0 collective-permute-done.10.refs_0_
  30.0 0.6 %shard_map.82 = f32[128,128]{1,0:T(8,128)} custom-call(f32[128,128]{1,0:T(8,128)S(1)} %get-tuple-element.23.kept, bf16[128,128]{1,0:T(8,128)(2,1)S(1)} %collective-permute-done.10.refs_0_, bf16[128,128]{1,0:T(8,128)(2,1)S(1)} %collective-permute-done.11.refs_1_, bf16[128,128]{1,0:T(8,128)(2,1)S(1)} %collective-permute-done.12.refs_2_), custom_call_target="tpu_custom_call" | custom-call | tf_op jit(solution)/shard_map/pallas_call | solution.py:305
  (6 shorter events, 0.1 us)
Async XLA Ops:
  0.0 0.7 %copy-start.6 = (f32[128]{0:T(128)S(1)}, f32[128]{0:T(128)}, u32[]{:S(2)}) copy-start(f32[128]{0:T(128)} %param.8) | copy-start | bytes 1540
  0.0 0.7 %copy-start.2 = (f32[2,128]{1,0:T(2,128)S(1)}, f32[2,128]{1,0:T(2,128)}, u32[]{:S(2)}) copy-start(f32[2,128]{1,0:T(2,128)} %feed_plane.1) | copy-start | bytes 3076
  0.7 0.8 %copy-start = (bf16[128,128]{1,0:T(8,128)(2,1)S(1)}, bf16[128,128]{1,0:T(8,128)(2,1)}, u32[]{:S(2)}) copy-start(bf16[128,128]{1,0:T(8,128)(2,1)} %weights.1) | copy-start | bytes 98308
  1.5 0.7 %copy-start.3 = (f32[2,128]{1,0:T(2,128)S(1)}, f32[2,128]{1,0:T(2,128)}, u32[]{:S(2)}) copy-start(f32[2,128]{1,0:T(2,128)} %cosines.1) | copy-start | bytes 3076
  2.1 5.6 %copy-start.5 = (f32[256]{0:T(256)S(1)}, f32[256]{0:T(256)}, u32[]{:S(2)}) copy-start(f32[256]{0:T(256)} %param.12) | copy-start | bytes 3076
  2.2 5.6 %copy-start.1 = (f32[2,256]{1,0:T(2,128)S(1)}, f32[2,256]{1,0:T(2,128)}, u32[]{:S(2)}) copy-start(f32[2,256]{1,0:T(2,128)} %plane.1) | copy-start | bytes 6148
  2.2 7.6 %collective-permute-start.6 = (bf16[144,128]{1,0:T(8,128)(2,1)S(1)}, bf16[144,128]{1,0:T(8,128)(2,1)S(1)}, u32[]{:S(2)}, u32[]{:S(2)}) collective-permute-start(bf16[144,128]{1,0:T(8,128)(2,1)S(1)} %shard_map.74), channel_id=1, source_target_pairs={{0,13},{1,12},{2,15},{3,14},{4,9},{5,8},{6,11},{7,10},{8,5},{9,4},... | collective-permute-start | bytes 110600 | tf_op jit(solution)/shard_map/ppermute | solution.py:252
  6.9 4.3 %collective-permute-start.4 = (bf16[144,128]{1,0:T(8,128)(2,1)S(1)}, bf16[144,128]{1,0:T(8,128)(2,1)S(1)}, u32[]{:S(2)}, u32[]{:S(2)}) collective-permute-start(bf16[144,128]{1,0:T(8,128)(2,1)S(1)} %shard_map.74), channel_id=1, source_target_pairs={{0,9},{1,8},{2,11},{3,10},{4,13},{5,12},{6,15},{7,14},{8,1},{9,0},... | collective-permute-start | bytes 110600 | tf_op jit(solution)/shard_map/ppermute | solution.py:252
  6.9 4.5 %collective-permute-start.2 = (bf16[144,128]{1,0:T(8,128)(2,1)S(1)}, bf16[144,128]{1,0:T(8,128)(2,1)S(1)}, u32[]{:S(2)}, u32[]{:S(2)}) collective-permute-start(bf16[144,128]{1,0:T(8,128)(2,1)S(1)} %shard_map.74), channel_id=1, source_target_pairs={{0,5},{1,4},{2,7},{3,6},{4,1},{5,0},{6,3},{7,2},{8,13},{9,12},{10,... | collective-permute-start | bytes 110600 | tf_op jit(solution)/shard_map/ppermute | solution.py:252
  7.0 6.9 %collective-permute-start.1 = (bf16[144,128]{1,0:T(8,128)(2,1)S(1)}, bf16[144,128]{1,0:T(8,128)(2,1)S(1)}, u32[]{:S(2)}, u32[]{:S(2)}) collective-permute-start(bf16[144,128]{1,0:T(8,128)(2,1)S(1)} %shard_map.74), channel_id=1, source_target_pairs={{0,1},{1,0},{2,3},{3,2},{4,5},{5,4},{6,7},{7,6},{8,9},{9,8},{10,11... | collective-permute-start | bytes 110600 | tf_op jit(solution)/shard_map/ppermute | solution.py:252
  7.7 0.7 %copy-start.4 = (f32[256]{0:T(256)S(1)}, f32[256]{0:T(256)}, u32[]{:S(2)}) copy-start(f32[256]{0:T(256)} %param.11) | copy-start | bytes 3076
  8.4 4.4 %collective-permute-start = (f32[8,128]{1,0:T(8,128)S(1)}, f32[8,128]{1,0:T(8,128)S(1)}, u32[]{:S(2)}, u32[]{:S(2)}) collective-permute-start(f32[8,128]{1,0:T(8,128)S(1)} %shard_map.73.refs_0_.own_points), channel_id=1, source_target_pairs={{0,3},{1,2},{2,1},{3,0},{4,7},{5,6},{6,5},{7,4},{8,11},{9,10},{10,... | collective-permute-start | bytes 12296 | tf_op jit(solution)/shard_map/ppermute | solution.py:252
  9.8 4.1 %collective-permute-start.7 = (bf16[144,128]{1,0:T(8,128)(2,1)S(1)}, bf16[144,128]{1,0:T(8,128)(2,1)S(1)}, u32[]{:S(2)}, u32[]{:S(2)}) collective-permute-start(bf16[144,128]{1,0:T(8,128)(2,1)S(1)} %collective-permute-done.6), channel_id=1, source_target_pairs={{0,1},{1,0},{2,3},{3,2},{4,5},{5,4},{6,7},{7,6},{8,9},{9,8},{10,11... | collective-permute-start | bytes 110600 | tf_op jit(solution)/shard_map/ppermute | solution.py:252
  11.2 2.7 %collective-permute-start.5 = (bf16[144,128]{1,0:T(8,128)(2,1)S(1)}, bf16[144,128]{1,0:T(8,128)(2,1)S(1)}, u32[]{:S(2)}, u32[]{:S(2)}) collective-permute-start(bf16[144,128]{1,0:T(8,128)(2,1)S(1)} %collective-permute-done.4), channel_id=1, source_target_pairs={{0,1},{1,0},{2,3},{3,2},{4,5},{5,4},{6,7},{7,6},{8,9},{9,8},{10,11... | collective-permute-start | bytes 110600 | tf_op jit(solution)/shard_map/ppermute | solution.py:252
  11.4 2.5 %collective-permute-start.3 = (bf16[144,128]{1,0:T(8,128)(2,1)S(1)}, bf16[144,128]{1,0:T(8,128)(2,1)S(1)}, u32[]{:S(2)}, u32[]{:S(2)}) collective-permute-start(bf16[144,128]{1,0:T(8,128)(2,1)S(1)} %collective-permute-done.2), channel_id=1, source_target_pairs={{0,1},{1,0},{2,3},{3,2},{4,5},{5,4},{6,7},{7,6},{8,9},{9,8},{10,11... | collective-permute-start | bytes 110600 | tf_op jit(solution)/shard_map/ppermute | solution.py:252
  15.8 5.3 %collective-permute-start.8 = (bf16[512,128]{1,0:T(8,128)(2,1)S(1)}, bf16[512,128]{1,0:T(8,128)(2,1)S(1)}, u32[]{:S(2)}, u32[]{:S(2)}) collective-permute-start(bf16[512,128]{1,0:T(8,128)(2,1)S(1)} %get-tuple-element.16), channel_id=1, source_target_pairs={{0,3},{1,2},{2,1},{3,0},{4,7},{5,6},{6,5},{7,4},{8,11},{9,10},{10,... | collective-permute-start | bytes 393224 | tf_op jit(solution)/shard_map/ppermute | solution.py:252
  21.7 1.4 %collective-permute-start.9 = (bf16[512,128]{1,0:T(8,128)(2,1)S(1)}, bf16[512,128]{1,0:T(8,128)(2,1)S(1)}, u32[]{:S(2)}, u32[]{:S(2)}) collective-permute-start(bf16[512,128]{1,0:T(8,128)(2,1)S(1)} %get-tuple-element.22), channel_id=1, source_target_pairs={{0,1},{1,0},{2,3},{3,2},{4,5},{5,4},{6,7},{7,6},{8,9},{9,8},{10,11... | collective-permute-start | bytes 393224 | tf_op jit(solution)/shard_map/ppermute | solution.py:252
  23.1 5.2 %collective-permute-start.12 = (bf16[128,128]{1,0:T(8,128)(2,1)S(1)}, bf16[128,128]{1,0:T(8,128)(2,1)S(1)}, u32[]{:S(2)}, u32[]{:S(2)}) collective-permute-start(bf16[128,128]{1,0:T(8,128)(2,1)S(1)} %get-tuple-element.25), channel_id=1, source_target_pairs={{13,0},{12,1},{15,2},{14,3},{9,4},{8,5},{11,6},{10,7},{5,8},{4,9},... | collective-permute-start | bytes 98312 | tf_op jit(solution)/shard_map/ppermute | solution.py:252
  25.7 4.2 %collective-permute-start.11 = (bf16[128,128]{1,0:T(8,128)(2,1)S(1)}, bf16[128,128]{1,0:T(8,128)(2,1)S(1)}, u32[]{:S(2)}, u32[]{:S(2)}) collective-permute-start(bf16[128,128]{1,0:T(8,128)(2,1)S(1)} %get-tuple-element.26), channel_id=1, source_target_pairs={{9,0},{8,1},{11,2},{10,3},{13,4},{12,5},{15,6},{14,7},{1,8},{0,9},... | collective-permute-start | bytes 98312 | tf_op jit(solution)/shard_map/ppermute | solution.py:252
  25.7 4.2 %collective-permute-start.10 = (bf16[128,128]{1,0:T(8,128)(2,1)S(1)}, bf16[128,128]{1,0:T(8,128)(2,1)S(1)}, u32[]{:S(2)}, u32[]{:S(2)}) collective-permute-start(bf16[128,128]{1,0:T(8,128)(2,1)S(1)} %get-tuple-element.27), channel_id=1, source_target_pairs={{5,0},{4,1},{7,2},{6,3},{1,4},{0,5},{3,6},{2,7},{13,8},{12,9},{15,... | collective-permute-start | bytes 98312 | tf_op jit(solution)/shard_map/ppermute | solution.py:252

commit v3 on v2

--- a/solution.py
+++ b/solution.py
@@ -41,10 +41,31 @@
     return jnp.concatenate([-columns[:, half:], columns[:, :half]], axis=1)
 
 
-def pack_body(weights, feed_plane, feed_height, cosines, message):
+def pack_body(
+    weights, feed_plane, feed_height, cosines, plane, height, patch, message, points, coords, ends, sems
+):
     rows, lanes = weights.shape
-    message[:rows, :] = weights[...]
-    exact = jnp.concatenate([feed_plane[...], feed_height[...], cosines[...]], axis=0)
+    sources = [feed_plane, feed_height, cosines, plane, height, patch, weights]
+    targets = [
+        coords.at[0:2, :],
+        coords.at[2:3, :],
+        coords.at[3:5, :],
+        ends,
+        points.at[4:6, :],
+        points.at[6:8, :],
+        message.at[0:rows, :],
+    ]
+    copies = [
+        pltpu.make_async_copy(source, target, sems.at[at])
+        for at, (source, target) in enumerate(zip(sources, targets))
+    ]
+    for copy in copies:
+        copy.start()
+    for copy in copies[:4]:
+        copy.wait()
+    points[0:2, :] = ends[:, :lanes]
+    points[2:4, :] = ends[:, lanes:]
+    exact = coords[0:COORDS, :]
     high = exact.astype(BF16)
     rest = exact - high.astype(F32)
     middle = rest.astype(BF16)
@@ -53,14 +74,8 @@
     message[rows:, :] = jnp.concatenate(
         [high.astype(F32), middle.astype(F32), low.astype(F32), pad], axis=0
     ).astype(BF16)
-
-
-def points_body(plane, height, patch, points):
-    lanes = points.shape[1]
-    points[0:2, :] = plane[:, :lanes]
-    points[2:4, :] = plane[:, lanes:]
-    points[4:6, :] = height[...]
-    points[6:8, :] = patch[...]
+    for copy in copies[4:]:
+        copy.wait()
 
 
 def unpack(tail):
@@ -212,13 +227,15 @@
     refs[-1][...] = total
 
 
-def call(body, outs, scratch=(), flops=0, moved=0):
+def call(body, outs, scratch=(), flops=0, anywhere=0, room=32 << 20):
+    places = [pl.BlockSpec(memory_space=pltpu.HBM)] * anywhere
     return pl.pallas_call(
         body,
         out_shape=[jax.ShapeDtypeStruct(*out) for out in outs],
         scratch_shapes=list(scratch),
-        compiler_params=pltpu.CompilerParams(vmem_limit_bytes=32 * 1024 * 1024),
-        cost_estimate=pl.CostEstimate(flops=flops, bytes_accessed=moved, transcendentals=0),
+        compiler_params=pltpu.CompilerParams(vmem_limit_bytes=room),
+        cost_estimate=pl.CostEstimate(flops=flops, bytes_accessed=0, transcendentals=0),
+        **(dict(in_specs=places) if anywhere else {}),
     )
 
 
@@ -251,16 +268,31 @@
         links = pairs(step)
         return lax.ppermute(x, "refl", [(b, a) for a, b in links] if back else links)
 
-    message = call(pack_body, [((sources + PACK_ROWS, lanes), BF16)])(
-        feed_weights, feed_plane, feed_height.reshape(1, lanes), direction_cosines
-    )[0]
-    points = call(points_body, [((8, lanes), F32)])(
-        point_plane, point_height.reshape(2, lanes), patch_factor.reshape(2, lanes)
-    )[0]
+    message, points = call(
+        pack_body,
+        [((sources + PACK_ROWS, lanes), BF16), ((8, lanes), F32)],
+        [pltpu.VMEM((8, lanes), F32), pltpu.VMEM((2, 2 * lanes), F32), pltpu.SemaphoreType.DMA((7,))],
+        anywhere=7,
+        room=32 << 20,
+    )(
+        *[
+            pltpu.with_memory_space_constraint(x, pltpu.HBM)
+            for x in (
+                feed_weights,
+                feed_plane,
+                feed_height.reshape(1, lanes),
+                direction_cosines,
+                point_plane,
+                point_height.reshape(2, lanes),
+                patch_factor.reshape(2, lanes),
+            )
+        ]
+    )
     arrived = [swap(message, 4 * k + 1) for k in range(1, line)]
     far_points = swap(points, 3)
+    far_points, *arrived = lax.optimization_barrier((far_points, *arrived))
     near_messages = jnp.stack([message, *arrived])
-    side_messages = jnp.stack([swap(x, 1) for x in [message, *arrived]])
+    side_messages = swap(near_messages, 1)
 
     part = line * sources
     chunk = local_points // 2
@@ -281,8 +313,9 @@
             0,
         )(*points, messages, *bases)
 
-    bases = [green([which], near_messages, [], [F32])[0] for which in (points, far_points)]
-    mine, told = green([points, far_points], side_messages, bases, [F32, BF16])
+    sets = [points, far_points]
+    bases = green(sets, near_messages, [], [F32])
+    mine, told = green(sets, side_messages, bases, [F32, BF16])
     theirs = swap(told, 3)
 
     count = line * directions

time: 31 us -> 29.6 us (0.955)
  local copies, waits for them, and re-layouts: 2.82 us -> 0.01 us
  waiting for transfers between devices: 6.31 us -> 7.67 us
  Pallas kernels: 7.95 us -> 8.54 us
  starting transfers between devices: 13.4 us -> 13 us
    unnamed x14 -> x0, local copies, waits for them, and re-layouts: 2.81 us -> none
    ppermute x13 -> x10, waiting for transfers between devices: 6.31 us -> 7.67 us  [swap(): lax.ppermute(x, 'refl', [(b, a) for a, b in links] if back else links)]
    pallas_call x2 -> x1, Pallas kernels: 0.02 us -> 0.91 us  [per_device(): call(pack_body, [((sources + PACK_ROWS, lanes), BF16), ((8, lanes), F32)]...]
    ppermute x13 -> x10, starting transfers between devices: 13.4 us -> 13 us  [swap(): lax.ppermute(x, 'refl', [(b, a) for a, b in links] if back else links)]
    pallas_call x3 -> x2, Pallas kernels: 3.94 us -> 3.64 us  [green(): call(functools.partial(green_body, len(points), len(bases), scale), [((ro...]
  transfers between devices with their start and end apart: 13 -> 10, of which waited for: 5 -> 6; matrix products, arithmetic and copies ran while one was open for 0% -> 0% of each run, Pallas kernels for 16% -> 16%
where the time goes in v3:
time: 29.6 us; the launch traced here: 29.3 us
  starting transfers between devices  13 us (44%)
  Pallas kernels  8.54 us (29%)
  waiting for transfers between devices  7.67 us (26%)
    ppermute x10, starting transfers between devices, swap(): lax.ppermute(x, 'refl', [(b, a) for a, b in links] if back else links)  13 us
    ppermute x10, waiting for transfers between devices, swap(): lax.ppermute(x, 'refl', [(b, a) for a, b in links] if back else links)  7.67 us
    pallas_call x2, Pallas kernels, green(): call(functools.partial(green_body, len(points), len(bases), scale), [((ro...  3.64 us
    pallas_call x1, Pallas kernels, per_device(): call(kernel_body, [((count, half_points), BF16)] * 4, [pltpu.VMEM((2 * co...  2.31 us
    pallas_call x1, Pallas kernels, per_device(): call(pack_body, [((sources + PACK_ROWS, lanes), BF16), ((8, lanes), F32)]...  0.91 us
    pallas_call x1, Pallas kernels, per_device(): return call(finish_body, [((directions, lanes), F32)])(kept, *arrived)[0]  0.65 us
  transfers between devices with their start and end apart: 10, of which 6 were waited for; matrix products, arithmetic and copies ran while one was open for 0% of the time, Pallas kernels for 16%

profile of v3, /device:TPU:1, one launch (start us, length us, event | category | flops | bytes accessed | tf_op | source)
XLA Modules:
  0.0 29.3 jit_solution(18075268199533367110)
XLA Ops:
  0.0 0.9 %shard_map.73 = (bf16[144,128]{1,0:T(8,128)(2,1)S(1)}, f32[8,128]{1,0:T(8,128)S(1)}) custom-call(bf16[128,128]{1,0:T(8,128)(2,1)} %weights.1, f32[2,128]{1,0:T(2,128)} %feed_plane.1, f32[1,128]{1,0:T(1,128)} %bitcast.13, f32[2,128]{1,0:T(2,128)} %cosines.1, f32[2,256]{1,0:T(2,128)} %plane.1, f32[2,128]{1,0:T(2,128)} %bitcast.11, f32[2,128]{1,0:T(2,128)} %bitcast.12), custom_call_target="tpu_custom_call" | custom-call | tf_op jit(solution)/shard_map/pallas_call | solution.py:271
  0.9 4.8 %collective-permute-start.3 = (bf16[144,128]{1,0:T(8,128)(2,1)S(1)}, bf16[144,128]{1,0:T(8,128)(2,1)S(1)}, u32[]{:S(2)}, u32[]{:S(2)}) collective-permute-start(bf16[144,128]{1,0:T(8,128)(2,1)S(1)} %get-tuple-element.22), channel_id=1, source_target_pairs={{0,13},{1,12},{2,15},{3,14},{4,9},{5,8},{6,11},{7,10},{8,5},{9,4},... | collective-permute-start | bytes 110600 | tf_op jit(solution)/shard_map/ppermute | solution.py:269
  5.7 0.0 collective-permute-start.2
  5.7 0.1 collective-permute-start.1
  5.8 1.8 %collective-permute-start = (f32[8,128]{1,0:T(8,128)S(1)}, f32[8,128]{1,0:T(8,128)S(1)}, u32[]{:S(2)}, u32[]{:S(2)}) collective-permute-start(f32[8,128]{1,0:T(8,128)S(1)} %get-tuple-element.21.refs_0_.own_points), channel_id=1, source_target_pairs={{0,3},{1,2},{2,1},{3,0},{4,7},{5,6},{6,5},{7,4},{8,11},{9,10},{10,... | collective-permute-start | bytes 12296 | tf_op jit(solution)/shard_map/ppermute | solution.py:269
  7.6 1.6 %collective-permute-done.refs_1_.far_points = f32[8,128]{1,0:T(8,128)S(1)} collective-permute-done((f32[8,128]{1,0:T(8,128)S(1)}, f32[8,128]{1,0:T(8,128)S(1)}, u32[]{:S(2)}, u32[]{:S(2)}) %collective-permute-start) | collective-permute-done | bytes 4128 | tf_op jit(solution)/shard_map/ppermute | solution.py:269
  9.2 0.0 collective-permute-done.3
  9.2 0.8 %collective-permute-done.2 = bf16[144,128]{1,0:T(8,128)(2,1)S(1)} collective-permute-done((bf16[144,128]{1,0:T(8,128)(2,1)S(1)}, bf16[144,128]{1,0:T(8,128)(2,1)S(1)}, u32[]{:S(2)}, u32[]{:S(2)}) %collective-permute-start.2) | collective-permute-done | bytes 36896 | tf_op jit(solution)/shard_map/ppermute | solution.py:269
  10.0 0.0 collective-permute-done.1
  10.0 0.2 collective-permute-start.4
  10.3 1.8 %shard_map.74.refs_3_ = f32[512,128]{1,0:T(8,128)S(1)} custom-call(f32[8,128]{1,0:T(8,128)S(1)} %get-tuple-element.21.refs_0_.own_points, f32[8,128]{1,0:T(8,128)S(1)} %collective-permute-done.refs_1_.far_points, bf16[4,144,128]{2,1,0:T(8,128)(2,1)S(1)} %pad_maximum_fusion.refs_2_.refs_0_), custom_call_target="tpu_custom_call" | custom-call | tf_op jit(solution)/shard_map/pallas_call | solution.py:309
  12.1 0.0 collective-permute-done.4.refs_2_.refs_1_
  12.1 1.8 %shard_map.75 = (f32[512,128]{1,0:T(8,128)S(1)}, bf16[512,128]{1,0:T(8,128)(2,1)S(1)}) custom-call(f32[8,128]{1,0:T(8,128)S(1)} %get-tuple-element.21.refs_0_.own_points, f32[8,128]{1,0:T(8,128)S(1)} %collective-permute-done.refs_1_.far_points, bf16[4,144,128]{2,1,0:T(8,128)(2,1)S(1)} %collective-permute-done.4.refs_2_.refs_1_, f32[512,128]{1,0:T(8,128)S(1)} %shard_map.74.refs_3_), custom_call_target="tpu_custom_call" | custom-call | tf_op jit(solution)/shard_map/pallas_call | solution.py:309
  13.9 1.5 %collective-permute-start.5 = (bf16[512,128]{1,0:T(8,128)(2,1)S(1)}, bf16[512,128]{1,0:T(8,128)(2,1)S(1)}, u32[]{:S(2)}, u32[]{:S(2)}) collective-permute-start(bf16[512,128]{1,0:T(8,128)(2,1)S(1)} %get-tuple-element.28), channel_id=1, source_target_pairs={{0,3},{1,2},{2,1},{3,0},{4,7},{5,6},{6,5},{7,4},{8,11},{9,10},{10,... | collective-permute-start | bytes 393224 | tf_op jit(solution)/shard_map/ppermute | solution.py:269
  15.4 2.3 %shard_map.76 = (bf16[512,512]{1,0:T(8,128)(2,1)S(1)}, bf16[512,512]{1,0:T(8,128)(2,1)S(1)}, bf16[512,512]{1,0:T(8,128)(2,1)S(1)}, bf16[512,512]{1,0:T(8,128)(2,1)S(1)}) custom-call(f32[8,128]{1,0:T(8,128)S(1)} %get-tuple-element.21.refs_0_.own_points, f32[8,128]{1,0:T(8,128)S(1)} %collective-permute-done.refs_1_.far_points, ...), custom_call_target="tpu_custom_call" | custom-call | flops 15728640 | tf_op jit(solution)/shard_map/pallas_call | solution.py:322
  17.7 1.7 %collective-permute-done.5.theirs = bf16[512,128]{1,0:T(8,128)(2,1)S(1)} collective-permute-done((bf16[512,128]{1,0:T(8,128)(2,1)S(1)}, bf16[512,128]{1,0:T(8,128)(2,1)S(1)}, u32[]{:S(2)}, u32[]{:S(2)}) %collective-permute-start.5) | collective-permute-done | bytes 131104 | tf_op jit(solution)/shard_map/ppermute | solution.py:269
  19.4 0.5 %shard_map.77 = (bf16[512,128]{1,0:T(8,128)(2,1)S(1)}, bf16[512,128]{1,0:T(8,128)(2,1)S(1)}) custom-call(f32[512,128]{1,0:T(8,128)S(1)} %get-tuple-element.27.mine, bf16[512,128]{1,0:T(8,128)(2,1)S(1)} %collective-permute-done.5.theirs, bf16[512,512]{1,0:T(8,128)(2,1)S(1)} %get-tuple-element.29.kernel_re, bf16[512,512]{1,0:T(8,128)(2,1)S(1)} %get-tuple-element.30.kernel_im), custom_call_target="tpu_custom_call" | custom-call | tf_op jit(solution)/shard_map/pallas_call | solution.py:328
  20.0 0.5 %collective-permute-start.6 = (bf16[512,128]{1,0:T(8,128)(2,1)S(1)}, bf16[512,128]{1,0:T(8,128)(2,1)S(1)}, u32[]{:S(2)}, u32[]{:S(2)}) collective-permute-start(bf16[512,128]{1,0:T(8,128)(2,1)S(1)} %get-tuple-element.34), channel_id=1, source_target_pairs={{0,1},{1,0},{2,3},{3,2},{4,5},{5,4},{6,7},{7,6},{8,9},{9,8},{10,11... | collective-permute-start | bytes 393224 | tf_op jit(solution)/shard_map/ppermute | solution.py:269
  20.4 0.5 %shard_map.78.mine = f32[512,128]{1,0:T(8,128)S(1)} custom-call(bf16[512,128]{1,0:T(8,128)(2,1)S(1)} %get-tuple-element.31.currents, bf16[512,512]{1,0:T(8,128)(2,1)S(1)} %get-tuple-element.32.kernel_re, bf16[512,512]{1,0:T(8,128)(2,1)S(1)} %get-tuple-element.33.kernel_im), custom_call_target="tpu_custom_call" | custom-call | tf_op jit(solution)/shard_map/pallas_call | solution.py:332
  20.9 0.5 %collective-permute-done.6.theirs = bf16[512,128]{1,0:T(8,128)(2,1)S(1)} collective-permute-done((bf16[512,128]{1,0:T(8,128)(2,1)S(1)}, bf16[512,128]{1,0:T(8,128)(2,1)S(1)}, u32[]{:S(2)}, u32[]{:S(2)}) %collective-permute-start.6) | collective-permute-done | bytes 131104 | tf_op jit(solution)/shard_map/ppermute | solution.py:269
  21.5 3.0 %collective-permute-start.9 = (bf16[128,128]{1,0:T(8,128)(2,1)S(1)}, bf16[128,128]{1,0:T(8,128)(2,1)S(1)}, u32[]{:S(2)}, u32[]{:S(2)}) collective-permute-start(bf16[128,128]{1,0:T(8,128)(2,1)S(1)} %get-tuple-element.37), channel_id=1, source_target_pairs={{13,0},{12,1},{15,2},{14,3},{9,4},{8,5},{11,6},{10,7},{5,8},{4,9},... | collective-permute-start | bytes 98312 | tf_op jit(solution)/shard_map/ppermute | solution.py:269
  24.4 0.0 collective-permute-start.8
  24.4 1.2 %collective-permute-start.7 = (bf16[128,128]{1,0:T(8,128)(2,1)S(1)}, bf16[128,128]{1,0:T(8,128)(2,1)S(1)}, u32[]{:S(2)}, u32[]{:S(2)}) collective-permute-start(bf16[128,128]{1,0:T(8,128)(2,1)S(1)} %get-tuple-element.39), channel_id=1, source_target_pairs={{5,0},{4,1},{7,2},{6,3},{1,4},{0,5},{3,6},{2,7},{13,8},{12,9},{15,... | collective-permute-start | bytes 98312 | tf_op jit(solution)/shard_map/ppermute | solution.py:269
  25.6 1.1 %collective-permute-done.9.refs_2_ = bf16[128,128]{1,0:T(8,128)(2,1)S(1)} collective-permute-done((bf16[128,128]{1,0:T(8,128)(2,1)S(1)}, bf16[128,128]{1,0:T(8,128)(2,1)S(1)}, u32[]{:S(2)}, u32[]{:S(2)}) %collective-permute-start.9) | collective-permute-done | bytes 32800 | tf_op jit(solution)/shard_map/ppermute | solution.py:269
  26.7 2.0 %collective-permute-done.8.refs_1_ = bf16[128,128]{1,0:T(8,128)(2,1)S(1)} collective-permute-done((bf16[128,128]{1,0:T(8,128)(2,1)S(1)}, bf16[128,128]{1,0:T(8,128)(2,1)S(1)}, u32[]{:S(2)}, u32[]{:S(2)}) %collective-permute-start.8) | collective-permute-done | bytes 32800 | tf_op jit(solution)/shard_map/ppermute | solution.py:269
  28.7 0.0 collective-permute-done.7.refs_0_
  28.7 0.6 %shard_map.80 = f32[128,128]{1,0:T(8,128)} custom-call(f32[128,128]{1,0:T(8,128)S(1)} %get-tuple-element.35.kept, bf16[128,128]{1,0:T(8,128)(2,1)S(1)} %collective-permute-done.7.refs_0_, bf16[128,128]{1,0:T(8,128)(2,1)S(1)} %collective-permute-done.8.refs_1_, bf16[128,128]{1,0:T(8,128)(2,1)S(1)} %collective-permute-done.9.refs_2_), custom_call_target="tpu_custom_call" | custom-call | tf_op jit(solution)/shard_map/pallas_call | solution.py:338
  (3 shorter events, 0.1 us)
Async XLA Ops:
  0.9 8.2 %collective-permute-start.3 = (bf16[144,128]{1,0:T(8,128)(2,1)S(1)}, bf16[144,128]{1,0:T(8,128)(2,1)S(1)}, u32[]{:S(2)}, u32[]{:S(2)}) collective-permute-start(bf16[144,128]{1,0:T(8,128)(2,1)S(1)} %get-tuple-element.22), channel_id=1, source_target_pairs={{0,13},{1,12},{2,15},{3,14},{4,9},{5,8},{6,11},{7,10},{8,5},{9,4},... | collective-permute-start | bytes 110600 | tf_op jit(solution)/shard_map/ppermute | solution.py:269
  5.7 4.3 %collective-permute-start.2 = (bf16[144,128]{1,0:T(8,128)(2,1)S(1)}, bf16[144,128]{1,0:T(8,128)(2,1)S(1)}, u32[]{:S(2)}, u32[]{:S(2)}) collective-permute-start(bf16[144,128]{1,0:T(8,128)(2,1)S(1)} %get-tuple-element.22), channel_id=1, source_target_pairs={{0,9},{1,8},{2,11},{3,10},{4,13},{5,12},{6,15},{7,14},{8,1},{9,0},... | collective-permute-start | bytes 110600 | tf_op jit(solution)/shard_map/ppermute | solution.py:269
  5.7 4.3 %collective-permute-start.1 = (bf16[144,128]{1,0:T(8,128)(2,1)S(1)}, bf16[144,128]{1,0:T(8,128)(2,1)S(1)}, u32[]{:S(2)}, u32[]{:S(2)}) collective-permute-start(bf16[144,128]{1,0:T(8,128)(2,1)S(1)} %get-tuple-element.22), channel_id=1, source_target_pairs={{0,5},{1,4},{2,7},{3,6},{4,1},{5,0},{6,3},{7,2},{8,13},{9,12},{10,... | collective-permute-start | bytes 110600 | tf_op jit(solution)/shard_map/ppermute | solution.py:269
  5.8 3.4 %collective-permute-start = (f32[8,128]{1,0:T(8,128)S(1)}, f32[8,128]{1,0:T(8,128)S(1)}, u32[]{:S(2)}, u32[]{:S(2)}) collective-permute-start(f32[8,128]{1,0:T(8,128)S(1)} %get-tuple-element.21.refs_0_.own_points), channel_id=1, source_target_pairs={{0,3},{1,2},{2,1},{3,0},{4,7},{5,6},{6,5},{7,4},{8,11},{9,10},{10,... | collective-permute-start | bytes 12296 | tf_op jit(solution)/shard_map/ppermute | solution.py:269
  10.0 2.1 %collective-permute-start.4 = (bf16[4,144,128]{2,1,0:T(8,128)(2,1)S(1)}, bf16[4,144,128]{2,1,0:T(8,128)(2,1)S(1)}, u32[]{:S(2)}, u32[]{:S(2)}) collective-permute-start(bf16[4,144,128]{2,1,0:T(8,128)(2,1)S(1)} %pad_maximum_fusion.refs_2_.refs_0_), channel_id=1, source_target_pairs={{0,1},{1,0},{2,3},{3,2},{4,5},{5,4},{6,7},{7,6},{8,9},{9,8},{10,11... | collective-permute-start | bytes 442376 | tf_op jit(solution)/shard_map/ppermute | solution.py:269
  13.9 5.5 %collective-permute-start.5 = (bf16[512,128]{1,0:T(8,128)(2,1)S(1)}, bf16[512,128]{1,0:T(8,128)(2,1)S(1)}, u32[]{:S(2)}, u32[]{:S(2)}) collective-permute-start(bf16[512,128]{1,0:T(8,128)(2,1)S(1)} %get-tuple-element.28), channel_id=1, source_target_pairs={{0,3},{1,2},{2,1},{3,0},{4,7},{5,6},{6,5},{7,4},{8,11},{9,10},{10,... | collective-permute-start | bytes 393224 | tf_op jit(solution)/shard_map/ppermute | solution.py:269
  20.0 1.4 %collective-permute-start.6 = (bf16[512,128]{1,0:T(8,128)(2,1)S(1)}, bf16[512,128]{1,0:T(8,128)(2,1)S(1)}, u32[]{:S(2)}, u32[]{:S(2)}) collective-permute-start(bf16[512,128]{1,0:T(8,128)(2,1)S(1)} %get-tuple-element.34), channel_id=1, source_target_pairs={{0,1},{1,0},{2,3},{3,2},{4,5},{5,4},{6,7},{7,6},{8,9},{9,8},{10,11... | collective-permute-start | bytes 393224 | tf_op jit(solution)/shard_map/ppermute | solution.py:269
  21.5 5.2 %collective-permute-start.9 = (bf16[128,128]{1,0:T(8,128)(2,1)S(1)}, bf16[128,128]{1,0:T(8,128)(2,1)S(1)}, u32[]{:S(2)}, u32[]{:S(2)}) collective-permute-start(bf16[128,128]{1,0:T(8,128)(2,1)S(1)} %get-tuple-element.37), channel_id=1, source_target_pairs={{13,0},{12,1},{15,2},{14,3},{9,4},{8,5},{11,6},{10,7},{5,8},{4,9},... | collective-permute-start | bytes 98312 | tf_op jit(solution)/shard_map/ppermute | solution.py:269
  24.4 4.2 %collective-permute-start.8 = (bf16[128,128]{1,0:T(8,128)(2,1)S(1)}, bf16[128,128]{1,0:T(8,128)(2,1)S(1)}, u32[]{:S(2)}, u32[]{:S(2)}) collective-permute-start(bf16[128,128]{1,0:T(8,128)(2,1)S(1)} %get-tuple-element.38), channel_id=1, source_target_pairs={{9,0},{8,1},{11,2},{10,3},{13,4},{12,5},{15,6},{14,7},{1,8},{0,9},... | collective-permute-start | bytes 98312 | tf_op jit(solution)/shard_map/ppermute | solution.py:269
  24.4 4.2 %collective-permute-start.7 = (bf16[128,128]{1,0:T(8,128)(2,1)S(1)}, bf16[128,128]{1,0:T(8,128)(2,1)S(1)}, u32[]{:S(2)}, u32[]{:S(2)}) collective-permute-start(bf16[128,128]{1,0:T(8,128)(2,1)S(1)} %get-tuple-element.39), channel_id=1, source_target_pairs={{5,0},{4,1},{7,2},{6,3},{1,4},{0,5},{3,6},{2,7},{13,8},{12,9},{15,... | collective-permute-start | bytes 98312 | tf_op jit(solution)/shard_map/ppermute | solution.py:269

commit v4 on v3

--- a/solution.py
+++ b/solution.py
@@ -15,6 +15,9 @@
 COS_HALF = (0.9999932952798736, -4.933938014977294, 4.041283824377777, -1.222127057577997)
 
 ROUNDER = 1.5 * 2.0**23
+
+TERMS = 32
+MIDDLE = 22.0
 
 COORDS = 5
 PACK_ROWS = 16
@@ -83,6 +86,25 @@
     return (tail[:COORDS] + tail[COORDS : 2 * COORDS]) + tail[2 * COORDS : 3 * COORDS]
 
 
+def split(value):
+    high = value.astype(BF16).astype(F32)
+    rest = value - high
+    middle = rest.astype(BF16).astype(F32)
+    return high, middle, (rest - middle).astype(BF16).astype(F32)
+
+
+def distance_terms(x, y, z, is_point):
+    z = z - MIDDLE
+    square = x * x + y * y + z * z
+    out = []
+    for value in (x, y, z):
+        high, middle, low = split(value if is_point else -2.0 * value)
+        out += [high, high, middle, high, middle, low] if is_point else [high, middle, high, low, middle, high]
+    ones = [jnp.ones_like(x)] * 3
+    out += list(split(square)) + ones if is_point else ones + list(split(square))
+    return jnp.concatenate(out + [jnp.zeros_like(x)] * (TERMS - len(out)), axis=0)
+
+
 def point_rows(points, at):
     return (2 * at, 2 * at + 1, 4 + at, 6 + at)
 
@@ -96,7 +118,7 @@
         )
 
 
-TILE = 16
+TILE = 32
 LANES = 512
 
 
@@ -106,37 +128,44 @@
 
 def green_body(point_sets, bases, scale, *refs):
     points, messages, refs = refs[:point_sets], refs[point_sets], refs[point_sets + 1 :]
-    base, outs = refs[:bases], refs[bases:-8]
-    columns, rows, weights, weights_turned, even_re, even_im, odd_re, odd_im = refs[-8:]
+    base, outs = refs[:bases], refs[bases:-12]
+    columns, left, heights, right, weights, weights_turned, *slots = refs[-12:]
+    slots = (slots[:3], slots[3:])
     count, height, lanes = messages.shape
     sources = height - PACK_ROWS
     total_points = columns.shape[0]
     for at in range(point_sets):
         fill_point_columns(points[at], columns, 2 * lanes * at)
+        for half in range(2):
+            x, y, z = (points[at][k : k + 1, :] for k in point_rows(points[at], half)[:3])
+            start = (2 * at + half) * lanes
+            left[start : start + lanes, :] = distance_terms(x, y, z, True).T.astype(BF16)
     for at in range(count):
         where = slice(at * sources, (at + 1) * sources)
-        rows[0:COORDS, where] = unpack(messages[at, sources:, :])
+        coords = unpack(messages[at, sources:, :])
+        x, y, z = coords[0:1], coords[1:2], coords[2:3]
+        heights[0:1, where] = z
+        right[:, where] = distance_terms(x, y, z, False).astype(BF16)
         block = messages[at, :sources, :]
         weights[where, :] = block
         weights_turned[where, :] = turned(block)
-    chunk = even_re.shape[0]
-
-    def fill(start, green_re, green_im):
+    chunk = slots[0][0].shape[0]
+
+    def fill(start, green_re, green_im, squares):
+        squares[...] = jnp.dot(
+            left[start : start + chunk, :], right[...], preferred_element_type=F32
+        )
         for at in range(0, chunk, TILE):
-            here = slice(start + at, start + at + TILE)
-            x, y, z = columns[here, 0:1], columns[here, 1:2], columns[here, 2:3]
+            low = columns[start + at : start + at + TILE, 2:3]
             for part in blocks(count * sources, LANES):
-                across = x - rows[0:1, part]
-                along = y - rows[1:2, part]
-                height = rows[2:3, part] - z
-                squared = across * across + along * along + height * height
+                squared = squares[at : at + TILE, part]
                 inverse = lax.rsqrt(squared)
                 cosine, sine = circle(squared * inverse, -RANGE_REF)
-                amplitude = height * (inverse * inverse)
+                amplitude = (heights[0:1, part] - low) * (inverse * inverse)
                 green_re[at : at + TILE, part] = (amplitude * cosine).astype(BF16)
                 green_im[at : at + TILE, part] = (amplitude * sine).astype(BF16)
 
-    def add_up(start, green_re, green_im):
+    def add_up(start, green_re, green_im, _):
         here = slice(start, start + chunk)
         total = jnp.dot(green_re[...], weights[...], preferred_element_type=F32) + jnp.dot(
             green_im[...], weights_turned[...], preferred_element_type=F32
@@ -148,7 +177,6 @@
         for out in outs:
             out[here, :] = total.astype(out.dtype)
 
-    slots = ((even_re, even_im), (odd_re, odd_im))
     turns = total_points // chunk
     for at in range(turns + 1):
         if at < turns:
@@ -295,17 +323,23 @@
     side_messages = swap(near_messages, 1)
 
     part = line * sources
-    chunk = local_points // 2
+    chunk = local_points
     scale = 1.0 / math.sqrt(local_points * size)
 
     def green(points, messages, bases, types):
         rows = len(points) * local_points
+        slot = [((chunk, part), BF16), ((chunk, part), BF16), ((chunk, part), F32)]
         scratch = [
-            pltpu.VMEM((rows, 4), F32),
-            pltpu.VMEM((8, part), F32),
-            pltpu.VMEM((part, lanes), BF16),
-            pltpu.VMEM((part, lanes), BF16),
-        ] + [pltpu.VMEM((chunk, part), BF16)] * 4
+            ((rows, 4), F32),
+            ((rows, TERMS), BF16),
+            ((8, part), F32),
+            ((TERMS, part), BF16),
+            ((part, lanes), BF16),
+            ((part, lanes), BF16),
+            *slot,
+            *slot,
+        ]
+        scratch = [pltpu.VMEM(*which) for which in scratch]
         return call(
             functools.partial(green_body, len(points), len(bases), scale),
             [((rows, lanes), kind) for kind in types],

time: 29.6 us -> 29.1 us (0.983)
  Pallas kernels: 8.54 us -> 7.81 us
    pallas_call x2, Pallas kernels: 3.64 us -> 3.11 us  [green(): call(functools.partial(green_body, len(points), len(bases), scale), [((ro...]
  transfers between devices with their start and end apart: 10 -> 10, of which waited for: 6 -> 6; matrix products, arithmetic and copies ran while one was open for 0% -> 0% of each run, Pallas kernels for 16% -> 14%
where the time goes in v4:
time: 29.1 us; the launch traced here: 28.8 us
  starting transfers between devices  13 us (45%)
  waiting for transfers between devices  7.88 us (27%)
  Pallas kernels  7.81 us (27%)
    ppermute x10, starting transfers between devices, swap(): lax.ppermute(x, 'refl', [(b, a) for a, b in links] if back else links)  13 us
    ppermute x10, waiting for transfers between devices, swap(): lax.ppermute(x, 'refl', [(b, a) for a, b in links] if back else links)  7.88 us
    pallas_call x2, Pallas kernels, green(): call(functools.partial(green_body, len(points), len(bases), scale), [((ro...  3.11 us
    pallas_call x1, Pallas kernels, per_device(): call(kernel_body, [((count, half_points), BF16)] * 4, [pltpu.VMEM((2 * co...  2.1 us
    pallas_call x1, Pallas kernels, per_device(): call(pack_body, [((sources + PACK_ROWS, lanes), BF16), ((8, lanes), F32)]...  0.91 us
    pallas_call x1, Pallas kernels, per_device(): return call(finish_body, [((directions, lanes), F32)])(kept, *arrived)[0]  0.65 us
  transfers between devices with their start and end apart: 10, of which 6 were waited for; matrix products, arithmetic and copies ran while one was open for 0% of the time, Pallas kernels for 14%

profile of v4, /device:TPU:1, one launch (start us, length us, event | category | flops | bytes accessed | tf_op | source)
XLA Modules:
  0.0 28.8 jit_solution(1878808407882132621)
XLA Ops:
  0.0 0.9 %shard_map.73 = (bf16[144,128]{1,0:T(8,128)(2,1)S(1)}, f32[8,128]{1,0:T(8,128)S(1)}) custom-call(bf16[128,128]{1,0:T(8,128)(2,1)} %weights.1, f32[2,128]{1,0:T(2,128)} %feed_plane.1, f32[1,128]{1,0:T(1,128)} %bitcast.13, f32[2,128]{1,0:T(2,128)} %cosines.1, f32[2,256]{1,0:T(2,128)} %plane.1, f32[2,128]{1,0:T(2,128)} %bitcast.11, f32[2,128]{1,0:T(2,128)} %bitcast.12), custom_call_target="tpu_custom_call" | custom-call | tf_op jit(solution)/shard_map/pallas_call | solution.py:299
  0.9 4.8 %collective-permute-start.3 = (bf16[144,128]{1,0:T(8,128)(2,1)S(1)}, bf16[144,128]{1,0:T(8,128)(2,1)S(1)}, u32[]{:S(2)}, u32[]{:S(2)}) collective-permute-start(bf16[144,128]{1,0:T(8,128)(2,1)S(1)} %get-tuple-element.22), channel_id=1, source_target_pairs={{0,13},{1,12},{2,15},{3,14},{4,9},{5,8},{6,11},{7,10},{8,5},{9,4},... | collective-permute-start | bytes 110600 | tf_op jit(solution)/shard_map/ppermute | solution.py:297
  5.7 0.0 collective-permute-start.2
  5.7 0.1 collective-permute-start.1
  5.8 1.8 %collective-permute-start = (f32[8,128]{1,0:T(8,128)S(1)}, f32[8,128]{1,0:T(8,128)S(1)}, u32[]{:S(2)}, u32[]{:S(2)}) collective-permute-start(f32[8,128]{1,0:T(8,128)S(1)} %get-tuple-element.21.refs_0_.own_points), channel_id=1, source_target_pairs={{0,3},{1,2},{2,1},{3,0},{4,7},{5,6},{6,5},{7,4},{8,11},{9,10},{10,... | collective-permute-start | bytes 12296 | tf_op jit(solution)/shard_map/ppermute | solution.py:297
  7.6 1.6 %collective-permute-done.refs_1_.far_points = f32[8,128]{1,0:T(8,128)S(1)} collective-permute-done((f32[8,128]{1,0:T(8,128)S(1)}, f32[8,128]{1,0:T(8,128)S(1)}, u32[]{:S(2)}, u32[]{:S(2)}) %collective-permute-start) | collective-permute-done | bytes 4128 | tf_op jit(solution)/shard_map/ppermute | solution.py:297
  9.2 0.0 collective-permute-done.3
  9.2 0.8 %collective-permute-done.2 = bf16[144,128]{1,0:T(8,128)(2,1)S(1)} collective-permute-done((bf16[144,128]{1,0:T(8,128)(2,1)S(1)}, bf16[144,128]{1,0:T(8,128)(2,1)S(1)}, u32[]{:S(2)}, u32[]{:S(2)}) %collective-permute-start.2) | collective-permute-done | bytes 36896 | tf_op jit(solution)/shard_map/ppermute | solution.py:297
  10.0 0.0 collective-permute-done.1
  10.0 0.2 collective-permute-start.4
  10.3 1.5 %shard_map.74.refs_3_ = f32[512,128]{1,0:T(8,128)S(1)} custom-call(f32[8,128]{1,0:T(8,128)S(1)} %get-tuple-element.21.refs_0_.own_points, f32[8,128]{1,0:T(8,128)S(1)} %collective-permute-done.refs_1_.far_points, bf16[4,144,128]{2,1,0:T(8,128)(2,1)S(1)} %pad_maximum_fusion.refs_2_.refs_0_), custom_call_target="tpu_custom_call" | custom-call | tf_op jit(solution)/shard_map/pallas_call | solution.py:343
  11.8 0.0 collective-permute-done.4.refs_2_.refs_1_
  11.8 1.6 %shard_map.75 = (f32[512,128]{1,0:T(8,128)S(1)}, bf16[512,128]{1,0:T(8,128)(2,1)S(1)}) custom-call(f32[8,128]{1,0:T(8,128)S(1)} %get-tuple-element.21.refs_0_.own_points, f32[8,128]{1,0:T(8,128)S(1)} %collective-permute-done.refs_1_.far_points, bf16[4,144,128]{2,1,0:T(8,128)(2,1)S(1)} %collective-permute-done.4.refs_2_.refs_1_, f32[512,128]{1,0:T(8,128)S(1)} %shard_map.74.refs_3_), custom_call_target="tpu_custom_call" | custom-call | tf_op jit(solution)/shard_map/pallas_call | solution.py:343
  13.4 1.5 %collective-permute-start.5 = (bf16[512,128]{1,0:T(8,128)(2,1)S(1)}, bf16[512,128]{1,0:T(8,128)(2,1)S(1)}, u32[]{:S(2)}, u32[]{:S(2)}) collective-permute-start(bf16[512,128]{1,0:T(8,128)(2,1)S(1)} %get-tuple-element.28), channel_id=1, source_target_pairs={{0,3},{1,2},{2,1},{3,0},{4,7},{5,6},{6,5},{7,4},{8,11},{9,10},{10,... | collective-permute-start | bytes 393224 | tf_op jit(solution)/shard_map/ppermute | solution.py:297
  14.9 2.1 %shard_map.76 = (bf16[512,512]{1,0:T(8,128)(2,1)S(1)}, bf16[512,512]{1,0:T(8,128)(2,1)S(1)}, bf16[512,512]{1,0:T(8,128)(2,1)S(1)}, bf16[512,512]{1,0:T(8,128)(2,1)S(1)}) custom-call(f32[8,128]{1,0:T(8,128)S(1)} %get-tuple-element.21.refs_0_.own_points, f32[8,128]{1,0:T(8,128)S(1)} %collective-permute-done.refs_1_.far_points, ...), custom_call_target="tpu_custom_call" | custom-call | flops 15728640 | tf_op jit(solution)/shard_map/pallas_call | solution.py:356
  17.0 1.9 %collective-permute-done.5.theirs = bf16[512,128]{1,0:T(8,128)(2,1)S(1)} collective-permute-done((bf16[512,128]{1,0:T(8,128)(2,1)S(1)}, bf16[512,128]{1,0:T(8,128)(2,1)S(1)}, u32[]{:S(2)}, u32[]{:S(2)}) %collective-permute-start.5) | collective-permute-done | bytes 131104 | tf_op jit(solution)/shard_map/ppermute | solution.py:297
  18.9 0.5 %shard_map.77 = (bf16[512,128]{1,0:T(8,128)(2,1)S(1)}, bf16[512,128]{1,0:T(8,128)(2,1)S(1)}) custom-call(f32[512,128]{1,0:T(8,128)S(1)} %get-tuple-element.27.mine, bf16[512,128]{1,0:T(8,128)(2,1)S(1)} %collective-permute-done.5.theirs, bf16[512,512]{1,0:T(8,128)(2,1)S(1)} %get-tuple-element.29.kernel_re, bf16[512,512]{1,0:T(8,128)(2,1)S(1)} %get-tuple-element.30.kernel_im), custom_call_target="tpu_custom_call" | custom-call | tf_op jit(solution)/shard_map/pallas_call | solution.py:362
  19.5 0.5 %collective-permute-start.6 = (bf16[512,128]{1,0:T(8,128)(2,1)S(1)}, bf16[512,128]{1,0:T(8,128)(2,1)S(1)}, u32[]{:S(2)}, u32[]{:S(2)}) collective-permute-start(bf16[512,128]{1,0:T(8,128)(2,1)S(1)} %get-tuple-element.34), channel_id=1, source_target_pairs={{0,1},{1,0},{2,3},{3,2},{4,5},{5,4},{6,7},{7,6},{8,9},{9,8},{10,11... | collective-permute-start | bytes 393224 | tf_op jit(solution)/shard_map/ppermute | solution.py:297
  19.9 0.5 %shard_map.78.mine = f32[512,128]{1,0:T(8,128)S(1)} custom-call(bf16[512,128]{1,0:T(8,128)(2,1)S(1)} %get-tuple-element.31.currents, bf16[512,512]{1,0:T(8,128)(2,1)S(1)} %get-tuple-element.32.kernel_re, bf16[512,512]{1,0:T(8,128)(2,1)S(1)} %get-tuple-element.33.kernel_im), custom_call_target="tpu_custom_call" | custom-call | tf_op jit(solution)/shard_map/pallas_call | solution.py:366
  20.4 0.5 %collective-permute-done.6.theirs = bf16[512,128]{1,0:T(8,128)(2,1)S(1)} collective-permute-done((bf16[512,128]{1,0:T(8,128)(2,1)S(1)}, bf16[512,128]{1,0:T(8,128)(2,1)S(1)}, u32[]{:S(2)}, u32[]{:S(2)}) %collective-permute-start.6) | collective-permute-done | bytes 131104 | tf_op jit(solution)/shard_map/ppermute | solution.py:297
  21.0 2.9 %collective-permute-start.9 = (bf16[128,128]{1,0:T(8,128)(2,1)S(1)}, bf16[128,128]{1,0:T(8,128)(2,1)S(1)}, u32[]{:S(2)}, u32[]{:S(2)}) collective-permute-start(bf16[128,128]{1,0:T(8,128)(2,1)S(1)} %get-tuple-element.37), channel_id=1, source_target_pairs={{13,0},{12,1},{15,2},{14,3},{9,4},{8,5},{11,6},{10,7},{5,8},{4,9},... | collective-permute-start | bytes 98312 | tf_op jit(solution)/shard_map/ppermute | solution.py:297
  23.9 0.0 collective-permute-start.8
  23.9 1.2 %collective-permute-start.7 = (bf16[128,128]{1,0:T(8,128)(2,1)S(1)}, bf16[128,128]{1,0:T(8,128)(2,1)S(1)}, u32[]{:S(2)}, u32[]{:S(2)}) collective-permute-start(bf16[128,128]{1,0:T(8,128)(2,1)S(1)} %get-tuple-element.39), channel_id=1, source_target_pairs={{5,0},{4,1},{7,2},{6,3},{1,4},{0,5},{3,6},{2,7},{13,8},{12,9},{15,... | collective-permute-start | bytes 98312 | tf_op jit(solution)/shard_map/ppermute | solution.py:297
  25.1 1.1 %collective-permute-done.9.refs_2_ = bf16[128,128]{1,0:T(8,128)(2,1)S(1)} collective-permute-done((bf16[128,128]{1,0:T(8,128)(2,1)S(1)}, bf16[128,128]{1,0:T(8,128)(2,1)S(1)}, u32[]{:S(2)}, u32[]{:S(2)}) %collective-permute-start.9) | collective-permute-done | bytes 32800 | tf_op jit(solution)/shard_map/ppermute | solution.py:297
  26.2 2.0 %collective-permute-done.8.refs_1_ = bf16[128,128]{1,0:T(8,128)(2,1)S(1)} collective-permute-done((bf16[128,128]{1,0:T(8,128)(2,1)S(1)}, bf16[128,128]{1,0:T(8,128)(2,1)S(1)}, u32[]{:S(2)}, u32[]{:S(2)}) %collective-permute-start.8) | collective-permute-done | bytes 32800 | tf_op jit(solution)/shard_map/ppermute | solution.py:297
  28.2 0.0 collective-permute-done.7.refs_0_
  28.2 0.6 %shard_map.80 = f32[128,128]{1,0:T(8,128)} custom-call(f32[128,128]{1,0:T(8,128)S(1)} %get-tuple-element.35.kept, bf16[128,128]{1,0:T(8,128)(2,1)S(1)} %collective-permute-done.7.refs_0_, bf16[128,128]{1,0:T(8,128)(2,1)S(1)} %collective-permute-done.8.refs_1_, bf16[128,128]{1,0:T(8,128)(2,1)S(1)} %collective-permute-done.9.refs_2_), custom_call_target="tpu_custom_call" | custom-call | tf_op jit(solution)/shard_map/pallas_call | solution.py:372
  (3 shorter events, 0.1 us)
Async XLA Ops:
  0.9 8.2 %collective-permute-start.3 = (bf16[144,128]{1,0:T(8,128)(2,1)S(1)}, bf16[144,128]{1,0:T(8,128)(2,1)S(1)}, u32[]{:S(2)}, u32[]{:S(2)}) collective-permute-start(bf16[144,128]{1,0:T(8,128)(2,1)S(1)} %get-tuple-element.22), channel_id=1, source_target_pairs={{0,13},{1,12},{2,15},{3,14},{4,9},{5,8},{6,11},{7,10},{8,5},{9,4},... | collective-permute-start | bytes 110600 | tf_op jit(solution)/shard_map/ppermute | solution.py:297
  5.7 4.3 %collective-permute-start.2 = (bf16[144,128]{1,0:T(8,128)(2,1)S(1)}, bf16[144,128]{1,0:T(8,128)(2,1)S(1)}, u32[]{:S(2)}, u32[]{:S(2)}) collective-permute-start(bf16[144,128]{1,0:T(8,128)(2,1)S(1)} %get-tuple-element.22), channel_id=1, source_target_pairs={{0,9},{1,8},{2,11},{3,10},{4,13},{5,12},{6,15},{7,14},{8,1},{9,0},... | collective-permute-start | bytes 110600 | tf_op jit(solution)/shard_map/ppermute | solution.py:297
  5.7 4.3 %collective-permute-start.1 = (bf16[144,128]{1,0:T(8,128)(2,1)S(1)}, bf16[144,128]{1,0:T(8,128)(2,1)S(1)}, u32[]{:S(2)}, u32[]{:S(2)}) collective-permute-start(bf16[144,128]{1,0:T(8,128)(2,1)S(1)} %get-tuple-element.22), channel_id=1, source_target_pairs={{0,5},{1,4},{2,7},{3,6},{4,1},{5,0},{6,3},{7,2},{8,13},{9,12},{10,... | collective-permute-start | bytes 110600 | tf_op jit(solution)/shard_map/ppermute | solution.py:297
  5.8 3.4 %collective-permute-start = (f32[8,128]{1,0:T(8,128)S(1)}, f32[8,128]{1,0:T(8,128)S(1)}, u32[]{:S(2)}, u32[]{:S(2)}) collective-permute-start(f32[8,128]{1,0:T(8,128)S(1)} %get-tuple-element.21.refs_0_.own_points), channel_id=1, source_target_pairs={{0,3},{1,2},{2,1},{3,0},{4,7},{5,6},{6,5},{7,4},{8,11},{9,10},{10,... | collective-permute-start | bytes 12296 | tf_op jit(solution)/shard_map/ppermute | solution.py:297
  10.0 1.8 %collective-permute-start.4 = (bf16[4,144,128]{2,1,0:T(8,128)(2,1)S(1)}, bf16[4,144,128]{2,1,0:T(8,128)(2,1)S(1)}, u32[]{:S(2)}, u32[]{:S(2)}) collective-permute-start(bf16[4,144,128]{2,1,0:T(8,128)(2,1)S(1)} %pad_maximum_fusion.refs_2_.refs_0_), channel_id=1, source_target_pairs={{0,1},{1,0},{2,3},{3,2},{4,5},{5,4},{6,7},{7,6},{8,9},{9,8},{10,11... | collective-permute-start | bytes 442376 | tf_op jit(solution)/shard_map/ppermute | solution.py:297
  13.4 5.6 %collective-permute-start.5 = (bf16[512,128]{1,0:T(8,128)(2,1)S(1)}, bf16[512,128]{1,0:T(8,128)(2,1)S(1)}, u32[]{:S(2)}, u32[]{:S(2)}) collective-permute-start(bf16[512,128]{1,0:T(8,128)(2,1)S(1)} %get-tuple-element.28), channel_id=1, source_target_pairs={{0,3},{1,2},{2,1},{3,0},{4,7},{5,6},{6,5},{7,4},{8,11},{9,10},{10,... | collective-permute-start | bytes 393224 | tf_op jit(solution)/shard_map/ppermute | solution.py:297
  19.5 1.4 %collective-permute-start.6 = (bf16[512,128]{1,0:T(8,128)(2,1)S(1)}, bf16[512,128]{1,0:T(8,128)(2,1)S(1)}, u32[]{:S(2)}, u32[]{:S(2)}) collective-permute-start(bf16[512,128]{1,0:T(8,128)(2,1)S(1)} %get-tuple-element.34), channel_id=1, source_target_pairs={{0,1},{1,0},{2,3},{3,2},{4,5},{5,4},{6,7},{7,6},{8,9},{9,8},{10,11... | collective-permute-start | bytes 393224 | tf_op jit(solution)/shard_map/ppermute | solution.py:297
  21.0 5.2 %collective-permute-start.9 = (bf16[128,128]{1,0:T(8,128)(2,1)S(1)}, bf16[128,128]{1,0:T(8,128)(2,1)S(1)}, u32[]{:S(2)}, u32[]{:S(2)}) collective-permute-start(bf16[128,128]{1,0:T(8,128)(2,1)S(1)} %get-tuple-element.37), channel_id=1, source_target_pairs={{13,0},{12,1},{15,2},{14,3},{9,4},{8,5},{11,6},{10,7},{5,8},{4,9},... | collective-permute-start | bytes 98312 | tf_op jit(solution)/shard_map/ppermute | solution.py:297
  23.9 4.2 %collective-permute-start.8 = (bf16[128,128]{1,0:T(8,128)(2,1)S(1)}, bf16[128,128]{1,0:T(8,128)(2,1)S(1)}, u32[]{:S(2)}, u32[]{:S(2)}) collective-permute-start(bf16[128,128]{1,0:T(8,128)(2,1)S(1)} %get-tuple-element.38), channel_id=1, source_target_pairs={{9,0},{8,1},{11,2},{10,3},{13,4},{12,5},{15,6},{14,7},{1,8},{0,9},... | collective-permute-start | bytes 98312 | tf_op jit(solution)/shard_map/ppermute | solution.py:297
  23.9 4.2 %collective-permute-start.7 = (bf16[128,128]{1,0:T(8,128)(2,1)S(1)}, bf16[128,128]{1,0:T(8,128)(2,1)S(1)}, u32[]{:S(2)}, u32[]{:S(2)}) collective-permute-start(bf16[128,128]{1,0:T(8,128)(2,1)S(1)} %get-tuple-element.39), channel_id=1, source_target_pairs={{5,0},{4,1},{7,2},{6,3},{1,4},{0,5},{3,6},{2,7},{13,8},{12,9},{15,... | collective-permute-start | bytes 98312 | tf_op jit(solution)/shard_map/ppermute | solution.py:297

commit v5 on v4

--- a/solution.py
+++ b/solution.py
@@ -62,7 +62,7 @@
         pltpu.make_async_copy(source, target, sems.at[at])
         for at, (source, target) in enumerate(zip(sources, targets))
     ]
-    for copy in copies:
+    for copy in copies[::-1]:
         copy.start()
     for copy in copies[:4]:
         copy.wait()
@@ -189,12 +189,11 @@
     groups = refs[:2]
     outs = refs[2:6]
     columns, rows = refs[6:]
-    count, height, lanes = groups[0].shape
-    sources = height - PACK_ROWS
+    count, _, lanes = groups[0].shape
     size = count * lanes
     for which, messages in enumerate(groups):
         for at in range(count):
-            uv = unpack(messages[at, sources:, :])[3:5]
+            uv = unpack(messages[at])[3:5]
             normal = jnp.sqrt(1.0 - uv[0:1] * uv[0:1] - uv[1:2] * uv[1:2])
             pad = jnp.zeros((5, lanes), F32)
             base = which * size + at * lanes
@@ -241,17 +240,26 @@
     out[...] = radiate(kernel_re, kernel_im, currents[...])
 
 
-def fold_body(mine, theirs, kept, sent):
-    first = kept.shape[0]
+def fold_body(mine, theirs, *outs):
     total = mine[...] + theirs[...].astype(F32)
-    kept[...] = total[:first]
-    sent[...] = total[first:].astype(BF16)
+    start = 0
+    for out in outs:
+        out[...] = total[start : start + out.shape[0]].astype(out.dtype)
+        start += out.shape[0]
+
+
+def pass_body(*refs):
+    total = refs[0][...].astype(F32)
+    for ref in refs[1:-1]:
+        total = total + ref[...].astype(F32)
+    refs[-1][...] = total.astype(BF16)
 
 
 def finish_body(kept, *refs):
     total = kept[...]
+    rows = total.shape[0]
     for ref in refs[:-1]:
-        total = total + ref[...].astype(F32)
+        total = total + ref[0:rows, :].astype(F32)
     refs[-1][...] = total
 
 
@@ -292,8 +300,10 @@
             out.append((at, to * 4 + (place ^ near)))
         return out
 
-    def swap(x, step, back=False):
+    def swap(x, step, back=False, odd_step=None):
         links = pairs(step)
+        if odd_step is not None:
+            links = links[::2] + pairs(odd_step)[1::2]
         return lax.ppermute(x, "refl", [(b, a) for a, b in links] if back else links)
 
     message, points = call(
@@ -352,23 +362,46 @@
     mine, told = green(sets, side_messages, bases, [F32, BF16])
     theirs = swap(told, 3)
 
+    even = lax.rem(lax.axis_index("refl"), 2) == 0
+    near, side = ([x[k, sources:] for k in range(line)] for x in (near_messages, side_messages))
+    keep, give = [near[0]], [side[0]]
+    middle = [line // 2] if line % 2 == 0 and line > 1 else []
+    for k in middle:
+        keep.append(near[k])
+        give.append(side[k])
+    couples = [(k, line - k) for k in range(1, (line + 1) // 2)]
+    for low, high in couples:
+        keep += [jnp.where(even, side[low], side[high]), jnp.where(even, near[low], near[high])]
+        give += [jnp.where(even, near[high], near[low]), jnp.where(even, side[high], side[low])]
+
     count = line * directions
     near_re, near_im, side_re, side_im = call(
         kernel_body,
         [((count, half_points), BF16)] * 4,
         [pltpu.VMEM((2 * count, 8), F32), pltpu.VMEM((8, half_points), F32)],
         60 * count * half_points,
-    )(points, far_points, near_messages, side_messages)
+    )(points, far_points, jnp.stack(keep), jnp.stack(give))
     currents, told = call(side_body, [((half_points, lanes), BF16), ((count, lanes), BF16)])(
         mine, theirs, side_re, side_im
     )
     given = swap(told, 1)
     near = call(near_body, [((count, lanes), F32)])(currents, near_re, near_im)[0]
-    kept, sent = call(
-        fold_body, [((directions, lanes), F32), (((line - 1) * directions, lanes), BF16)]
+    block, double = (directions, lanes), (2 * directions, lanes)
+    kept, *sent = call(
+        fold_body,
+        [(block, F32)] + [(block, BF16)] * len(middle) + [(double, BF16)] * len(couples),
     )(near, given)
-    sent = sent.reshape(line - 1, directions, lanes)
-    arrived = [swap(sent[k - 1], 4 * k + 1, back=True) for k in range(1, line)]
+    doubles = [
+        swap(x, 4 * low, back=True, odd_step=4 * high)
+        for x, (low, high) in zip(sent[len(middle) :], couples)
+    ]
+    singles = [swap(x, 4 * k + 1, back=True) for x, k in zip(sent, middle)]
+    arrived = singles + doubles
+    if doubles:
+        passed = [x[directions:] for x in doubles]
+        if len(passed) > 1:
+            passed = call(pass_body, [(block, BF16)])(*passed)
+        arrived.append(swap(passed[0], 1))
     return call(finish_body, [((directions, lanes), F32)])(kept, *arrived)[0]
 
 

time: 29.1 us -> 28.7 us (0.986)
  starting transfers between devices: 13 us -> 12.5 us
  waiting for transfers between devices: 7.88 us -> 8.2 us
    ppermute x10, starting transfers between devices: 13 us -> 12.5 us  [swap(): lax.ppermute(x, 'refl', [(b, a) for a, b in links] if back else links)]
    ppermute x10, waiting for transfers between devices: 7.88 us -> 8.2 us  [swap(): lax.ppermute(x, 'refl', [(b, a) for a, b in links] if back else links)]
  transfers between devices with their start and end apart: 10 -> 10, of which waited for: 6 -> 6; matrix products, arithmetic and copies ran while one was open for 0% -> 0% of each run, Pallas kernels for 14% -> 15%
where the time goes in v5:
time: 28.7 us; the launch traced here: 28.5 us
  starting transfers between devices  12.5 us (44%)
  waiting for transfers between devices  8.2 us (29%)
  Pallas kernels  7.76 us (27%)
    ppermute x10, starting transfers between devices, swap(): lax.ppermute(x, 'refl', [(b, a) for a, b in links] if back else links)  12.5 us
    ppermute x10, waiting for transfers between devices, swap(): lax.ppermute(x, 'refl', [(b, a) for a, b in links] if back else links)  8.2 us
    pallas_call x2, Pallas kernels, green(): call(functools.partial(green_body, len(points), len(bases), scale), [((ro...  3.12 us
    pallas_call x1, Pallas kernels, per_device(): call(kernel_body, [((count, half_points), BF16)] * 4, [pltpu.VMEM((2 * co...  2.1 us
    pallas_call x1, Pallas kernels, per_device(): call(pack_body, [((sources + PACK_ROWS, lanes), BF16), ((8, lanes), F32)]...  0.85 us
    pallas_call x1, Pallas kernels, per_device(): return call(finish_body, [((directions, lanes), F32)])(kept, *arrived)[0]  0.65 us
  transfers between devices with their start and end apart: 10, of which 6 were waited for; matrix products, arithmetic and copies ran while one was open for 0% of the time, Pallas kernels for 15%

profile of v5, /device:TPU:1, one launch (start us, length us, event | category | flops | bytes accessed | tf_op | source)
XLA Modules:
  0.0 28.5 jit_solution(14359590498094822686)
XLA Ops:
  0.0 0.9 %shard_map.73 = (bf16[144,128]{1,0:T(8,128)(2,1)S(1)}, f32[8,128]{1,0:T(8,128)S(1)}) custom-call(bf16[128,128]{1,0:T(8,128)(2,1)} %weights.1, f32[2,128]{1,0:T(2,128)} %feed_plane.1, f32[1,128]{1,0:T(1,128)} %bitcast.17, f32[2,128]{1,0:T(2,128)} %cosines.1, f32[2,256]{1,0:T(2,128)} %plane.1, f32[2,128]{1,0:T(2,128)} %bitcast.15, f32[2,128]{1,0:T(2,128)} %bitcast.16), custom_call_target="tpu_custom_call" | custom-call | tf_op jit(solution)/shard_map/pallas_call | solution.py:309
  0.9 4.8 %collective-permute-start.3 = (bf16[144,128]{1,0:T(8,128)(2,1)S(1)}, bf16[144,128]{1,0:T(8,128)(2,1)S(1)}, u32[]{:S(2)}, u32[]{:S(2)}) collective-permute-start(bf16[144,128]{1,0:T(8,128)(2,1)S(1)} %get-tuple-element.23), channel_id=1, source_target_pairs={{0,13},{1,12},{2,15},{3,14},{4,9},{5,8},{6,11},{7,10},{8,5},{9,4},... | collective-permute-start | bytes 110600 | tf_op jit(solution)/shard_map/ppermute | solution.py:307
  5.6 0.0 collective-permute-start.2
  5.6 0.1 collective-permute-start.1
  5.7 1.8 %collective-permute-start = (f32[8,128]{1,0:T(8,128)S(1)}, f32[8,128]{1,0:T(8,128)S(1)}, u32[]{:S(2)}, u32[]{:S(2)}) collective-permute-start(f32[8,128]{1,0:T(8,128)S(1)} %get-tuple-element.22.refs_0_.own_points), channel_id=1, source_target_pairs={{0,3},{1,2},{2,1},{3,0},{4,7},{5,6},{6,5},{7,4},{8,11},{9,10},{10,... | collective-permute-start | bytes 12296 | tf_op jit(solution)/shard_map/ppermute | solution.py:307
  7.5 1.6 %collective-permute-done.refs_1_.far_points = f32[8,128]{1,0:T(8,128)S(1)} collective-permute-done((f32[8,128]{1,0:T(8,128)S(1)}, f32[8,128]{1,0:T(8,128)S(1)}, u32[]{:S(2)}, u32[]{:S(2)}) %collective-permute-start) | collective-permute-done | bytes 4128 | tf_op jit(solution)/shard_map/ppermute | solution.py:307
  9.1 0.0 collective-permute-done.3
  9.1 0.8 %collective-permute-done.2 = bf16[144,128]{1,0:T(8,128)(2,1)S(1)} collective-permute-done((bf16[144,128]{1,0:T(8,128)(2,1)S(1)}, bf16[144,128]{1,0:T(8,128)(2,1)S(1)}, u32[]{:S(2)}, u32[]{:S(2)}) %collective-permute-start.2) | collective-permute-done | bytes 36896 | tf_op jit(solution)/shard_map/ppermute | solution.py:307
  9.9 0.0 collective-permute-done.1
  10.0 0.2 collective-permute-start.4
  10.2 1.5 %shard_map.74.refs_3_ = f32[512,128]{1,0:T(8,128)S(1)} custom-call(f32[8,128]{1,0:T(8,128)S(1)} %get-tuple-element.22.refs_0_.own_points, f32[8,128]{1,0:T(8,128)S(1)} %collective-permute-done.refs_1_.far_points, bf16[4,144,128]{2,1,0:T(8,128)(2,1)S(1)} %pad_maximum_fusion.refs_2_), custom_call_target="tpu_custom_call" | custom-call | tf_op jit(solution)/shard_map/pallas_call | solution.py:353
  11.8 0.0 collective-permute-done.4.refs_2_
  11.8 1.6 %shard_map.75 = (f32[512,128]{1,0:T(8,128)S(1)}, bf16[512,128]{1,0:T(8,128)(2,1)S(1)}) custom-call(f32[8,128]{1,0:T(8,128)S(1)} %get-tuple-element.22.refs_0_.own_points, f32[8,128]{1,0:T(8,128)S(1)} %collective-permute-done.refs_1_.far_points, bf16[4,144,128]{2,1,0:T(8,128)(2,1)S(1)} %collective-permute-done.4.refs_2_, f32[512,128]{1,0:T(8,128)S(1)} %shard_map.74.refs_3_), custom_call_target="tpu_custom_call" | custom-call | tf_op jit(solution)/shard_map/pallas_call | solution.py:353
  13.4 1.5 %collective-permute-start.5 = (bf16[512,128]{1,0:T(8,128)(2,1)S(1)}, bf16[512,128]{1,0:T(8,128)(2,1)S(1)}, u32[]{:S(2)}, u32[]{:S(2)}) collective-permute-start(bf16[512,128]{1,0:T(8,128)(2,1)S(1)} %get-tuple-element.29), channel_id=1, source_target_pairs={{0,3},{1,2},{2,1},{3,0},{4,7},{5,6},{6,5},{7,4},{8,11},{9,10},{10,... | collective-permute-start | bytes 393224 | tf_op jit(solution)/shard_map/ppermute | solution.py:307
  14.9 2.1 %shard_map.76 = (bf16[512,512]{1,0:T(8,128)(2,1)S(1)}, bf16[512,512]{1,0:T(8,128)(2,1)S(1)}, bf16[512,512]{1,0:T(8,128)(2,1)S(1)}, bf16[512,512]{1,0:T(8,128)(2,1)S(1)}) custom-call(f32[8,128]{1,0:T(8,128)S(1)} %get-tuple-element.22.refs_0_.own_points, f32[8,128]{1,0:T(8,128)S(1)} %collective-permute-done.refs_1_.far_points, ...), custom_call_target="tpu_custom_call" | custom-call | flops 15728640 | tf_op jit(solution)/shard_map/pallas_call | solution.py:378
  17.0 1.9 %collective-permute-done.5.theirs = bf16[512,128]{1,0:T(8,128)(2,1)S(1)} collective-permute-done((bf16[512,128]{1,0:T(8,128)(2,1)S(1)}, bf16[512,128]{1,0:T(8,128)(2,1)S(1)}, u32[]{:S(2)}, u32[]{:S(2)}) %collective-permute-start.5) | collective-permute-done | bytes 131104 | tf_op jit(solution)/shard_map/ppermute | solution.py:307
  18.9 0.5 %shard_map.77 = (bf16[512,128]{1,0:T(8,128)(2,1)S(1)}, bf16[512,128]{1,0:T(8,128)(2,1)S(1)}) custom-call(f32[512,128]{1,0:T(8,128)S(1)} %get-tuple-element.28.mine, bf16[512,128]{1,0:T(8,128)(2,1)S(1)} %collective-permute-done.5.theirs, bf16[512,512]{1,0:T(8,128)(2,1)S(1)} %get-tuple-element.30.kernel_re, bf16[512,512]{1,0:T(8,128)(2,1)S(1)} %get-tuple-element.31.kernel_im), custom_call_target="tpu_custom_call" | custom-call | tf_op jit(solution)/shard_map/pallas_call | solution.py:384
  19.4 0.4 %collective-permute-start.6 = (bf16[512,128]{1,0:T(8,128)(2,1)S(1)}, bf16[512,128]{1,0:T(8,128)(2,1)S(1)}, u32[]{:S(2)}, u32[]{:S(2)}) collective-permute-start(bf16[512,128]{1,0:T(8,128)(2,1)S(1)} %get-tuple-element.35), channel_id=1, source_target_pairs={{0,1},{1,0},{2,3},{3,2},{4,5},{5,4},{6,7},{7,6},{8,9},{9,8},{10,11... | collective-permute-start | bytes 393224 | tf_op jit(solution)/shard_map/ppermute | solution.py:307
  19.8 0.5 %shard_map.78.mine = f32[512,128]{1,0:T(8,128)S(1)} custom-call(bf16[512,128]{1,0:T(8,128)(2,1)S(1)} %get-tuple-element.32.currents, bf16[512,512]{1,0:T(8,128)(2,1)S(1)} %get-tuple-element.33.kernel_re, bf16[512,512]{1,0:T(8,128)(2,1)S(1)} %get-tuple-element.34.kernel_im), custom_call_target="tpu_custom_call" | custom-call | tf_op jit(solution)/shard_map/pallas_call | solution.py:388
  20.3 0.5 %collective-permute-done.6.theirs = bf16[512,128]{1,0:T(8,128)(2,1)S(1)} collective-permute-done((bf16[512,128]{1,0:T(8,128)(2,1)S(1)}, bf16[512,128]{1,0:T(8,128)(2,1)S(1)}, u32[]{:S(2)}, u32[]{:S(2)}) %collective-permute-start.6) | collective-permute-done | bytes 131104 | tf_op jit(solution)/shard_map/ppermute | solution.py:307
  20.8 2.8 %collective-permute-start.8 = (bf16[256,128]{1,0:T(8,128)(2,1)S(1)}, bf16[256,128]{1,0:T(8,128)(2,1)S(1)}, u32[]{:S(2)}, u32[]{:S(2)}) collective-permute-start(bf16[256,128]{1,0:T(8,128)(2,1)S(1)} %get-tuple-element.38), channel_id=1, source_target_pairs={{4,0},{6,2},{0,4},{2,6},{12,8},{14,10},{8,12},{10,14},{13,1},{15,3... | collective-permute-start | bytes 196616 | tf_op jit(solution)/shard_map/ppermute | solution.py:307
  23.6 0.8 %collective-permute-start.7 = (bf16[128,128]{1,0:T(8,128)(2,1)S(1)}, bf16[128,128]{1,0:T(8,128)(2,1)S(1)}, u32[]{:S(2)}, u32[]{:S(2)}) collective-permute-start(bf16[128,128]{1,0:T(8,128)(2,1)S(1)} %get-tuple-element.37), channel_id=1, source_target_pairs={{9,0},{8,1},{11,2},{10,3},{13,4},{12,5},{15,6},{14,7},{1,8},{0,9},... | collective-permute-start | bytes 98312 | tf_op jit(solution)/shard_map/ppermute | solution.py:307
  24.5 1.8 %collective-permute-done.8.refs_1_ = bf16[256,128]{1,0:T(8,128)(2,1)S(1)} collective-permute-done((bf16[256,128]{1,0:T(8,128)(2,1)S(1)}, bf16[256,128]{1,0:T(8,128)(2,1)S(1)}, u32[]{:S(2)}, u32[]{:S(2)}) %collective-permute-start.8) | collective-permute-done | bytes 65568 | tf_op jit(solution)/shard_map/ppermute | solution.py:307
  26.3 0.0 collective-permute-start.9
  26.3 1.6 %collective-permute-done.7.refs_0_ = bf16[128,128]{1,0:T(8,128)(2,1)S(1)} collective-permute-done((bf16[128,128]{1,0:T(8,128)(2,1)S(1)}, bf16[128,128]{1,0:T(8,128)(2,1)S(1)}, u32[]{:S(2)}, u32[]{:S(2)}) %collective-permute-start.7) | collective-permute-done | bytes 32800 | tf_op jit(solution)/shard_map/ppermute | solution.py:307
  27.9 0.0 collective-permute-done.9.refs_2_
  27.9 0.6 %shard_map.80 = f32[128,128]{1,0:T(8,128)} custom-call(f32[128,128]{1,0:T(8,128)S(1)} %get-tuple-element.36.kept, bf16[128,128]{1,0:T(8,128)(2,1)S(1)} %collective-permute-done.7.refs_0_, bf16[256,128]{1,0:T(8,128)(2,1)S(1)} %collective-permute-done.8.refs_1_, bf16[128,128]{1,0:T(8,128)(2,1)S(1)} %collective-permute-done.9.refs_2_), custom_call_target="tpu_custom_call" | custom-call | tf_op jit(solution)/shard_map/pallas_call | solution.py:405
  (8 shorter events, 0.1 us)
Async XLA Ops:
  0.9 8.2 %collective-permute-start.3 = (bf16[144,128]{1,0:T(8,128)(2,1)S(1)}, bf16[144,128]{1,0:T(8,128)(2,1)S(1)}, u32[]{:S(2)}, u32[]{:S(2)}) collective-permute-start(bf16[144,128]{1,0:T(8,128)(2,1)S(1)} %get-tuple-element.23), channel_id=1, source_target_pairs={{0,13},{1,12},{2,15},{3,14},{4,9},{5,8},{6,11},{7,10},{8,5},{9,4},... | collective-permute-start | bytes 110600 | tf_op jit(solution)/shard_map/ppermute | solution.py:307
  5.6 4.3 %collective-permute-start.2 = (bf16[144,128]{1,0:T(8,128)(2,1)S(1)}, bf16[144,128]{1,0:T(8,128)(2,1)S(1)}, u32[]{:S(2)}, u32[]{:S(2)}) collective-permute-start(bf16[144,128]{1,0:T(8,128)(2,1)S(1)} %get-tuple-element.23), channel_id=1, source_target_pairs={{0,9},{1,8},{2,11},{3,10},{4,13},{5,12},{6,15},{7,14},{8,1},{9,0},... | collective-permute-start | bytes 110600 | tf_op jit(solution)/shard_map/ppermute | solution.py:307
  5.6 4.3 %collective-permute-start.1 = (bf16[144,128]{1,0:T(8,128)(2,1)S(1)}, bf16[144,128]{1,0:T(8,128)(2,1)S(1)}, u32[]{:S(2)}, u32[]{:S(2)}) collective-permute-start(bf16[144,128]{1,0:T(8,128)(2,1)S(1)} %get-tuple-element.23), channel_id=1, source_target_pairs={{0,5},{1,4},{2,7},{3,6},{4,1},{5,0},{6,3},{7,2},{8,13},{9,12},{10,... | collective-permute-start | bytes 110600 | tf_op jit(solution)/shard_map/ppermute | solution.py:307
  5.7 3.4 %collective-permute-start = (f32[8,128]{1,0:T(8,128)S(1)}, f32[8,128]{1,0:T(8,128)S(1)}, u32[]{:S(2)}, u32[]{:S(2)}) collective-permute-start(f32[8,128]{1,0:T(8,128)S(1)} %get-tuple-element.22.refs_0_.own_points), channel_id=1, source_target_pairs={{0,3},{1,2},{2,1},{3,0},{4,7},{5,6},{6,5},{7,4},{8,11},{9,10},{10,... | collective-permute-start | bytes 12296 | tf_op jit(solution)/shard_map/ppermute | solution.py:307
  10.0 1.8 %collective-permute-start.4 = (bf16[4,144,128]{2,1,0:T(8,128)(2,1)S(1)}, bf16[4,144,128]{2,1,0:T(8,128)(2,1)S(1)}, u32[]{:S(2)}, u32[]{:S(2)}) collective-permute-start(bf16[4,144,128]{2,1,0:T(8,128)(2,1)S(1)} %pad_maximum_fusion.refs_2_), channel_id=1, source_target_pairs={{0,1},{1,0},{2,3},{3,2},{4,5},{5,4},{6,7},{7,6},{8,9},{9,8},{10,11... | collective-permute-start | bytes 442376 | tf_op jit(solution)/shard_map/ppermute | solution.py:307
  13.4 5.5 %collective-permute-start.5 = (bf16[512,128]{1,0:T(8,128)(2,1)S(1)}, bf16[512,128]{1,0:T(8,128)(2,1)S(1)}, u32[]{:S(2)}, u32[]{:S(2)}) collective-permute-start(bf16[512,128]{1,0:T(8,128)(2,1)S(1)} %get-tuple-element.29), channel_id=1, source_target_pairs={{0,3},{1,2},{2,1},{3,0},{4,7},{5,6},{6,5},{7,4},{8,11},{9,10},{10,... | collective-permute-start | bytes 393224 | tf_op jit(solution)/shard_map/ppermute | solution.py:307
  19.4 1.4 %collective-permute-start.6 = (bf16[512,128]{1,0:T(8,128)(2,1)S(1)}, bf16[512,128]{1,0:T(8,128)(2,1)S(1)}, u32[]{:S(2)}, u32[]{:S(2)}) collective-permute-start(bf16[512,128]{1,0:T(8,128)(2,1)S(1)} %get-tuple-element.35), channel_id=1, source_target_pairs={{0,1},{1,0},{2,3},{3,2},{4,5},{5,4},{6,7},{7,6},{8,9},{9,8},{10,11... | collective-permute-start | bytes 393224 | tf_op jit(solution)/shard_map/ppermute | solution.py:307
  20.8 5.4 %collective-permute-start.8 = (bf16[256,128]{1,0:T(8,128)(2,1)S(1)}, bf16[256,128]{1,0:T(8,128)(2,1)S(1)}, u32[]{:S(2)}, u32[]{:S(2)}) collective-permute-start(bf16[256,128]{1,0:T(8,128)(2,1)S(1)} %get-tuple-element.38), channel_id=1, source_target_pairs={{4,0},{6,2},{0,4},{2,6},{12,8},{14,10},{8,12},{10,14},{13,1},{15,3... | collective-permute-start | bytes 196616 | tf_op jit(solution)/shard_map/ppermute | solution.py:307
  23.6 4.2 %collective-permute-start.7 = (bf16[128,128]{1,0:T(8,128)(2,1)S(1)}, bf16[128,128]{1,0:T(8,128)(2,1)S(1)}, u32[]{:S(2)}, u32[]{:S(2)}) collective-permute-start(bf16[128,128]{1,0:T(8,128)(2,1)S(1)} %get-tuple-element.37), channel_id=1, source_target_pairs={{9,0},{8,1},{11,2},{10,3},{13,4},{12,5},{15,6},{14,7},{1,8},{0,9},... | collective-permute-start | bytes 98312 | tf_op jit(solution)/shard_map/ppermute | solution.py:307
  26.3 1.6 %collective-permute-start.9 = (bf16[128,128]{1,0:T(8,128)(2,1)S(1)}, bf16[128,128]{1,0:T(8,128)(2,1)S(1)}, u32[]{:S(2)}, u32[]{:S(2)}) collective-permute-start(bf16[128,128]{1,0:T(8,128)(2,1)S(1)} %slice.44), channel_id=1, source_target_pairs={{0,1},{1,0},{2,3},{3,2},{4,5},{5,4},{6,7},{7,6},{8,9},{9,8},{10,11... | collective-permute-start | bytes 98312 | tf_op jit(solution)/shard_map/ppermute | solution.py:307

commit v6 on v5

--- a/solution.py
+++ b/solution.py
@@ -11,8 +11,7 @@
 RANGE_REF = 20.0
 F32, BF16 = jnp.float32, jnp.bfloat16
 
-SIN_HALF = (3.1415902835895886, -5.167407697719414, 2.544020810735872, -0.5594899090940457)
-COS_HALF = (0.9999932952798736, -4.933938014977294, 4.041283824377777, -1.222127057577997)
+SIN_HALF = (3.1415898893585, -5.167370491466989, 2.5435336188246254, -0.557959530770679)
 
 ROUNDER = 1.5 * 2.0**23
 
@@ -30,13 +29,12 @@
     return total
 
 
-def circle(turns, gain):
-    part = turns - ((turns + ROUNDER) - ROUNDER)
-    square = part * part
-    root = math.sqrt(2.0 * abs(gain))
-    half_sin = part * horner(square, SIN_HALF, root)
-    half_cos = horner(square, COS_HALF, 2.0 * gain / root)
-    return abs(gain) - half_sin * half_sin, half_sin * half_cos
+def half_turns(turns, flip):
+    whole = (turns + ROUNDER) - ROUNDER
+    part = whole - turns if flip else turns - whole
+    sine = part * horner(part * part, SIN_HALF, math.sqrt(2.0))
+    rest = jnp.maximum(2.0 - sine * sine, 1e-12)
+    return sine, rest * lax.rsqrt(rest)
 
 
 def turned(columns):
@@ -144,7 +142,7 @@
         where = slice(at * sources, (at + 1) * sources)
         coords = unpack(messages[at, sources:, :])
         x, y, z = coords[0:1], coords[1:2], coords[2:3]
-        heights[0:1, where] = z
+        heights[0:1, where] = z * RANGE_REF
         right[:, where] = distance_terms(x, y, z, False).astype(BF16)
         block = messages[at, :sources, :]
         weights[where, :] = block
@@ -156,14 +154,15 @@
             left[start : start + chunk, :], right[...], preferred_element_type=F32
         )
         for at in range(0, chunk, TILE):
-            low = columns[start + at : start + at + TILE, 2:3]
+            low = columns[start + at : start + at + TILE, 2:3] * RANGE_REF
             for part in blocks(count * sources, LANES):
                 squared = squares[at : at + TILE, part]
                 inverse = lax.rsqrt(squared)
-                cosine, sine = circle(squared * inverse, -RANGE_REF)
+                sine, cosine = half_turns(squared * inverse, True)
                 amplitude = (heights[0:1, part] - low) * (inverse * inverse)
-                green_re[at : at + TILE, part] = (amplitude * cosine).astype(BF16)
-                green_im[at : at + TILE, part] = (amplitude * sine).astype(BF16)
+                scaled = amplitude * sine
+                green_re[at : at + TILE, part] = (amplitude - scaled * sine).astype(BF16)
+                green_im[at : at + TILE, part] = (scaled * cosine).astype(BF16)
 
     def add_up(start, green_re, green_im, _):
         here = slice(start, start + chunk)
@@ -215,9 +214,9 @@
                 + columns[from_, 1:2] * rows[1:2, :]
                 + columns[from_, 2:3] * rows[2:3, :]
             )
-            cosine, sine = circle(turns, 1.0)
-            kernel_re[here, :] = cosine.astype(BF16)
-            kernel_im[here, :] = sine.astype(BF16)
+            sine, cosine = half_turns(turns, False)
+            kernel_re[here, :] = (1.0 - sine * sine).astype(BF16)
+            kernel_im[here, :] = (sine * cosine).astype(BF16)
             return carry
 
         lax.fori_loop(0, size // TILE, one, 0, unroll=16)

time: 28.7 us -> 28.6 us (level)
  transfers between devices with their start and end apart: 10 -> 10, of which waited for: 6 -> 6; matrix products, arithmetic and copies ran while one was open for 0% -> 0% of each run, Pallas kernels for 15% -> 14%
where the time goes in v6:
time: 28.6 us; the launch traced here: 28.4 us
  starting transfers between devices  12.4 us (43%)
  waiting for transfers between devices  8.38 us (29%)
  Pallas kernels  7.48 us (26%)
    ppermute x10, starting transfers between devices, swap(): lax.ppermute(x, 'refl', [(b, a) for a, b in links] if back else links)  12.4 us
    ppermute x10, waiting for transfers between devices, swap(): lax.ppermute(x, 'refl', [(b, a) for a, b in links] if back else links)  8.38 us
    pallas_call x2, Pallas kernels, green(): call(functools.partial(green_body, len(points), len(bases), scale), [((ro...  3.02 us
    pallas_call x1, Pallas kernels, per_device(): call(kernel_body, [((count, half_points), BF16)] * 4, [pltpu.VMEM((2 * co...  1.93 us
    pallas_call x1, Pallas kernels, per_device(): call(pack_body, [((sources + PACK_ROWS, lanes), BF16), ((8, lanes), F32)]...  0.85 us
    pallas_call x1, Pallas kernels, per_device(): return call(finish_body, [((directions, lanes), F32)])(kept, *arrived)[0]  0.65 us
  transfers between devices with their start and end apart: 10, of which 6 were waited for; matrix products, arithmetic and copies ran while one was open for 0% of the time, Pallas kernels for 14%

profile of v6, /device:TPU:1, one launch (start us, length us, event | category | flops | bytes accessed | tf_op | source)
XLA Modules:
  0.0 28.4 jit_solution(14846996602529140207)
XLA Ops:
  0.0 0.9 %shard_map.73 = (bf16[144,128]{1,0:T(8,128)(2,1)S(1)}, f32[8,128]{1,0:T(8,128)S(1)}) custom-call(bf16[128,128]{1,0:T(8,128)(2,1)} %weights.1, f32[2,128]{1,0:T(2,128)} %feed_plane.1, f32[1,128]{1,0:T(1,128)} %bitcast.17, f32[2,128]{1,0:T(2,128)} %cosines.1, f32[2,256]{1,0:T(2,128)} %plane.1, f32[2,128]{1,0:T(2,128)} %bitcast.15, f32[2,128]{1,0:T(2,128)} %bitcast.16), custom_call_target="tpu_custom_call" | custom-call | tf_op jit(solution)/shard_map/pallas_call | solution.py:308
  0.9 4.8 %collective-permute-start.3 = (bf16[144,128]{1,0:T(8,128)(2,1)S(1)}, bf16[144,128]{1,0:T(8,128)(2,1)S(1)}, u32[]{:S(2)}, u32[]{:S(2)}) collective-permute-start(bf16[144,128]{1,0:T(8,128)(2,1)S(1)} %get-tuple-element.23), channel_id=1, source_target_pairs={{0,13},{1,12},{2,15},{3,14},{4,9},{5,8},{6,11},{7,10},{8,5},{9,4},... | collective-permute-start | bytes 110600 | tf_op jit(solution)/shard_map/ppermute | solution.py:306
  5.6 0.0 collective-permute-start.2
  5.6 0.1 collective-permute-start.1
  5.7 1.8 %collective-permute-start = (f32[8,128]{1,0:T(8,128)S(1)}, f32[8,128]{1,0:T(8,128)S(1)}, u32[]{:S(2)}, u32[]{:S(2)}) collective-permute-start(f32[8,128]{1,0:T(8,128)S(1)} %get-tuple-element.22.refs_0_.own_points), channel_id=1, source_target_pairs={{0,3},{1,2},{2,1},{3,0},{4,7},{5,6},{6,5},{7,4},{8,11},{9,10},{10,... | collective-permute-start | bytes 12296 | tf_op jit(solution)/shard_map/ppermute | solution.py:306
  7.5 1.6 %collective-permute-done.refs_1_.far_points = f32[8,128]{1,0:T(8,128)S(1)} collective-permute-done((f32[8,128]{1,0:T(8,128)S(1)}, f32[8,128]{1,0:T(8,128)S(1)}, u32[]{:S(2)}, u32[]{:S(2)}) %collective-permute-start) | collective-permute-done | bytes 4128 | tf_op jit(solution)/shard_map/ppermute | solution.py:306
  9.1 0.0 collective-permute-done.3
  9.1 0.8 %collective-permute-done.2 = bf16[144,128]{1,0:T(8,128)(2,1)S(1)} collective-permute-done((bf16[144,128]{1,0:T(8,128)(2,1)S(1)}, bf16[144,128]{1,0:T(8,128)(2,1)S(1)}, u32[]{:S(2)}, u32[]{:S(2)}) %collective-permute-start.2) | collective-permute-done | bytes 36896 | tf_op jit(solution)/shard_map/ppermute | solution.py:306
  9.9 0.0 collective-permute-done.1
  10.0 0.2 collective-permute-start.4
  10.2 1.5 %shard_map.74.refs_3_ = f32[512,128]{1,0:T(8,128)S(1)} custom-call(f32[8,128]{1,0:T(8,128)S(1)} %get-tuple-element.22.refs_0_.own_points, f32[8,128]{1,0:T(8,128)S(1)} %collective-permute-done.refs_1_.far_points, bf16[4,144,128]{2,1,0:T(8,128)(2,1)S(1)} %pad_maximum_fusion.refs_2_), custom_call_target="tpu_custom_call" | custom-call | tf_op jit(solution)/shard_map/pallas_call | solution.py:352
  11.7 0.0 collective-permute-done.4.refs_2_
  11.7 1.5 %shard_map.75 = (f32[512,128]{1,0:T(8,128)S(1)}, bf16[512,128]{1,0:T(8,128)(2,1)S(1)}) custom-call(f32[8,128]{1,0:T(8,128)S(1)} %get-tuple-element.22.refs_0_.own_points, f32[8,128]{1,0:T(8,128)S(1)} %collective-permute-done.refs_1_.far_points, bf16[4,144,128]{2,1,0:T(8,128)(2,1)S(1)} %collective-permute-done.4.refs_2_, f32[512,128]{1,0:T(8,128)S(1)} %shard_map.74.refs_3_), custom_call_target="tpu_custom_call" | custom-call | tf_op jit(solution)/shard_map/pallas_call | solution.py:352
  13.2 1.5 %collective-permute-start.5 = (bf16[512,128]{1,0:T(8,128)(2,1)S(1)}, bf16[512,128]{1,0:T(8,128)(2,1)S(1)}, u32[]{:S(2)}, u32[]{:S(2)}) collective-permute-start(bf16[512,128]{1,0:T(8,128)(2,1)S(1)} %get-tuple-element.29), channel_id=1, source_target_pairs={{0,3},{1,2},{2,1},{3,0},{4,7},{5,6},{6,5},{7,4},{8,11},{9,10},{10,... | collective-permute-start | bytes 393224 | tf_op jit(solution)/shard_map/ppermute | solution.py:306
  14.8 1.9 %shard_map.76 = (bf16[512,512]{1,0:T(8,128)(2,1)S(1)}, bf16[512,512]{1,0:T(8,128)(2,1)S(1)}, bf16[512,512]{1,0:T(8,128)(2,1)S(1)}, bf16[512,512]{1,0:T(8,128)(2,1)S(1)}) custom-call(f32[8,128]{1,0:T(8,128)S(1)} %get-tuple-element.22.refs_0_.own_points, f32[8,128]{1,0:T(8,128)S(1)} %collective-permute-done.refs_1_.far_points, ...), custom_call_target="tpu_custom_call" | custom-call | flops 15728640 | tf_op jit(solution)/shard_map/pallas_call | solution.py:377
  16.7 2.1 %collective-permute-done.5.theirs = bf16[512,128]{1,0:T(8,128)(2,1)S(1)} collective-permute-done((bf16[512,128]{1,0:T(8,128)(2,1)S(1)}, bf16[512,128]{1,0:T(8,128)(2,1)S(1)}, u32[]{:S(2)}, u32[]{:S(2)}) %collective-permute-start.5) | collective-permute-done | bytes 131104 | tf_op jit(solution)/shard_map/ppermute | solution.py:306
  18.8 0.5 %shard_map.77 = (bf16[512,128]{1,0:T(8,128)(2,1)S(1)}, bf16[512,128]{1,0:T(8,128)(2,1)S(1)}) custom-call(f32[512,128]{1,0:T(8,128)S(1)} %get-tuple-element.28.mine, bf16[512,128]{1,0:T(8,128)(2,1)S(1)} %collective-permute-done.5.theirs, bf16[512,512]{1,0:T(8,128)(2,1)S(1)} %get-tuple-element.30.kernel_re, bf16[512,512]{1,0:T(8,128)(2,1)S(1)} %get-tuple-element.31.kernel_im), custom_call_target="tpu_custom_call" | custom-call | tf_op jit(solution)/shard_map/pallas_call | solution.py:383
  19.3 0.5 %collective-permute-start.6 = (bf16[512,128]{1,0:T(8,128)(2,1)S(1)}, bf16[512,128]{1,0:T(8,128)(2,1)S(1)}, u32[]{:S(2)}, u32[]{:S(2)}) collective-permute-start(bf16[512,128]{1,0:T(8,128)(2,1)S(1)} %get-tuple-element.35), channel_id=1, source_target_pairs={{0,1},{1,0},{2,3},{3,2},{4,5},{5,4},{6,7},{7,6},{8,9},{9,8},{10,11... | collective-permute-start | bytes 393224 | tf_op jit(solution)/shard_map/ppermute | solution.py:306
  19.8 0.5 %shard_map.78.mine = f32[512,128]{1,0:T(8,128)S(1)} custom-call(bf16[512,128]{1,0:T(8,128)(2,1)S(1)} %get-tuple-element.32.currents, bf16[512,512]{1,0:T(8,128)(2,1)S(1)} %get-tuple-element.33.kernel_re, bf16[512,512]{1,0:T(8,128)(2,1)S(1)} %get-tuple-element.34.kernel_im), custom_call_target="tpu_custom_call" | custom-call | tf_op jit(solution)/shard_map/pallas_call | solution.py:387
  20.3 0.5 %collective-permute-done.6.theirs = bf16[512,128]{1,0:T(8,128)(2,1)S(1)} collective-permute-done((bf16[512,128]{1,0:T(8,128)(2,1)S(1)}, bf16[512,128]{1,0:T(8,128)(2,1)S(1)}, u32[]{:S(2)}, u32[]{:S(2)}) %collective-permute-start.6) | collective-permute-done | bytes 131104 | tf_op jit(solution)/shard_map/ppermute | solution.py:306
  20.8 2.7 %collective-permute-start.8 = (bf16[256,128]{1,0:T(8,128)(2,1)S(1)}, bf16[256,128]{1,0:T(8,128)(2,1)S(1)}, u32[]{:S(2)}, u32[]{:S(2)}) collective-permute-start(bf16[256,128]{1,0:T(8,128)(2,1)S(1)} %get-tuple-element.38), channel_id=1, source_target_pairs={{4,0},{6,2},{0,4},{2,6},{12,8},{14,10},{8,12},{10,14},{13,1},{15,3... | collective-permute-start | bytes 196616 | tf_op jit(solution)/shard_map/ppermute | solution.py:306
  23.5 0.8 %collective-permute-start.7 = (bf16[128,128]{1,0:T(8,128)(2,1)S(1)}, bf16[128,128]{1,0:T(8,128)(2,1)S(1)}, u32[]{:S(2)}, u32[]{:S(2)}) collective-permute-start(bf16[128,128]{1,0:T(8,128)(2,1)S(1)} %get-tuple-element.37), channel_id=1, source_target_pairs={{9,0},{8,1},{11,2},{10,3},{13,4},{12,5},{15,6},{14,7},{1,8},{0,9},... | collective-permute-start | bytes 98312 | tf_op jit(solution)/shard_map/ppermute | solution.py:306
  24.3 1.8 %collective-permute-done.8.refs_1_ = bf16[256,128]{1,0:T(8,128)(2,1)S(1)} collective-permute-done((bf16[256,128]{1,0:T(8,128)(2,1)S(1)}, bf16[256,128]{1,0:T(8,128)(2,1)S(1)}, u32[]{:S(2)}, u32[]{:S(2)}) %collective-permute-start.8) | collective-permute-done | bytes 65568 | tf_op jit(solution)/shard_map/ppermute | solution.py:306
  26.2 0.0 collective-permute-start.9
  26.2 1.6 %collective-permute-done.7.refs_0_ = bf16[128,128]{1,0:T(8,128)(2,1)S(1)} collective-permute-done((bf16[128,128]{1,0:T(8,128)(2,1)S(1)}, bf16[128,128]{1,0:T(8,128)(2,1)S(1)}, u32[]{:S(2)}, u32[]{:S(2)}) %collective-permute-start.7) | collective-permute-done | bytes 32800 | tf_op jit(solution)/shard_map/ppermute | solution.py:306
  27.8 0.0 collective-permute-done.9.refs_2_
  27.8 0.6 %shard_map.80 = f32[128,128]{1,0:T(8,128)} custom-call(f32[128,128]{1,0:T(8,128)S(1)} %get-tuple-element.36.kept, bf16[128,128]{1,0:T(8,128)(2,1)S(1)} %collective-permute-done.7.refs_0_, bf16[256,128]{1,0:T(8,128)(2,1)S(1)} %collective-permute-done.8.refs_1_, bf16[128,128]{1,0:T(8,128)(2,1)S(1)} %collective-permute-done.9.refs_2_), custom_call_target="tpu_custom_call" | custom-call | tf_op jit(solution)/shard_map/pallas_call | solution.py:404
  (8 shorter events, 0.1 us)
Async XLA Ops:
  0.9 8.2 %collective-permute-start.3 = (bf16[144,128]{1,0:T(8,128)(2,1)S(1)}, bf16[144,128]{1,0:T(8,128)(2,1)S(1)}, u32[]{:S(2)}, u32[]{:S(2)}) collective-permute-start(bf16[144,128]{1,0:T(8,128)(2,1)S(1)} %get-tuple-element.23), channel_id=1, source_target_pairs={{0,13},{1,12},{2,15},{3,14},{4,9},{5,8},{6,11},{7,10},{8,5},{9,4},... | collective-permute-start | bytes 110600 | tf_op jit(solution)/shard_map/ppermute | solution.py:306
  5.6 4.3 %collective-permute-start.2 = (bf16[144,128]{1,0:T(8,128)(2,1)S(1)}, bf16[144,128]{1,0:T(8,128)(2,1)S(1)}, u32[]{:S(2)}, u32[]{:S(2)}) collective-permute-start(bf16[144,128]{1,0:T(8,128)(2,1)S(1)} %get-tuple-element.23), channel_id=1, source_target_pairs={{0,9},{1,8},{2,11},{3,10},{4,13},{5,12},{6,15},{7,14},{8,1},{9,0},... | collective-permute-start | bytes 110600 | tf_op jit(solution)/shard_map/ppermute | solution.py:306
  5.6 4.3 %collective-permute-start.1 = (bf16[144,128]{1,0:T(8,128)(2,1)S(1)}, bf16[144,128]{1,0:T(8,128)(2,1)S(1)}, u32[]{:S(2)}, u32[]{:S(2)}) collective-permute-start(bf16[144,128]{1,0:T(8,128)(2,1)S(1)} %get-tuple-element.23), channel_id=1, source_target_pairs={{0,5},{1,4},{2,7},{3,6},{4,1},{5,0},{6,3},{7,2},{8,13},{9,12},{10,... | collective-permute-start | bytes 110600 | tf_op jit(solution)/shard_map/ppermute | solution.py:306
  5.7 3.4 %collective-permute-start = (f32[8,128]{1,0:T(8,128)S(1)}, f32[8,128]{1,0:T(8,128)S(1)}, u32[]{:S(2)}, u32[]{:S(2)}) collective-permute-start(f32[8,128]{1,0:T(8,128)S(1)} %get-tuple-element.22.refs_0_.own_points), channel_id=1, source_target_pairs={{0,3},{1,2},{2,1},{3,0},{4,7},{5,6},{6,5},{7,4},{8,11},{9,10},{10,... | collective-permute-start | bytes 12296 | tf_op jit(solution)/shard_map/ppermute | solution.py:306
  10.0 1.8 %collective-permute-start.4 = (bf16[4,144,128]{2,1,0:T(8,128)(2,1)S(1)}, bf16[4,144,128]{2,1,0:T(8,128)(2,1)S(1)}, u32[]{:S(2)}, u32[]{:S(2)}) collective-permute-start(bf16[4,144,128]{2,1,0:T(8,128)(2,1)S(1)} %pad_maximum_fusion.refs_2_), channel_id=1, source_target_pairs={{0,1},{1,0},{2,3},{3,2},{4,5},{5,4},{6,7},{7,6},{8,9},{9,8},{10,11... | collective-permute-start | bytes 442376 | tf_op jit(solution)/shard_map/ppermute | solution.py:306
  13.2 5.5 %collective-permute-start.5 = (bf16[512,128]{1,0:T(8,128)(2,1)S(1)}, bf16[512,128]{1,0:T(8,128)(2,1)S(1)}, u32[]{:S(2)}, u32[]{:S(2)}) collective-permute-start(bf16[512,128]{1,0:T(8,128)(2,1)S(1)} %get-tuple-element.29), channel_id=1, source_target_pairs={{0,3},{1,2},{2,1},{3,0},{4,7},{5,6},{6,5},{7,4},{8,11},{9,10},{10,... | collective-permute-start | bytes 393224 | tf_op jit(solution)/shard_map/ppermute | solution.py:306
  19.3 1.4 %collective-permute-start.6 = (bf16[512,128]{1,0:T(8,128)(2,1)S(1)}, bf16[512,128]{1,0:T(8,128)(2,1)S(1)}, u32[]{:S(2)}, u32[]{:S(2)}) collective-permute-start(bf16[512,128]{1,0:T(8,128)(2,1)S(1)} %get-tuple-element.35), channel_id=1, source_target_pairs={{0,1},{1,0},{2,3},{3,2},{4,5},{5,4},{6,7},{7,6},{8,9},{9,8},{10,11... | collective-permute-start | bytes 393224 | tf_op jit(solution)/shard_map/ppermute | solution.py:306
  20.8 5.4 %collective-permute-start.8 = (bf16[256,128]{1,0:T(8,128)(2,1)S(1)}, bf16[256,128]{1,0:T(8,128)(2,1)S(1)}, u32[]{:S(2)}, u32[]{:S(2)}) collective-permute-start(bf16[256,128]{1,0:T(8,128)(2,1)S(1)} %get-tuple-element.38), channel_id=1, source_target_pairs={{4,0},{6,2},{0,4},{2,6},{12,8},{14,10},{8,12},{10,14},{13,1},{15,3... | collective-permute-start | bytes 196616 | tf_op jit(solution)/shard_map/ppermute | solution.py:306
  23.5 4.2 %collective-permute-start.7 = (bf16[128,128]{1,0:T(8,128)(2,1)S(1)}, bf16[128,128]{1,0:T(8,128)(2,1)S(1)}, u32[]{:S(2)}, u32[]{:S(2)}) collective-permute-start(bf16[128,128]{1,0:T(8,128)(2,1)S(1)} %get-tuple-element.37), channel_id=1, source_target_pairs={{9,0},{8,1},{11,2},{10,3},{13,4},{12,5},{15,6},{14,7},{1,8},{0,9},... | collective-permute-start | bytes 98312 | tf_op jit(solution)/shard_map/ppermute | solution.py:306
  26.2 1.6 %collective-permute-start.9 = (bf16[128,128]{1,0:T(8,128)(2,1)S(1)}, bf16[128,128]{1,0:T(8,128)(2,1)S(1)}, u32[]{:S(2)}, u32[]{:S(2)}) collective-permute-start(bf16[128,128]{1,0:T(8,128)(2,1)S(1)} %slice.44), channel_id=1, source_target_pairs={{0,1},{1,0},{2,3},{3,2},{4,5},{5,4},{6,7},{7,6},{8,9},{9,8},{10,11... | collective-permute-start | bytes 98312 | tf_op jit(solution)/shard_map/ppermute | solution.py:306

commit v7 on v6

--- a/solution.py
+++ b/solution.py
@@ -126,13 +126,16 @@
 
 def green_body(point_sets, bases, scale, *refs):
     points, messages, refs = refs[:point_sets], refs[point_sets], refs[point_sets + 1 :]
-    base, outs = refs[:bases], refs[bases:-12]
-    columns, left, heights, right, weights, weights_turned, *slots = refs[-12:]
+    if bases:
+        base, (columns, left), outs = refs[:bases], refs[bases : bases + 2], refs[bases + 2 : -10]
+    else:
+        base, outs, (columns, left) = (), refs[:-12], refs[-12:-10]
+    heights, right, weights, weights_turned, *slots = refs[-10:]
     slots = (slots[:3], slots[3:])
     count, height, lanes = messages.shape
     sources = height - PACK_ROWS
     total_points = columns.shape[0]
-    for at in range(point_sets):
+    for at in range(0 if bases else point_sets):
         fill_point_columns(points[at], columns, 2 * lanes * at)
         for half in range(2):
             x, y, z = (points[at][k : k + 1, :] for k in point_rows(points[at], half)[:3])
@@ -222,21 +225,25 @@
         lax.fori_loop(0, size // TILE, one, 0, unroll=16)
 
 
-def radiate(kernel_re, kernel_im, held):
-    return jnp.dot(kernel_re[...], held, preferred_element_type=F32) + jnp.dot(
-        kernel_im[...], turned(held), preferred_element_type=F32
+def radiate(kernel_re, kernel_im, held, held_turned):
+    return jnp.dot(kernel_re[...], held[...], preferred_element_type=F32) + jnp.dot(
+        kernel_im[...], held_turned[...], preferred_element_type=F32
     )
 
 
-def side_body(mine, theirs, kernel_re, kernel_im, currents, out):
-    half = mine.shape[0] // 2
+def side_body(mine, theirs, kernel_re, kernel_im, held, held_turned, out):
+    half, lanes = mine.shape[0] // 2, mine.shape[1]
+    is_real = lax.broadcasted_iota(jnp.int32, (half, lanes), 1) < lanes // 2
     for here, there in ((slice(0, half), slice(half, None)), (slice(half, None), slice(0, half))):
-        currents[here, :] = (mine[here, :] + theirs[there, :].astype(F32)).astype(BF16)
-    out[...] = radiate(kernel_re, kernel_im, currents[...]).astype(out.dtype)
-
-
-def near_body(currents, kernel_re, kernel_im, out):
-    out[...] = radiate(kernel_re, kernel_im, currents[...])
+        total = mine[here, :] + theirs[there, :].astype(F32)
+        moved = pltpu.roll(total, lanes // 2, 1)
+        held[here, :] = total.astype(BF16)
+        held_turned[here, :] = jnp.where(is_real, -moved, moved).astype(BF16)
+    out[...] = radiate(kernel_re, kernel_im, held, held_turned).astype(out.dtype)
+
+
+def near_body(held, held_turned, kernel_re, kernel_im, out):
+    out[...] = radiate(kernel_re, kernel_im, held, held_turned)
 
 
 def fold_body(mine, theirs, *outs):
@@ -338,9 +345,8 @@
     def green(points, messages, bases, types):
         rows = len(points) * local_points
         slot = [((chunk, part), BF16), ((chunk, part), BF16), ((chunk, part), F32)]
+        tables = [] if bases else [((rows, 4), F32), ((rows, TERMS), BF16)]
         scratch = [
-            ((rows, 4), F32),
-            ((rows, TERMS), BF16),
             ((8, part), F32),
             ((TERMS, part), BF16),
             ((part, lanes), BF16),
@@ -350,15 +356,15 @@
         ]
         scratch = [pltpu.VMEM(*which) for which in scratch]
         return call(
-            functools.partial(green_body, len(points), len(bases), scale),
-            [((rows, lanes), kind) for kind in types],
+            functools.partial(green_body, len(points), len(bases[:1]), scale),
+            [((rows, lanes), kind) for kind in types] + tables,
             scratch,
             0,
         )(*points, messages, *bases)
 
     sets = [points, far_points]
-    bases = green(sets, near_messages, [], [F32])
-    mine, told = green(sets, side_messages, bases, [F32, BF16])
+    first, *tables = green(sets, near_messages, [], [F32])
+    mine, told = green(sets, side_messages, [first, *tables], [F32, BF16])
     theirs = swap(told, 3)
 
     even = lax.rem(lax.axis_index("refl"), 2) == 0
@@ -380,11 +386,11 @@
         [pltpu.VMEM((2 * count, 8), F32), pltpu.VMEM((8, half_points), F32)],
         60 * count * half_points,
     )(points, far_points, jnp.stack(keep), jnp.stack(give))
-    currents, told = call(side_body, [((half_points, lanes), BF16), ((count, lanes), BF16)])(
-        mine, theirs, side_re, side_im
-    )
+    *currents, told = call(
+        side_body, [((half_points, lanes), BF16)] * 2 + [((count, lanes), BF16)]
+    )(mine, theirs, side_re, side_im)
     given = swap(told, 1)
-    near = call(near_body, [((count, lanes), F32)])(currents, near_re, near_im)[0]
+    near = call(near_body, [((count, lanes), F32)])(*currents, near_re, near_im)[0]
     block, double = (directions, lanes), (2 * directions, lanes)
     kept, *sent = call(
         fold_body,

time: 28.6 us -> 28.4 us (level)
  no operation moved by 1% of the time
where the time goes in v7:
time: 28.4 us; the launch traced here: 28.3 us
  starting transfers between devices  12.4 us (44%)
  waiting for transfers between devices  8.42 us (30%)
  Pallas kernels  7.29 us (26%)
    ppermute x10, starting transfers between devices, swap(): lax.ppermute(x, 'refl', [(b, a) for a, b in links] if back else links)  12.4 us
    ppermute x10, waiting for transfers between devices, swap(): lax.ppermute(x, 'refl', [(b, a) for a, b in links] if back else links)  8.42 us
    pallas_call x2, Pallas kernels, green(): call(functools.partial(green_body, len(points), len(bases[:1]), scale), [...  2.87 us
    pallas_call x1, Pallas kernels, per_device(): call(kernel_body, [((count, half_points), BF16)] * 4, [pltpu.VMEM((2 * co...  1.93 us
    pallas_call x1, Pallas kernels, per_device(): call(pack_body, [((sources + PACK_ROWS, lanes), BF16), ((8, lanes), F32)]...  0.85 us
    pallas_call x1, Pallas kernels, per_device(): return call(finish_body, [((directions, lanes), F32)])(kept, *arrived)[0]  0.65 us
  transfers between devices with their start and end apart: 10, of which 6 were waited for; matrix products, arithmetic and copies ran while one was open for 0% of the time, Pallas kernels for 14%

profile of v7, /device:TPU:1, one launch (start us, length us, event | category | flops | bytes accessed | tf_op | source)
XLA Modules:
  0.0 28.3 jit_solution(4538997719933854523)
XLA Ops:
  0.0 0.9 %shard_map.73 = (bf16[144,128]{1,0:T(8,128)(2,1)S(1)}, f32[8,128]{1,0:T(8,128)S(1)}) custom-call(bf16[128,128]{1,0:T(8,128)(2,1)} %weights.1, f32[2,128]{1,0:T(2,128)} %feed_plane.1, f32[1,128]{1,0:T(1,128)} %bitcast.17, f32[2,128]{1,0:T(2,128)} %cosines.1, f32[2,256]{1,0:T(2,128)} %plane.1, f32[2,128]{1,0:T(2,128)} %bitcast.15, f32[2,128]{1,0:T(2,128)} %bitcast.16), custom_call_target="tpu_custom_call" | custom-call | tf_op jit(solution)/shard_map/pallas_call | solution.py:315
  0.9 4.8 %collective-permute-start.3 = (bf16[144,128]{1,0:T(8,128)(2,1)S(1)}, bf16[144,128]{1,0:T(8,128)(2,1)S(1)}, u32[]{:S(2)}, u32[]{:S(2)}) collective-permute-start(bf16[144,128]{1,0:T(8,128)(2,1)S(1)} %get-tuple-element.27), channel_id=1, source_target_pairs={{0,13},{1,12},{2,15},{3,14},{4,9},{5,8},{6,11},{7,10},{8,5},{9,4},... | collective-permute-start | bytes 110600 | tf_op jit(solution)/shard_map/ppermute | solution.py:313
  5.6 0.0 collective-permute-start.2
  5.6 0.1 collective-permute-start.1
  5.7 1.8 %collective-permute-start = (f32[8,128]{1,0:T(8,128)S(1)}, f32[8,128]{1,0:T(8,128)S(1)}, u32[]{:S(2)}, u32[]{:S(2)}) collective-permute-start(f32[8,128]{1,0:T(8,128)S(1)} %get-tuple-element.26.refs_0_.own_points), channel_id=1, source_target_pairs={{0,3},{1,2},{2,1},{3,0},{4,7},{5,6},{6,5},{7,4},{8,11},{9,10},{10,... | collective-permute-start | bytes 12296 | tf_op jit(solution)/shard_map/ppermute | solution.py:313
  7.5 1.6 %collective-permute-done.refs_1_.far_points = f32[8,128]{1,0:T(8,128)S(1)} collective-permute-done((f32[8,128]{1,0:T(8,128)S(1)}, f32[8,128]{1,0:T(8,128)S(1)}, u32[]{:S(2)}, u32[]{:S(2)}) %collective-permute-start) | collective-permute-done | bytes 4128 | tf_op jit(solution)/shard_map/ppermute | solution.py:313
  9.1 0.0 collective-permute-done.3
  9.1 0.8 %collective-permute-done.2 = bf16[144,128]{1,0:T(8,128)(2,1)S(1)} collective-permute-done((bf16[144,128]{1,0:T(8,128)(2,1)S(1)}, bf16[144,128]{1,0:T(8,128)(2,1)S(1)}, u32[]{:S(2)}, u32[]{:S(2)}) %collective-permute-start.2) | collective-permute-done | bytes 36896 | tf_op jit(solution)/shard_map/ppermute | solution.py:313
  9.9 0.0 collective-permute-done.1
  10.0 0.2 collective-permute-start.4
  10.2 1.5 %shard_map.74 = (f32[512,128]{1,0:T(8,128)S(1)}, f32[512,4]{1,0:T(8,128)S(1)}, bf16[512,32]{1,0:T(8,128)(2,1)S(1)}) custom-call(f32[8,128]{1,0:T(8,128)S(1)} %get-tuple-element.26.refs_0_.own_points, f32[8,128]{1,0:T(8,128)S(1)} %collective-permute-done.refs_1_.far_points, bf16[4,144,128]{2,1,0:T(8,128)(2,1)S(1)} %pad_maximum_fusion.refs_2_), custom_call_target="tpu_custom_call" | custom-call | tf_op jit(solution)/shard_map/pallas_call | solution.py:358
  11.7 0.0 collective-permute-done.4.refs_2_
  11.7 1.4 %shard_map.75 = (f32[512,128]{1,0:T(8,128)S(1)}, bf16[512,128]{1,0:T(8,128)(2,1)S(1)}) custom-call(f32[8,128]{1,0:T(8,128)S(1)} %get-tuple-element.26.refs_0_.own_points, f32[8,128]{1,0:T(8,128)S(1)} %collective-permute-done.refs_1_.far_points, bf16[4,144,128]{2,1,0:T(8,128)(2,1)S(1)} %collective-permute-done.4.refs_2_, ...), custom_call_target="tpu_custom_call" | custom-call | tf_op jit(solution)/shard_map/pallas_call | solution.py:358
  13.1 1.5 %collective-permute-start.5 = (bf16[512,128]{1,0:T(8,128)(2,1)S(1)}, bf16[512,128]{1,0:T(8,128)(2,1)S(1)}, u32[]{:S(2)}, u32[]{:S(2)}) collective-permute-start(bf16[512,128]{1,0:T(8,128)(2,1)S(1)} %get-tuple-element.36), channel_id=1, source_target_pairs={{0,3},{1,2},{2,1},{3,0},{4,7},{5,6},{6,5},{7,4},{8,11},{9,10},{10,... | collective-permute-start | bytes 393224 | tf_op jit(solution)/shard_map/ppermute | solution.py:313
  14.7 1.9 %shard_map.76 = (bf16[512,512]{1,0:T(8,128)(2,1)S(1)}, bf16[512,512]{1,0:T(8,128)(2,1)S(1)}, bf16[512,512]{1,0:T(8,128)(2,1)S(1)}, bf16[512,512]{1,0:T(8,128)(2,1)S(1)}) custom-call(f32[8,128]{1,0:T(8,128)S(1)} %get-tuple-element.26.refs_0_.own_points, f32[8,128]{1,0:T(8,128)S(1)} %collective-permute-done.refs_1_.far_points, ...), custom_call_target="tpu_custom_call" | custom-call | flops 15728640 | tf_op jit(solution)/shard_map/pallas_call | solution.py:383
  16.6 2.1 %collective-permute-done.5.theirs = bf16[512,128]{1,0:T(8,128)(2,1)S(1)} collective-permute-done((bf16[512,128]{1,0:T(8,128)(2,1)S(1)}, bf16[512,128]{1,0:T(8,128)(2,1)S(1)}, u32[]{:S(2)}, u32[]{:S(2)}) %collective-permute-start.5) | collective-permute-done | bytes 131104 | tf_op jit(solution)/shard_map/ppermute | solution.py:313
  18.6 0.5 %shard_map.77 = (bf16[512,128]{1,0:T(8,128)(2,1)S(1)}, bf16[512,128]{1,0:T(8,128)(2,1)S(1)}, bf16[512,128]{1,0:T(8,128)(2,1)S(1)}) custom-call(f32[512,128]{1,0:T(8,128)S(1)} %get-tuple-element.35.mine, bf16[512,128]{1,0:T(8,128)(2,1)S(1)} %collective-permute-done.5.theirs, bf16[512,512]{1,0:T(8,128)(2,1)S(1)} %get-tuple-element.37.kernel_re, ...), custom_call_target="tpu_custom_call" | custom-call | tf_op jit(solution)/shard_map/pallas_call | solution.py:389
  19.2 0.5 %collective-permute-start.6 = (bf16[512,128]{1,0:T(8,128)(2,1)S(1)}, bf16[512,128]{1,0:T(8,128)(2,1)S(1)}, u32[]{:S(2)}, u32[]{:S(2)}) collective-permute-start(bf16[512,128]{1,0:T(8,128)(2,1)S(1)} %get-tuple-element.43), channel_id=1, source_target_pairs={{0,1},{1,0},{2,3},{3,2},{4,5},{5,4},{6,7},{7,6},{8,9},{9,8},{10,11... | collective-permute-start | bytes 393224 | tf_op jit(solution)/shard_map/ppermute | solution.py:313
  19.6 0.4 %shard_map.78.mine = f32[512,128]{1,0:T(8,128)S(1)} custom-call(bf16[512,128]{1,0:T(8,128)(2,1)S(1)} %get-tuple-element.39.held, bf16[512,128]{1,0:T(8,128)(2,1)S(1)} %get-tuple-element.40.held_turned, bf16[512,512]{1,0:T(8,128)(2,1)S(1)} %get-tuple-element.41.kernel_re, bf16[512,512]{1,0:T(8,128)(2,1)S(1)} %get-tuple-element.42.kernel_im), custom_call_target="tpu_custom_call" | custom-call | tf_op jit(solution)/shard_map/pallas_call | solution.py:393
  20.1 0.5 %collective-permute-done.6.theirs = bf16[512,128]{1,0:T(8,128)(2,1)S(1)} collective-permute-done((bf16[512,128]{1,0:T(8,128)(2,1)S(1)}, bf16[512,128]{1,0:T(8,128)(2,1)S(1)}, u32[]{:S(2)}, u32[]{:S(2)}) %collective-permute-start.6) | collective-permute-done | bytes 131104 | tf_op jit(solution)/shard_map/ppermute | solution.py:313
  20.7 2.7 %collective-permute-start.8 = (bf16[256,128]{1,0:T(8,128)(2,1)S(1)}, bf16[256,128]{1,0:T(8,128)(2,1)S(1)}, u32[]{:S(2)}, u32[]{:S(2)}) collective-permute-start(bf16[256,128]{1,0:T(8,128)(2,1)S(1)} %get-tuple-element.46), channel_id=1, source_target_pairs={{4,0},{6,2},{0,4},{2,6},{12,8},{14,10},{8,12},{10,14},{13,1},{15,3... | collective-permute-start | bytes 196616 | tf_op jit(solution)/shard_map/ppermute | solution.py:313
  23.4 0.8 %collective-permute-start.7 = (bf16[128,128]{1,0:T(8,128)(2,1)S(1)}, bf16[128,128]{1,0:T(8,128)(2,1)S(1)}, u32[]{:S(2)}, u32[]{:S(2)}) collective-permute-start(bf16[128,128]{1,0:T(8,128)(2,1)S(1)} %get-tuple-element.45), channel_id=1, source_target_pairs={{9,0},{8,1},{11,2},{10,3},{13,4},{12,5},{15,6},{14,7},{1,8},{0,9},... | collective-permute-start | bytes 98312 | tf_op jit(solution)/shard_map/ppermute | solution.py:313
  24.2 1.8 %collective-permute-done.8.refs_1_ = bf16[256,128]{1,0:T(8,128)(2,1)S(1)} collective-permute-done((bf16[256,128]{1,0:T(8,128)(2,1)S(1)}, bf16[256,128]{1,0:T(8,128)(2,1)S(1)}, u32[]{:S(2)}, u32[]{:S(2)}) %collective-permute-start.8) | collective-permute-done | bytes 65568 | tf_op jit(solution)/shard_map/ppermute | solution.py:313
  26.0 0.0 collective-permute-start.9
  26.0 1.6 %collective-permute-done.7.refs_0_ = bf16[128,128]{1,0:T(8,128)(2,1)S(1)} collective-permute-done((bf16[128,128]{1,0:T(8,128)(2,1)S(1)}, bf16[128,128]{1,0:T(8,128)(2,1)S(1)}, u32[]{:S(2)}, u32[]{:S(2)}) %collective-permute-start.7) | collective-permute-done | bytes 32800 | tf_op jit(solution)/shard_map/ppermute | solution.py:313
  27.6 0.0 collective-permute-done.9.refs_2_
  27.6 0.6 %shard_map.80 = f32[128,128]{1,0:T(8,128)} custom-call(f32[128,128]{1,0:T(8,128)S(1)} %get-tuple-element.44.kept, bf16[128,128]{1,0:T(8,128)(2,1)S(1)} %collective-permute-done.7.refs_0_, bf16[256,128]{1,0:T(8,128)(2,1)S(1)} %collective-permute-done.8.refs_1_, bf16[128,128]{1,0:T(8,128)(2,1)S(1)} %collective-permute-done.9.refs_2_), custom_call_target="tpu_custom_call" | custom-call | tf_op jit(solution)/shard_map/pallas_call | solution.py:410
  (8 shorter events, 0.1 us)
Async XLA Ops:
  0.9 8.2 %collective-permute-start.3 = (bf16[144,128]{1,0:T(8,128)(2,1)S(1)}, bf16[144,128]{1,0:T(8,128)(2,1)S(1)}, u32[]{:S(2)}, u32[]{:S(2)}) collective-permute-start(bf16[144,128]{1,0:T(8,128)(2,1)S(1)} %get-tuple-element.27), channel_id=1, source_target_pairs={{0,13},{1,12},{2,15},{3,14},{4,9},{5,8},{6,11},{7,10},{8,5},{9,4},... | collective-permute-start | bytes 110600 | tf_op jit(solution)/shard_map/ppermute | solution.py:313
  5.6 4.3 %collective-permute-start.2 = (bf16[144,128]{1,0:T(8,128)(2,1)S(1)}, bf16[144,128]{1,0:T(8,128)(2,1)S(1)}, u32[]{:S(2)}, u32[]{:S(2)}) collective-permute-start(bf16[144,128]{1,0:T(8,128)(2,1)S(1)} %get-tuple-element.27), channel_id=1, source_target_pairs={{0,9},{1,8},{2,11},{3,10},{4,13},{5,12},{6,15},{7,14},{8,1},{9,0},... | collective-permute-start | bytes 110600 | tf_op jit(solution)/shard_map/ppermute | solution.py:313
  5.6 4.3 %collective-permute-start.1 = (bf16[144,128]{1,0:T(8,128)(2,1)S(1)}, bf16[144,128]{1,0:T(8,128)(2,1)S(1)}, u32[]{:S(2)}, u32[]{:S(2)}) collective-permute-start(bf16[144,128]{1,0:T(8,128)(2,1)S(1)} %get-tuple-element.27), channel_id=1, source_target_pairs={{0,5},{1,4},{2,7},{3,6},{4,1},{5,0},{6,3},{7,2},{8,13},{9,12},{10,... | collective-permute-start | bytes 110600 | tf_op jit(solution)/shard_map/ppermute | solution.py:313
  5.7 3.4 %collective-permute-start = (f32[8,128]{1,0:T(8,128)S(1)}, f32[8,128]{1,0:T(8,128)S(1)}, u32[]{:S(2)}, u32[]{:S(2)}) collective-permute-start(f32[8,128]{1,0:T(8,128)S(1)} %get-tuple-element.26.refs_0_.own_points), channel_id=1, source_target_pairs={{0,3},{1,2},{2,1},{3,0},{4,7},{5,6},{6,5},{7,4},{8,11},{9,10},{10,... | collective-permute-start | bytes 12296 | tf_op jit(solution)/shard_map/ppermute | solution.py:313
  10.0 1.8 %collective-permute-start.4 = (bf16[4,144,128]{2,1,0:T(8,128)(2,1)S(1)}, bf16[4,144,128]{2,1,0:T(8,128)(2,1)S(1)}, u32[]{:S(2)}, u32[]{:S(2)}) collective-permute-start(bf16[4,144,128]{2,1,0:T(8,128)(2,1)S(1)} %pad_maximum_fusion.refs_2_), channel_id=1, source_target_pairs={{0,1},{1,0},{2,3},{3,2},{4,5},{5,4},{6,7},{7,6},{8,9},{9,8},{10,11... | collective-permute-start | bytes 442376 | tf_op jit(solution)/shard_map/ppermute | solution.py:313
  13.1 5.5 %collective-permute-start.5 = (bf16[512,128]{1,0:T(8,128)(2,1)S(1)}, bf16[512,128]{1,0:T(8,128)(2,1)S(1)}, u32[]{:S(2)}, u32[]{:S(2)}) collective-permute-start(bf16[512,128]{1,0:T(8,128)(2,1)S(1)} %get-tuple-element.36), channel_id=1, source_target_pairs={{0,3},{1,2},{2,1},{3,0},{4,7},{5,6},{6,5},{7,4},{8,11},{9,10},{10,... | collective-permute-start | bytes 393224 | tf_op jit(solution)/shard_map/ppermute | solution.py:313
  19.2 1.4 %collective-permute-start.6 = (bf16[512,128]{1,0:T(8,128)(2,1)S(1)}, bf16[512,128]{1,0:T(8,128)(2,1)S(1)}, u32[]{:S(2)}, u32[]{:S(2)}) collective-permute-start(bf16[512,128]{1,0:T(8,128)(2,1)S(1)} %get-tuple-element.43), channel_id=1, source_target_pairs={{0,1},{1,0},{2,3},{3,2},{4,5},{5,4},{6,7},{7,6},{8,9},{9,8},{10,11... | collective-permute-start | bytes 393224 | tf_op jit(solution)/shard_map/ppermute | solution.py:313
  20.7 5.4 %collective-permute-start.8 = (bf16[256,128]{1,0:T(8,128)(2,1)S(1)}, bf16[256,128]{1,0:T(8,128)(2,1)S(1)}, u32[]{:S(2)}, u32[]{:S(2)}) collective-permute-start(bf16[256,128]{1,0:T(8,128)(2,1)S(1)} %get-tuple-element.46), channel_id=1, source_target_pairs={{4,0},{6,2},{0,4},{2,6},{12,8},{14,10},{8,12},{10,14},{13,1},{15,3... | collective-permute-start | bytes 196616 | tf_op jit(solution)/shard_map/ppermute | solution.py:313
  23.4 4.2 %collective-permute-start.7 = (bf16[128,128]{1,0:T(8,128)(2,1)S(1)}, bf16[128,128]{1,0:T(8,128)(2,1)S(1)}, u32[]{:S(2)}, u32[]{:S(2)}) collective-permute-start(bf16[128,128]{1,0:T(8,128)(2,1)S(1)} %get-tuple-element.45), channel_id=1, source_target_pairs={{9,0},{8,1},{11,2},{10,3},{13,4},{12,5},{15,6},{14,7},{1,8},{0,9},... | collective-permute-start | bytes 98312 | tf_op jit(solution)/shard_map/ppermute | solution.py:313
  26.0 1.6 %collective-permute-start.9 = (bf16[128,128]{1,0:T(8,128)(2,1)S(1)}, bf16[128,128]{1,0:T(8,128)(2,1)S(1)}, u32[]{:S(2)}, u32[]{:S(2)}) collective-permute-start(bf16[128,128]{1,0:T(8,128)(2,1)S(1)} %slice.44), channel_id=1, source_target_pairs={{0,1},{1,0},{2,3},{3,2},{4,5},{5,4},{6,7},{7,6},{8,9},{9,8},{10,11... | collective-permute-start | bytes 98312 | tf_op jit(solution)/shard_map/ppermute | solution.py:313

commit v8 on v7

--- a/solution.py
+++ b/solution.py
@@ -231,7 +231,7 @@
     )
 
 
-def side_body(mine, theirs, kernel_re, kernel_im, held, held_turned, out):
+def side_body(mine, theirs, kernel_re, kernel_im, held, held_turned, *outs):
     half, lanes = mine.shape[0] // 2, mine.shape[1]
     is_real = lax.broadcasted_iota(jnp.int32, (half, lanes), 1) < lanes // 2
     for here, there in ((slice(0, half), slice(half, None)), (slice(half, None), slice(0, half))):
@@ -239,19 +239,22 @@
         moved = pltpu.roll(total, lanes // 2, 1)
         held[here, :] = total.astype(BF16)
         held_turned[here, :] = jnp.where(is_real, -moved, moved).astype(BF16)
-    out[...] = radiate(kernel_re, kernel_im, held, held_turned).astype(out.dtype)
-
-
-def near_body(held, held_turned, kernel_re, kernel_im, out):
-    out[...] = radiate(kernel_re, kernel_im, held, held_turned)
-
-
-def fold_body(mine, theirs, *outs):
-    total = mine[...] + theirs[...].astype(F32)
-    start = 0
+    total, start = radiate(kernel_re, kernel_im, held, held_turned), 0
     for out in outs:
         out[...] = total[start : start + out.shape[0]].astype(out.dtype)
         start += out.shape[0]
+
+
+def near_body(held, held_turned, kernel_re, kernel_im, out):
+    out[...] = radiate(kernel_re, kernel_im, held, held_turned)
+
+
+def fold_body(start, mine, theirs, *outs):
+    rows = theirs.shape[0]
+    total, at = mine[start : start + rows, :] + theirs[...].astype(F32), 0
+    for out in outs:
+        out[...] = total[at : at + out.shape[0]].astype(out.dtype)
+        at += out.shape[0]
 
 
 def pass_body(*refs):
@@ -386,16 +389,21 @@
         [pltpu.VMEM((2 * count, 8), F32), pltpu.VMEM((8, half_points), F32)],
         60 * count * half_points,
     )(points, far_points, jnp.stack(keep), jnp.stack(give))
-    *currents, told = call(
-        side_body, [((half_points, lanes), BF16)] * 2 + [((count, lanes), BF16)]
+    block, double = (directions, lanes), (2 * directions, lanes)
+    parts = [[(block, F32)] + [(block, BF16)] * len(middle), [(double, BF16)] * len(couples)]
+    parts = [part for part in parts if part]
+    lengths = [sum(shape[0] for shape, _ in part) for part in parts]
+    held, held_turned, *told = call(
+        side_body,
+        [((half_points, lanes), BF16)] * 2 + [((rows, lanes), BF16) for rows in lengths],
     )(mine, theirs, side_re, side_im)
-    given = swap(told, 1)
-    near = call(near_body, [((count, lanes), F32)])(*currents, near_re, near_im)[0]
-    block, double = (directions, lanes), (2 * directions, lanes)
-    kept, *sent = call(
-        fold_body,
-        [(block, F32)] + [(block, BF16)] * len(middle) + [(double, BF16)] * len(couples),
-    )(near, given)
+    given = [swap(x, 1) for x in told[::-1]][::-1]
+    near = call(near_body, [((count, lanes), F32)])(held, held_turned, near_re, near_im)[0]
+    folded = [
+        call(functools.partial(fold_body, sum(lengths[:at])), part)(near, given[at])
+        for at, part in enumerate(parts)
+    ]
+    kept, *sent = [x for group in folded for x in group]
     doubles = [
         swap(x, 4 * low, back=True, odd_step=4 * high)
         for x, (low, high) in zip(sent[len(middle) :], couples)

time: 28.4 us -> 28.4 us (level)
    ppermute x10 -> x11, waiting for transfers between devices: 8.42 us -> 8.23 us  [swap(): lax.ppermute(x, 'refl', [(b, a) for a, b in links] if back else links)]
    ppermute x10 -> x11, starting transfers between devices: 12.4 us -> 12.6 us  [swap(): lax.ppermute(x, 'refl', [(b, a) for a, b in links] if back else links)]
    pallas_call x3 -> x4, Pallas kernels: 0.99 us -> 0.99 us  [the longest x1 0.53 us: per_device(): call(side_body, [((half_points, lanes), BF16)] * 2 + [((rows, lanes), BF1...]
  transfers between devices with their start and end apart: 10 -> 11, of which waited for: 6 -> 6; matrix products, arithmetic and copies ran while one was open for 0% -> 0% of each run, Pallas kernels for 14% -> 14%
where the time goes in v8:
time: 28.4 us; the launch traced here: 28.3 us
  starting transfers between devices  12.6 us (44%)
  waiting for transfers between devices  8.23 us (29%)
  Pallas kernels  7.3 us (26%)
    ppermute x11, starting transfers between devices, swap(): lax.ppermute(x, 'refl', [(b, a) for a, b in links] if back else links)  12.6 us
    ppermute x11, waiting for transfers between devices, swap(): lax.ppermute(x, 'refl', [(b, a) for a, b in links] if back else links)  8.23 us
    pallas_call x2, Pallas kernels, green(): call(functools.partial(green_body, len(points), len(bases[:1]), scale), [...  2.87 us
    pallas_call x1, Pallas kernels, per_device(): call(kernel_body, [((count, half_points), BF16)] * 4, [pltpu.VMEM((2 * co...  1.93 us
    pallas_call x1, Pallas kernels, per_device(): call(pack_body, [((sources + PACK_ROWS, lanes), BF16), ((8, lanes), F32)]...  0.85 us
    pallas_call x1, Pallas kernels, per_device(): return call(finish_body, [((directions, lanes), F32)])(kept, *arrived)[0]  0.65 us
  transfers between devices with their start and end apart: 11, of which 6 were waited for; matrix products, arithmetic and copies ran while one was open for 0% of the time, Pallas kernels for 14%

profile of v8, /device:TPU:1, one launch (start us, length us, event | category | flops | bytes accessed | tf_op | source)
XLA Modules:
  0.0 28.3 jit_solution(9416581558395636610)
XLA Ops:
  0.0 0.9 %shard_map.73 = (bf16[144,128]{1,0:T(8,128)(2,1)S(1)}, f32[8,128]{1,0:T(8,128)S(1)}) custom-call(bf16[128,128]{1,0:T(8,128)(2,1)} %weights.1, f32[2,128]{1,0:T(2,128)} %feed_plane.1, f32[1,128]{1,0:T(1,128)} %bitcast.17, f32[2,128]{1,0:T(2,128)} %cosines.1, f32[2,256]{1,0:T(2,128)} %plane.1, f32[2,128]{1,0:T(2,128)} %bitcast.15, f32[2,128]{1,0:T(2,128)} %bitcast.16), custom_call_target="tpu_custom_call" | custom-call | tf_op jit(solution)/shard_map/pallas_call | solution.py:318
  0.9 4.8 %collective-permute-start.3 = (bf16[144,128]{1,0:T(8,128)(2,1)S(1)}, bf16[144,128]{1,0:T(8,128)(2,1)S(1)}, u32[]{:S(2)}, u32[]{:S(2)}) collective-permute-start(bf16[144,128]{1,0:T(8,128)(2,1)S(1)} %get-tuple-element.27), channel_id=1, source_target_pairs={{0,13},{1,12},{2,15},{3,14},{4,9},{5,8},{6,11},{7,10},{8,5},{9,4},... | collective-permute-start | bytes 110600 | tf_op jit(solution)/shard_map/ppermute | solution.py:316
  5.6 0.0 collective-permute-start.2
  5.6 0.1 collective-permute-start.1
  5.7 1.8 %collective-permute-start = (f32[8,128]{1,0:T(8,128)S(1)}, f32[8,128]{1,0:T(8,128)S(1)}, u32[]{:S(2)}, u32[]{:S(2)}) collective-permute-start(f32[8,128]{1,0:T(8,128)S(1)} %get-tuple-element.26.refs_0_.own_points), channel_id=1, source_target_pairs={{0,3},{1,2},{2,1},{3,0},{4,7},{5,6},{6,5},{7,4},{8,11},{9,10},{10,... | collective-permute-start | bytes 12296 | tf_op jit(solution)/shard_map/ppermute | solution.py:316
  7.5 1.6 %collective-permute-done.refs_1_.far_points = f32[8,128]{1,0:T(8,128)S(1)} collective-permute-done((f32[8,128]{1,0:T(8,128)S(1)}, f32[8,128]{1,0:T(8,128)S(1)}, u32[]{:S(2)}, u32[]{:S(2)}) %collective-permute-start) | collective-permute-done | bytes 4128 | tf_op jit(solution)/shard_map/ppermute | solution.py:316
  9.1 0.0 collective-permute-done.3
  9.1 0.8 %collective-permute-done.2 = bf16[144,128]{1,0:T(8,128)(2,1)S(1)} collective-permute-done((bf16[144,128]{1,0:T(8,128)(2,1)S(1)}, bf16[144,128]{1,0:T(8,128)(2,1)S(1)}, u32[]{:S(2)}, u32[]{:S(2)}) %collective-permute-start.2) | collective-permute-done | bytes 36896 | tf_op jit(solution)/shard_map/ppermute | solution.py:316
  9.9 0.0 collective-permute-done.1
  10.0 0.2 collective-permute-start.4
  10.2 1.5 %shard_map.74 = (f32[512,128]{1,0:T(8,128)S(1)}, f32[512,4]{1,0:T(8,128)S(1)}, bf16[512,32]{1,0:T(8,128)(2,1)S(1)}) custom-call(f32[8,128]{1,0:T(8,128)S(1)} %get-tuple-element.26.refs_0_.own_points, f32[8,128]{1,0:T(8,128)S(1)} %collective-permute-done.refs_1_.far_points, bf16[4,144,128]{2,1,0:T(8,128)(2,1)S(1)} %pad_maximum_fusion.refs_2_), custom_call_target="tpu_custom_call" | custom-call | tf_op jit(solution)/shard_map/pallas_call | solution.py:361
  11.7 0.0 collective-permute-done.4.refs_2_
  11.7 1.4 %shard_map.75 = (f32[512,128]{1,0:T(8,128)S(1)}, bf16[512,128]{1,0:T(8,128)(2,1)S(1)}) custom-call(f32[8,128]{1,0:T(8,128)S(1)} %get-tuple-element.26.refs_0_.own_points, f32[8,128]{1,0:T(8,128)S(1)} %collective-permute-done.refs_1_.far_points, bf16[4,144,128]{2,1,0:T(8,128)(2,1)S(1)} %collective-permute-done.4.refs_2_, ...), custom_call_target="tpu_custom_call" | custom-call | tf_op jit(solution)/shard_map/pallas_call | solution.py:361
  13.1 1.5 %collective-permute-start.5 = (bf16[512,128]{1,0:T(8,128)(2,1)S(1)}, bf16[512,128]{1,0:T(8,128)(2,1)S(1)}, u32[]{:S(2)}, u32[]{:S(2)}) collective-permute-start(bf16[512,128]{1,0:T(8,128)(2,1)S(1)} %get-tuple-element.36), channel_id=1, source_target_pairs={{0,3},{1,2},{2,1},{3,0},{4,7},{5,6},{6,5},{7,4},{8,11},{9,10},{10,... | collective-permute-start | bytes 393224 | tf_op jit(solution)/shard_map/ppermute | solution.py:316
  14.7 1.9 %shard_map.76 = (bf16[512,512]{1,0:T(8,128)(2,1)S(1)}, bf16[512,512]{1,0:T(8,128)(2,1)S(1)}, bf16[512,512]{1,0:T(8,128)(2,1)S(1)}, bf16[512,512]{1,0:T(8,128)(2,1)S(1)}) custom-call(f32[8,128]{1,0:T(8,128)S(1)} %get-tuple-element.26.refs_0_.own_points, f32[8,128]{1,0:T(8,128)S(1)} %collective-permute-done.refs_1_.far_points, ...), custom_call_target="tpu_custom_call" | custom-call | flops 15728640 | tf_op jit(solution)/shard_map/pallas_call | solution.py:386
  16.6 2.1 %collective-permute-done.5.theirs = bf16[512,128]{1,0:T(8,128)(2,1)S(1)} collective-permute-done((bf16[512,128]{1,0:T(8,128)(2,1)S(1)}, bf16[512,128]{1,0:T(8,128)(2,1)S(1)}, u32[]{:S(2)}, u32[]{:S(2)}) %collective-permute-start.5) | collective-permute-done | bytes 131104 | tf_op jit(solution)/shard_map/ppermute | solution.py:316
  18.6 0.5 %shard_map.77 = (bf16[512,128]{1,0:T(8,128)(2,1)S(1)}, bf16[512,128]{1,0:T(8,128)(2,1)S(1)}, bf16[256,128]{1,0:T(8,128)(2,1)S(1)}, bf16[256,128]{1,0:T(8,128)(2,1)S(1)}) custom-call(f32[512,128]{1,0:T(8,128)S(1)} %get-tuple-element.35.mine, bf16[512,128]{1,0:T(8,128)(2,1)S(1)} %collective-permute-done.5.theirs, ...), custom_call_target="tpu_custom_call" | custom-call | tf_op jit(solution)/shard_map/pallas_call | solution.py:396
  19.2 0.5 %collective-permute-start.8 = (bf16[256,128]{1,0:T(8,128)(2,1)S(1)}, bf16[256,128]{1,0:T(8,128)(2,1)S(1)}, u32[]{:S(2)}, u32[]{:S(2)}) collective-permute-start(bf16[256,128]{1,0:T(8,128)(2,1)S(1)} %get-tuple-element.46), channel_id=1, source_target_pairs={{0,1},{1,0},{2,3},{3,2},{4,5},{5,4},{6,7},{7,6},{8,9},{9,8},{10,11... | collective-permute-start | bytes 196616 | tf_op jit(solution)/shard_map/ppermute | solution.py:316
  19.6 0.1 collective-permute-start.6
  19.8 0.4 %shard_map.78.mine = f32[512,128]{1,0:T(8,128)S(1)} custom-call(bf16[512,128]{1,0:T(8,128)(2,1)S(1)} %get-tuple-element.39.held, bf16[512,128]{1,0:T(8,128)(2,1)S(1)} %get-tuple-element.40.held_turned, bf16[512,512]{1,0:T(8,128)(2,1)S(1)} %get-tuple-element.41.kernel_re, bf16[512,512]{1,0:T(8,128)(2,1)S(1)} %get-tuple-element.42.kernel_im), custom_call_target="tpu_custom_call" | custom-call | tf_op jit(solution)/shard_map/pallas_call | solution.py:401
  20.2 0.3 %collective-permute-done.8.theirs = bf16[256,128]{1,0:T(8,128)(2,1)S(1)} collective-permute-done((bf16[256,128]{1,0:T(8,128)(2,1)S(1)}, bf16[256,128]{1,0:T(8,128)(2,1)S(1)}, u32[]{:S(2)}, u32[]{:S(2)}) %collective-permute-start.8) | collective-permute-done | bytes 65568 | tf_op jit(solution)/shard_map/ppermute | solution.py:316
  20.6 2.7 %collective-permute-start.9 = (bf16[256,128]{1,0:T(8,128)(2,1)S(1)}, bf16[256,128]{1,0:T(8,128)(2,1)S(1)}, u32[]{:S(2)}, u32[]{:S(2)}) collective-permute-start(bf16[256,128]{1,0:T(8,128)(2,1)S(1)} %shard_map.80), channel_id=1, source_target_pairs={{4,0},{6,2},{0,4},{2,6},{12,8},{14,10},{8,12},{10,14},{13,1},{15,3... | collective-permute-start | bytes 196616 | tf_op jit(solution)/shard_map/ppermute | solution.py:316
  23.3 0.0 collective-permute-done.6.theirs
  23.3 0.9 %collective-permute-start.7 = (bf16[128,128]{1,0:T(8,128)(2,1)S(1)}, bf16[128,128]{1,0:T(8,128)(2,1)S(1)}, u32[]{:S(2)}, u32[]{:S(2)}) collective-permute-start(bf16[128,128]{1,0:T(8,128)(2,1)S(1)} %get-tuple-element.45), channel_id=1, source_target_pairs={{9,0},{8,1},{11,2},{10,3},{13,4},{12,5},{15,6},{14,7},{1,8},{0,9},... | collective-permute-start | bytes 98312 | tf_op jit(solution)/shard_map/ppermute | solution.py:316
  24.2 1.8 %collective-permute-done.9.refs_1_ = bf16[256,128]{1,0:T(8,128)(2,1)S(1)} collective-permute-done((bf16[256,128]{1,0:T(8,128)(2,1)S(1)}, bf16[256,128]{1,0:T(8,128)(2,1)S(1)}, u32[]{:S(2)}, u32[]{:S(2)}) %collective-permute-start.9) | collective-permute-done | bytes 65568 | tf_op jit(solution)/shard_map/ppermute | solution.py:316
  25.9 0.0 collective-permute-start.10
  25.9 1.7 %collective-permute-done.7.refs_0_ = bf16[128,128]{1,0:T(8,128)(2,1)S(1)} collective-permute-done((bf16[128,128]{1,0:T(8,128)(2,1)S(1)}, bf16[128,128]{1,0:T(8,128)(2,1)S(1)}, u32[]{:S(2)}, u32[]{:S(2)}) %collective-permute-start.7) | collective-permute-done | bytes 32800 | tf_op jit(solution)/shard_map/ppermute | solution.py:316
  27.6 0.0 collective-permute-done.10.refs_2_
  27.6 0.6 %shard_map.81 = f32[128,128]{1,0:T(8,128)} custom-call(f32[128,128]{1,0:T(8,128)S(1)} %get-tuple-element.44.kept, bf16[128,128]{1,0:T(8,128)(2,1)S(1)} %collective-permute-done.7.refs_0_, bf16[256,128]{1,0:T(8,128)(2,1)S(1)} %collective-permute-done.9.refs_1_, bf16[128,128]{1,0:T(8,128)(2,1)S(1)} %collective-permute-done.10.refs_2_), custom_call_target="tpu_custom_call" | custom-call | tf_op jit(solution)/shard_map/pallas_call | solution.py:418
  (9 shorter events, 0.1 us)
Async XLA Ops:
  0.9 8.2 %collective-permute-start.3 = (bf16[144,128]{1,0:T(8,128)(2,1)S(1)}, bf16[144,128]{1,0:T(8,128)(2,1)S(1)}, u32[]{:S(2)}, u32[]{:S(2)}) collective-permute-start(bf16[144,128]{1,0:T(8,128)(2,1)S(1)} %get-tuple-element.27), channel_id=1, source_target_pairs={{0,13},{1,12},{2,15},{3,14},{4,9},{5,8},{6,11},{7,10},{8,5},{9,4},... | collective-permute-start | bytes 110600 | tf_op jit(solution)/shard_map/ppermute | solution.py:316
  5.6 4.3 %collective-permute-start.2 = (bf16[144,128]{1,0:T(8,128)(2,1)S(1)}, bf16[144,128]{1,0:T(8,128)(2,1)S(1)}, u32[]{:S(2)}, u32[]{:S(2)}) collective-permute-start(bf16[144,128]{1,0:T(8,128)(2,1)S(1)} %get-tuple-element.27), channel_id=1, source_target_pairs={{0,9},{1,8},{2,11},{3,10},{4,13},{5,12},{6,15},{7,14},{8,1},{9,0},... | collective-permute-start | bytes 110600 | tf_op jit(solution)/shard_map/ppermute | solution.py:316
  5.6 4.3 %collective-permute-start.1 = (bf16[144,128]{1,0:T(8,128)(2,1)S(1)}, bf16[144,128]{1,0:T(8,128)(2,1)S(1)}, u32[]{:S(2)}, u32[]{:S(2)}) collective-permute-start(bf16[144,128]{1,0:T(8,128)(2,1)S(1)} %get-tuple-element.27), channel_id=1, source_target_pairs={{0,5},{1,4},{2,7},{3,6},{4,1},{5,0},{6,3},{7,2},{8,13},{9,12},{10,... | collective-permute-start | bytes 110600 | tf_op jit(solution)/shard_map/ppermute | solution.py:316
  5.7 3.4 %collective-permute-start = (f32[8,128]{1,0:T(8,128)S(1)}, f32[8,128]{1,0:T(8,128)S(1)}, u32[]{:S(2)}, u32[]{:S(2)}) collective-permute-start(f32[8,128]{1,0:T(8,128)S(1)} %get-tuple-element.26.refs_0_.own_points), channel_id=1, source_target_pairs={{0,3},{1,2},{2,1},{3,0},{4,7},{5,6},{6,5},{7,4},{8,11},{9,10},{10,... | collective-permute-start | bytes 12296 | tf_op jit(solution)/shard_map/ppermute | solution.py:316
  10.0 1.8 %collective-permute-start.4 = (bf16[4,144,128]{2,1,0:T(8,128)(2,1)S(1)}, bf16[4,144,128]{2,1,0:T(8,128)(2,1)S(1)}, u32[]{:S(2)}, u32[]{:S(2)}) collective-permute-start(bf16[4,144,128]{2,1,0:T(8,128)(2,1)S(1)} %pad_maximum_fusion.refs_2_), channel_id=1, source_target_pairs={{0,1},{1,0},{2,3},{3,2},{4,5},{5,4},{6,7},{7,6},{8,9},{9,8},{10,11... | collective-permute-start | bytes 442376 | tf_op jit(solution)/shard_map/ppermute | solution.py:316
  13.1 5.5 %collective-permute-start.5 = (bf16[512,128]{1,0:T(8,128)(2,1)S(1)}, bf16[512,128]{1,0:T(8,128)(2,1)S(1)}, u32[]{:S(2)}, u32[]{:S(2)}) collective-permute-start(bf16[512,128]{1,0:T(8,128)(2,1)S(1)} %get-tuple-element.36), channel_id=1, source_target_pairs={{0,3},{1,2},{2,1},{3,0},{4,7},{5,6},{6,5},{7,4},{8,11},{9,10},{10,... | collective-permute-start | bytes 393224 | tf_op jit(solution)/shard_map/ppermute | solution.py:316
  19.2 1.4 %collective-permute-start.8 = (bf16[256,128]{1,0:T(8,128)(2,1)S(1)}, bf16[256,128]{1,0:T(8,128)(2,1)S(1)}, u32[]{:S(2)}, u32[]{:S(2)}) collective-permute-start(bf16[256,128]{1,0:T(8,128)(2,1)S(1)} %get-tuple-element.46), channel_id=1, source_target_pairs={{0,1},{1,0},{2,3},{3,2},{4,5},{5,4},{6,7},{7,6},{8,9},{9,8},{10,11... | collective-permute-start | bytes 196616 | tf_op jit(solution)/shard_map/ppermute | solution.py:316
  19.6 3.6 %collective-permute-start.6 = (bf16[256,128]{1,0:T(8,128)(2,1)S(1)}, bf16[256,128]{1,0:T(8,128)(2,1)S(1)}, u32[]{:S(2)}, u32[]{:S(2)}) collective-permute-start(bf16[256,128]{1,0:T(8,128)(2,1)S(1)} %get-tuple-element.43), channel_id=1, source_target_pairs={{0,1},{1,0},{2,3},{3,2},{4,5},{5,4},{6,7},{7,6},{8,9},{9,8},{10,11... | collective-permute-start | bytes 196616 | tf_op jit(solution)/shard_map/ppermute | solution.py:316
  20.6 5.4 %collective-permute-start.9 = (bf16[256,128]{1,0:T(8,128)(2,1)S(1)}, bf16[256,128]{1,0:T(8,128)(2,1)S(1)}, u32[]{:S(2)}, u32[]{:S(2)}) collective-permute-start(bf16[256,128]{1,0:T(8,128)(2,1)S(1)} %shard_map.80), channel_id=1, source_target_pairs={{4,0},{6,2},{0,4},{2,6},{12,8},{14,10},{8,12},{10,14},{13,1},{15,3... | collective-permute-start | bytes 196616 | tf_op jit(solution)/shard_map/ppermute | solution.py:316
  23.3 4.3 %collective-permute-start.7 = (bf16[128,128]{1,0:T(8,128)(2,1)S(1)}, bf16[128,128]{1,0:T(8,128)(2,1)S(1)}, u32[]{:S(2)}, u32[]{:S(2)}) collective-permute-start(bf16[128,128]{1,0:T(8,128)(2,1)S(1)} %get-tuple-element.45), channel_id=1, source_target_pairs={{9,0},{8,1},{11,2},{10,3},{13,4},{12,5},{15,6},{14,7},{1,8},{0,9},... | collective-permute-start | bytes 98312 | tf_op jit(solution)/shard_map/ppermute | solution.py:316
  25.9 1.7 %collective-permute-start.10 = (bf16[128,128]{1,0:T(8,128)(2,1)S(1)}, bf16[128,128]{1,0:T(8,128)(2,1)S(1)}, u32[]{:S(2)}, u32[]{:S(2)}) collective-permute-start(bf16[128,128]{1,0:T(8,128)(2,1)S(1)} %slice.44), channel_id=1, source_target_pairs={{0,1},{1,0},{2,3},{3,2},{4,5},{5,4},{6,7},{7,6},{8,9},{9,8},{10,11... | collective-permute-start | bytes 98312 | tf_op jit(solution)/shard_map/ppermute | solution.py:316

commit v9 on v8

--- a/solution.py
+++ b/solution.py
@@ -117,7 +117,7 @@
 
 
 TILE = 32
-LANES = 512
+LANES = 256
 
 
 def blocks(total, most):

time: 28.4 us -> 28.4 us (level)
  no operation moved by 1% of the time
where the time goes in v9:
time: 28.4 us; the launch traced here: 28.2 us
  starting transfers between devices  12.6 us (44%)
  waiting for transfers between devices  8.23 us (29%)
  Pallas kernels  7.28 us (26%)
    ppermute x11, starting transfers between devices, swap(): lax.ppermute(x, 'refl', [(b, a) for a, b in links] if back else links)  12.6 us
    ppermute x11, waiting for transfers between devices, swap(): lax.ppermute(x, 'refl', [(b, a) for a, b in links] if back else links)  8.23 us
    pallas_call x2, Pallas kernels, green(): call(functools.partial(green_body, len(points), len(bases[:1]), scale), [...  2.86 us
    pallas_call x1, Pallas kernels, per_device(): call(kernel_body, [((count, half_points), BF16)] * 4, [pltpu.VMEM((2 * co...  1.93 us
    pallas_call x1, Pallas kernels, per_device(): call(pack_body, [((sources + PACK_ROWS, lanes), BF16), ((8, lanes), F32)]...  0.85 us
    pallas_call x1, Pallas kernels, per_device(): return call(finish_body, [((directions, lanes), F32)])(kept, *arrived)[0]  0.65 us
  transfers between devices with their start and end apart: 11, of which 6 were waited for; matrix products, arithmetic and copies ran while one was open for 0% of the time, Pallas kernels for 14%

profile of v9, /device:TPU:1, one launch (start us, length us, event | category | flops | bytes accessed | tf_op | source)
XLA Modules:
  0.0 28.2 jit_solution(37144447362087216)
XLA Ops:
  0.0 0.9 %shard_map.73 = (bf16[144,128]{1,0:T(8,128)(2,1)S(1)}, f32[8,128]{1,0:T(8,128)S(1)}) custom-call(bf16[128,128]{1,0:T(8,128)(2,1)} %weights.1, f32[2,128]{1,0:T(2,128)} %feed_plane.1, f32[1,128]{1,0:T(1,128)} %bitcast.17, f32[2,128]{1,0:T(2,128)} %cosines.1, f32[2,256]{1,0:T(2,128)} %plane.1, f32[2,128]{1,0:T(2,128)} %bitcast.15, f32[2,128]{1,0:T(2,128)} %bitcast.16), custom_call_target="tpu_custom_call" | custom-call | tf_op jit(solution)/shard_map/pallas_call | solution.py:318
  0.9 4.8 %collective-permute-start.3 = (bf16[144,128]{1,0:T(8,128)(2,1)S(1)}, bf16[144,128]{1,0:T(8,128)(2,1)S(1)}, u32[]{:S(2)}, u32[]{:S(2)}) collective-permute-start(bf16[144,128]{1,0:T(8,128)(2,1)S(1)} %get-tuple-element.27), channel_id=1, source_target_pairs={{0,13},{1,12},{2,15},{3,14},{4,9},{5,8},{6,11},{7,10},{8,5},{9,4},... | collective-permute-start | bytes 110600 | tf_op jit(solution)/shard_map/ppermute | solution.py:316
  5.6 0.0 collective-permute-start.2
  5.6 0.1 collective-permute-start.1
  5.7 1.8 %collective-permute-start = (f32[8,128]{1,0:T(8,128)S(1)}, f32[8,128]{1,0:T(8,128)S(1)}, u32[]{:S(2)}, u32[]{:S(2)}) collective-permute-start(f32[8,128]{1,0:T(8,128)S(1)} %get-tuple-element.26.refs_0_.own_points), channel_id=1, source_target_pairs={{0,3},{1,2},{2,1},{3,0},{4,7},{5,6},{6,5},{7,4},{8,11},{9,10},{10,... | collective-permute-start | bytes 12296 | tf_op jit(solution)/shard_map/ppermute | solution.py:316
  7.5 1.6 %collective-permute-done.refs_1_.far_points = f32[8,128]{1,0:T(8,128)S(1)} collective-permute-done((f32[8,128]{1,0:T(8,128)S(1)}, f32[8,128]{1,0:T(8,128)S(1)}, u32[]{:S(2)}, u32[]{:S(2)}) %collective-permute-start) | collective-permute-done | bytes 4128 | tf_op jit(solution)/shard_map/ppermute | solution.py:316
  9.1 0.0 collective-permute-done.3
  9.1 0.8 %collective-permute-done.2 = bf16[144,128]{1,0:T(8,128)(2,1)S(1)} collective-permute-done((bf16[144,128]{1,0:T(8,128)(2,1)S(1)}, bf16[144,128]{1,0:T(8,128)(2,1)S(1)}, u32[]{:S(2)}, u32[]{:S(2)}) %collective-permute-start.2) | collective-permute-done | bytes 36896 | tf_op jit(solution)/shard_map/ppermute | solution.py:316
  9.9 0.0 collective-permute-done.1
  10.0 0.2 collective-permute-start.4
  10.2 1.5 %shard_map.74 = (f32[512,128]{1,0:T(8,128)S(1)}, f32[512,4]{1,0:T(8,128)S(1)}, bf16[512,32]{1,0:T(8,128)(2,1)S(1)}) custom-call(f32[8,128]{1,0:T(8,128)S(1)} %get-tuple-element.26.refs_0_.own_points, f32[8,128]{1,0:T(8,128)S(1)} %collective-permute-done.refs_1_.far_points, bf16[4,144,128]{2,1,0:T(8,128)(2,1)S(1)} %pad_maximum_fusion.refs_2_), custom_call_target="tpu_custom_call" | custom-call | tf_op jit(solution)/shard_map/pallas_call | solution.py:361
  11.7 0.0 collective-permute-done.4.refs_2_
  11.7 1.4 %shard_map.75 = (f32[512,128]{1,0:T(8,128)S(1)}, bf16[512,128]{1,0:T(8,128)(2,1)S(1)}) custom-call(f32[8,128]{1,0:T(8,128)S(1)} %get-tuple-element.26.refs_0_.own_points, f32[8,128]{1,0:T(8,128)S(1)} %collective-permute-done.refs_1_.far_points, bf16[4,144,128]{2,1,0:T(8,128)(2,1)S(1)} %collective-permute-done.4.refs_2_, ...), custom_call_target="tpu_custom_call" | custom-call | tf_op jit(solution)/shard_map/pallas_call | solution.py:361
  13.1 1.5 %collective-permute-start.5 = (bf16[512,128]{1,0:T(8,128)(2,1)S(1)}, bf16[512,128]{1,0:T(8,128)(2,1)S(1)}, u32[]{:S(2)}, u32[]{:S(2)}) collective-permute-start(bf16[512,128]{1,0:T(8,128)(2,1)S(1)} %get-tuple-element.36), channel_id=1, source_target_pairs={{0,3},{1,2},{2,1},{3,0},{4,7},{5,6},{6,5},{7,4},{8,11},{9,10},{10,... | collective-permute-start | bytes 393224 | tf_op jit(solution)/shard_map/ppermute | solution.py:316
  14.6 1.9 %shard_map.76 = (bf16[512,512]{1,0:T(8,128)(2,1)S(1)}, bf16[512,512]{1,0:T(8,128)(2,1)S(1)}, bf16[512,512]{1,0:T(8,128)(2,1)S(1)}, bf16[512,512]{1,0:T(8,128)(2,1)S(1)}) custom-call(f32[8,128]{1,0:T(8,128)S(1)} %get-tuple-element.26.refs_0_.own_points, f32[8,128]{1,0:T(8,128)S(1)} %collective-permute-done.refs_1_.far_points, ...), custom_call_target="tpu_custom_call" | custom-call | flops 15728640 | tf_op jit(solution)/shard_map/pallas_call | solution.py:386
  16.6 2.1 %collective-permute-done.5.theirs = bf16[512,128]{1,0:T(8,128)(2,1)S(1)} collective-permute-done((bf16[512,128]{1,0:T(8,128)(2,1)S(1)}, bf16[512,128]{1,0:T(8,128)(2,1)S(1)}, u32[]{:S(2)}, u32[]{:S(2)}) %collective-permute-start.5) | collective-permute-done | bytes 131104 | tf_op jit(solution)/shard_map/ppermute | solution.py:316
  18.6 0.5 %shard_map.77 = (bf16[512,128]{1,0:T(8,128)(2,1)S(1)}, bf16[512,128]{1,0:T(8,128)(2,1)S(1)}, bf16[256,128]{1,0:T(8,128)(2,1)S(1)}, bf16[256,128]{1,0:T(8,128)(2,1)S(1)}) custom-call(f32[512,128]{1,0:T(8,128)S(1)} %get-tuple-element.35.mine, bf16[512,128]{1,0:T(8,128)(2,1)S(1)} %collective-permute-done.5.theirs, ...), custom_call_target="tpu_custom_call" | custom-call | tf_op jit(solution)/shard_map/pallas_call | solution.py:396
  19.2 0.5 %collective-permute-start.8 = (bf16[256,128]{1,0:T(8,128)(2,1)S(1)}, bf16[256,128]{1,0:T(8,128)(2,1)S(1)}, u32[]{:S(2)}, u32[]{:S(2)}) collective-permute-start(bf16[256,128]{1,0:T(8,128)(2,1)S(1)} %get-tuple-element.46), channel_id=1, source_target_pairs={{0,1},{1,0},{2,3},{3,2},{4,5},{5,4},{6,7},{7,6},{8,9},{9,8},{10,11... | collective-permute-start | bytes 196616 | tf_op jit(solution)/shard_map/ppermute | solution.py:316
  19.6 0.1 collective-permute-start.6
  19.7 0.4 %shard_map.78.mine = f32[512,128]{1,0:T(8,128)S(1)} custom-call(bf16[512,128]{1,0:T(8,128)(2,1)S(1)} %get-tuple-element.39.held, bf16[512,128]{1,0:T(8,128)(2,1)S(1)} %get-tuple-element.40.held_turned, bf16[512,512]{1,0:T(8,128)(2,1)S(1)} %get-tuple-element.41.kernel_re, bf16[512,512]{1,0:T(8,128)(2,1)S(1)} %get-tuple-element.42.kernel_im), custom_call_target="tpu_custom_call" | custom-call | tf_op jit(solution)/shard_map/pallas_call | solution.py:401
  20.2 0.3 %collective-permute-done.8.theirs = bf16[256,128]{1,0:T(8,128)(2,1)S(1)} collective-permute-done((bf16[256,128]{1,0:T(8,128)(2,1)S(1)}, bf16[256,128]{1,0:T(8,128)(2,1)S(1)}, u32[]{:S(2)}, u32[]{:S(2)}) %collective-permute-start.8) | collective-permute-done | bytes 65568 | tf_op jit(solution)/shard_map/ppermute | solution.py:316
  20.5 2.7 %collective-permute-start.9 = (bf16[256,128]{1,0:T(8,128)(2,1)S(1)}, bf16[256,128]{1,0:T(8,128)(2,1)S(1)}, u32[]{:S(2)}, u32[]{:S(2)}) collective-permute-start(bf16[256,128]{1,0:T(8,128)(2,1)S(1)} %shard_map.80), channel_id=1, source_target_pairs={{4,0},{6,2},{0,4},{2,6},{12,8},{14,10},{8,12},{10,14},{13,1},{15,3... | collective-permute-start | bytes 196616 | tf_op jit(solution)/shard_map/ppermute | solution.py:316
  23.3 0.0 collective-permute-done.6.theirs
  23.3 0.9 %collective-permute-start.7 = (bf16[128,128]{1,0:T(8,128)(2,1)S(1)}, bf16[128,128]{1,0:T(8,128)(2,1)S(1)}, u32[]{:S(2)}, u32[]{:S(2)}) collective-permute-start(bf16[128,128]{1,0:T(8,128)(2,1)S(1)} %get-tuple-element.45), channel_id=1, source_target_pairs={{9,0},{8,1},{11,2},{10,3},{13,4},{12,5},{15,6},{14,7},{1,8},{0,9},... | collective-permute-start | bytes 98312 | tf_op jit(solution)/shard_map/ppermute | solution.py:316
  24.2 1.8 %collective-permute-done.9.refs_1_ = bf16[256,128]{1,0:T(8,128)(2,1)S(1)} collective-permute-done((bf16[256,128]{1,0:T(8,128)(2,1)S(1)}, bf16[256,128]{1,0:T(8,128)(2,1)S(1)}, u32[]{:S(2)}, u32[]{:S(2)}) %collective-permute-start.9) | collective-permute-done | bytes 65568 | tf_op jit(solution)/shard_map/ppermute | solution.py:316
  25.9 0.0 collective-permute-start.10
  25.9 1.7 %collective-permute-done.7.refs_0_ = bf16[128,128]{1,0:T(8,128)(2,1)S(1)} collective-permute-done((bf16[128,128]{1,0:T(8,128)(2,1)S(1)}, bf16[128,128]{1,0:T(8,128)(2,1)S(1)}, u32[]{:S(2)}, u32[]{:S(2)}) %collective-permute-start.7) | collective-permute-done | bytes 32800 | tf_op jit(solution)/shard_map/ppermute | solution.py:316
  27.6 0.0 collective-permute-done.10.refs_2_
  27.6 0.6 %shard_map.81 = f32[128,128]{1,0:T(8,128)} custom-call(f32[128,128]{1,0:T(8,128)S(1)} %get-tuple-element.44.kept, bf16[128,128]{1,0:T(8,128)(2,1)S(1)} %collective-permute-done.7.refs_0_, bf16[256,128]{1,0:T(8,128)(2,1)S(1)} %collective-permute-done.9.refs_1_, bf16[128,128]{1,0:T(8,128)(2,1)S(1)} %collective-permute-done.10.refs_2_), custom_call_target="tpu_custom_call" | custom-call | tf_op jit(solution)/shard_map/pallas_call | solution.py:418
  (9 shorter events, 0.1 us)
Async XLA Ops:
  0.9 8.2 %collective-permute-start.3 = (bf16[144,128]{1,0:T(8,128)(2,1)S(1)}, bf16[144,128]{1,0:T(8,128)(2,1)S(1)}, u32[]{:S(2)}, u32[]{:S(2)}) collective-permute-start(bf16[144,128]{1,0:T(8,128)(2,1)S(1)} %get-tuple-element.27), channel_id=1, source_target_pairs={{0,13},{1,12},{2,15},{3,14},{4,9},{5,8},{6,11},{7,10},{8,5},{9,4},... | collective-permute-start | bytes 110600 | tf_op jit(solution)/shard_map/ppermute | solution.py:316
  5.6 4.3 %collective-permute-start.2 = (bf16[144,128]{1,0:T(8,128)(2,1)S(1)}, bf16[144,128]{1,0:T(8,128)(2,1)S(1)}, u32[]{:S(2)}, u32[]{:S(2)}) collective-permute-start(bf16[144,128]{1,0:T(8,128)(2,1)S(1)} %get-tuple-element.27), channel_id=1, source_target_pairs={{0,9},{1,8},{2,11},{3,10},{4,13},{5,12},{6,15},{7,14},{8,1},{9,0},... | collective-permute-start | bytes 110600 | tf_op jit(solution)/shard_map/ppermute | solution.py:316
  5.6 4.3 %collective-permute-start.1 = (bf16[144,128]{1,0:T(8,128)(2,1)S(1)}, bf16[144,128]{1,0:T(8,128)(2,1)S(1)}, u32[]{:S(2)}, u32[]{:S(2)}) collective-permute-start(bf16[144,128]{1,0:T(8,128)(2,1)S(1)} %get-tuple-element.27), channel_id=1, source_target_pairs={{0,5},{1,4},{2,7},{3,6},{4,1},{5,0},{6,3},{7,2},{8,13},{9,12},{10,... | collective-permute-start | bytes 110600 | tf_op jit(solution)/shard_map/ppermute | solution.py:316
  5.7 3.4 %collective-permute-start = (f32[8,128]{1,0:T(8,128)S(1)}, f32[8,128]{1,0:T(8,128)S(1)}, u32[]{:S(2)}, u32[]{:S(2)}) collective-permute-start(f32[8,128]{1,0:T(8,128)S(1)} %get-tuple-element.26.refs_0_.own_points), channel_id=1, source_target_pairs={{0,3},{1,2},{2,1},{3,0},{4,7},{5,6},{6,5},{7,4},{8,11},{9,10},{10,... | collective-permute-start | bytes 12296 | tf_op jit(solution)/shard_map/ppermute | solution.py:316
  10.0 1.7 %collective-permute-start.4 = (bf16[4,144,128]{2,1,0:T(8,128)(2,1)S(1)}, bf16[4,144,128]{2,1,0:T(8,128)(2,1)S(1)}, u32[]{:S(2)}, u32[]{:S(2)}) collective-permute-start(bf16[4,144,128]{2,1,0:T(8,128)(2,1)S(1)} %pad_maximum_fusion.refs_2_), channel_id=1, source_target_pairs={{0,1},{1,0},{2,3},{3,2},{4,5},{5,4},{6,7},{7,6},{8,9},{9,8},{10,11... | collective-permute-start | bytes 442376 | tf_op jit(solution)/shard_map/ppermute | solution.py:316
  13.1 5.5 %collective-permute-start.5 = (bf16[512,128]{1,0:T(8,128)(2,1)S(1)}, bf16[512,128]{1,0:T(8,128)(2,1)S(1)}, u32[]{:S(2)}, u32[]{:S(2)}) collective-permute-start(bf16[512,128]{1,0:T(8,128)(2,1)S(1)} %get-tuple-element.36), channel_id=1, source_target_pairs={{0,3},{1,2},{2,1},{3,0},{4,7},{5,6},{6,5},{7,4},{8,11},{9,10},{10,... | collective-permute-start | bytes 393224 | tf_op jit(solution)/shard_map/ppermute | solution.py:316
  19.2 1.4 %collective-permute-start.8 = (bf16[256,128]{1,0:T(8,128)(2,1)S(1)}, bf16[256,128]{1,0:T(8,128)(2,1)S(1)}, u32[]{:S(2)}, u32[]{:S(2)}) collective-permute-start(bf16[256,128]{1,0:T(8,128)(2,1)S(1)} %get-tuple-element.46), channel_id=1, source_target_pairs={{0,1},{1,0},{2,3},{3,2},{4,5},{5,4},{6,7},{7,6},{8,9},{9,8},{10,11... | collective-permute-start | bytes 196616 | tf_op jit(solution)/shard_map/ppermute | solution.py:316
  19.6 3.6 %collective-permute-start.6 = (bf16[256,128]{1,0:T(8,128)(2,1)S(1)}, bf16[256,128]{1,0:T(8,128)(2,1)S(1)}, u32[]{:S(2)}, u32[]{:S(2)}) collective-permute-start(bf16[256,128]{1,0:T(8,128)(2,1)S(1)} %get-tuple-element.43), channel_id=1, source_target_pairs={{0,1},{1,0},{2,3},{3,2},{4,5},{5,4},{6,7},{7,6},{8,9},{9,8},{10,11... | collective-permute-start | bytes 196616 | tf_op jit(solution)/shard_map/ppermute | solution.py:316
  20.5 5.4 %collective-permute-start.9 = (bf16[256,128]{1,0:T(8,128)(2,1)S(1)}, bf16[256,128]{1,0:T(8,128)(2,1)S(1)}, u32[]{:S(2)}, u32[]{:S(2)}) collective-permute-start(bf16[256,128]{1,0:T(8,128)(2,1)S(1)} %shard_map.80), channel_id=1, source_target_pairs={{4,0},{6,2},{0,4},{2,6},{12,8},{14,10},{8,12},{10,14},{13,1},{15,3... | collective-permute-start | bytes 196616 | tf_op jit(solution)/shard_map/ppermute | solution.py:316
  23.3 4.3 %collective-permute-start.7 = (bf16[128,128]{1,0:T(8,128)(2,1)S(1)}, bf16[128,128]{1,0:T(8,128)(2,1)S(1)}, u32[]{:S(2)}, u32[]{:S(2)}) collective-permute-start(bf16[128,128]{1,0:T(8,128)(2,1)S(1)} %get-tuple-element.45), channel_id=1, source_target_pairs={{9,0},{8,1},{11,2},{10,3},{13,4},{12,5},{15,6},{14,7},{1,8},{0,9},... | collective-permute-start | bytes 98312 | tf_op jit(solution)/shard_map/ppermute | solution.py:316
  25.9 1.7 %collective-permute-start.10 = (bf16[128,128]{1,0:T(8,128)(2,1)S(1)}, bf16[128,128]{1,0:T(8,128)(2,1)S(1)}, u32[]{:S(2)}, u32[]{:S(2)}) collective-permute-start(bf16[128,128]{1,0:T(8,128)(2,1)S(1)} %slice.44), channel_id=1, source_target_pairs={{0,1},{1,0},{2,3},{3,2},{4,5},{5,4},{6,7},{7,6},{8,9},{9,8},{10,11... | collective-permute-start | bytes 98312 | tf_op jit(solution)/shard_map/ppermute | solution.py:316

commit v10 on v9

--- a/solution.py
+++ b/solution.py
@@ -117,7 +117,7 @@
 
 
 TILE = 32
-LANES = 256
+LANES = 128
 
 
 def blocks(total, most):

time: 28.4 us -> 28.6 us (level)
  no operation moved by 1% of the time
where the time goes in v10:
time: 28.6 us; the launch traced here: 28.5 us
  starting transfers between devices  12.6 us (44%)
  waiting for transfers between devices  8.24 us (29%)
  Pallas kernels  7.49 us (26%)
    ppermute x11, starting transfers between devices, swap(): lax.ppermute(x, 'refl', [(b, a) for a, b in links] if back else links)  12.6 us
    ppermute x11, waiting for transfers between devices, swap(): lax.ppermute(x, 'refl', [(b, a) for a, b in links] if back else links)  8.24 us
    pallas_call x2, Pallas kernels, green(): call(functools.partial(green_body, len(points), len(bases[:1]), scale), [...  3.06 us
    pallas_call x1, Pallas kernels, per_device(): call(kernel_body, [((count, half_points), BF16)] * 4, [pltpu.VMEM((2 * co...  1.93 us
    pallas_call x1, Pallas kernels, per_device(): call(pack_body, [((sources + PACK_ROWS, lanes), BF16), ((8, lanes), F32)]...  0.85 us
    pallas_call x1, Pallas kernels, per_device(): return call(finish_body, [((directions, lanes), F32)])(kept, *arrived)[0]  0.65 us
  transfers between devices with their start and end apart: 11, of which 6 were waited for; matrix products, arithmetic and copies ran while one was open for 0% of the time, Pallas kernels for 14%

profile of v10, /device:TPU:1, one launch (start us, length us, event | category | flops | bytes accessed | tf_op | source)
XLA Modules:
  0.0 28.5 jit_solution(9822286084324689413)
XLA Ops:
  0.0 0.9 %shard_map.73 = (bf16[144,128]{1,0:T(8,128)(2,1)S(1)}, f32[8,128]{1,0:T(8,128)S(1)}) custom-call(bf16[128,128]{1,0:T(8,128)(2,1)} %weights.1, f32[2,128]{1,0:T(2,128)} %feed_plane.1, f32[1,128]{1,0:T(1,128)} %bitcast.17, f32[2,128]{1,0:T(2,128)} %cosines.1, f32[2,256]{1,0:T(2,128)} %plane.1, f32[2,128]{1,0:T(2,128)} %bitcast.15, f32[2,128]{1,0:T(2,128)} %bitcast.16), custom_call_target="tpu_custom_call" | custom-call | tf_op jit(solution)/shard_map/pallas_call | solution.py:318
  0.9 4.8 %collective-permute-start.3 = (bf16[144,128]{1,0:T(8,128)(2,1)S(1)}, bf16[144,128]{1,0:T(8,128)(2,1)S(1)}, u32[]{:S(2)}, u32[]{:S(2)}) collective-permute-start(bf16[144,128]{1,0:T(8,128)(2,1)S(1)} %get-tuple-element.27), channel_id=1, source_target_pairs={{0,13},{1,12},{2,15},{3,14},{4,9},{5,8},{6,11},{7,10},{8,5},{9,4},... | collective-permute-start | bytes 110600 | tf_op jit(solution)/shard_map/ppermute | solution.py:316
  5.6 0.0 collective-permute-start.2
  5.6 0.1 collective-permute-start.1
  5.7 1.8 %collective-permute-start = (f32[8,128]{1,0:T(8,128)S(1)}, f32[8,128]{1,0:T(8,128)S(1)}, u32[]{:S(2)}, u32[]{:S(2)}) collective-permute-start(f32[8,128]{1,0:T(8,128)S(1)} %get-tuple-element.26.refs_0_.own_points), channel_id=1, source_target_pairs={{0,3},{1,2},{2,1},{3,0},{4,7},{5,6},{6,5},{7,4},{8,11},{9,10},{10,... | collective-permute-start | bytes 12296 | tf_op jit(solution)/shard_map/ppermute | solution.py:316
  7.5 1.6 %collective-permute-done.refs_1_.far_points = f32[8,128]{1,0:T(8,128)S(1)} collective-permute-done((f32[8,128]{1,0:T(8,128)S(1)}, f32[8,128]{1,0:T(8,128)S(1)}, u32[]{:S(2)}, u32[]{:S(2)}) %collective-permute-start) | collective-permute-done | bytes 4128 | tf_op jit(solution)/shard_map/ppermute | solution.py:316
  9.1 0.0 collective-permute-done.3
  9.1 0.8 %collective-permute-done.2 = bf16[144,128]{1,0:T(8,128)(2,1)S(1)} collective-permute-done((bf16[144,128]{1,0:T(8,128)(2,1)S(1)}, bf16[144,128]{1,0:T(8,128)(2,1)S(1)}, u32[]{:S(2)}, u32[]{:S(2)}) %collective-permute-start.2) | collective-permute-done | bytes 36896 | tf_op jit(solution)/shard_map/ppermute | solution.py:316
  9.9 0.0 collective-permute-done.1
  10.0 0.2 collective-permute-start.4
  10.2 1.6 %shard_map.74 = (f32[512,128]{1,0:T(8,128)S(1)}, f32[512,4]{1,0:T(8,128)S(1)}, bf16[512,32]{1,0:T(8,128)(2,1)S(1)}) custom-call(f32[8,128]{1,0:T(8,128)S(1)} %get-tuple-element.26.refs_0_.own_points, f32[8,128]{1,0:T(8,128)S(1)} %collective-permute-done.refs_1_.far_points, bf16[4,144,128]{2,1,0:T(8,128)(2,1)S(1)} %pad_maximum_fusion.refs_2_), custom_call_target="tpu_custom_call" | custom-call | tf_op jit(solution)/shard_map/pallas_call | solution.py:361
  11.8 0.0 collective-permute-done.4.refs_2_
  11.9 1.4 %shard_map.75 = (f32[512,128]{1,0:T(8,128)S(1)}, bf16[512,128]{1,0:T(8,128)(2,1)S(1)}) custom-call(f32[8,128]{1,0:T(8,128)S(1)} %get-tuple-element.26.refs_0_.own_points, f32[8,128]{1,0:T(8,128)S(1)} %collective-permute-done.refs_1_.far_points, bf16[4,144,128]{2,1,0:T(8,128)(2,1)S(1)} %collective-permute-done.4.refs_2_, ...), custom_call_target="tpu_custom_call" | custom-call | tf_op jit(solution)/shard_map/pallas_call | solution.py:361
  13.3 1.5 %collective-permute-start.5 = (bf16[512,128]{1,0:T(8,128)(2,1)S(1)}, bf16[512,128]{1,0:T(8,128)(2,1)S(1)}, u32[]{:S(2)}, u32[]{:S(2)}) collective-permute-start(bf16[512,128]{1,0:T(8,128)(2,1)S(1)} %get-tuple-element.36), channel_id=1, source_target_pairs={{0,3},{1,2},{2,1},{3,0},{4,7},{5,6},{6,5},{7,4},{8,11},{9,10},{10,... | collective-permute-start | bytes 393224 | tf_op jit(solution)/shard_map/ppermute | solution.py:316
  14.8 1.9 %shard_map.76 = (bf16[512,512]{1,0:T(8,128)(2,1)S(1)}, bf16[512,512]{1,0:T(8,128)(2,1)S(1)}, bf16[512,512]{1,0:T(8,128)(2,1)S(1)}, bf16[512,512]{1,0:T(8,128)(2,1)S(1)}) custom-call(f32[8,128]{1,0:T(8,128)S(1)} %get-tuple-element.26.refs_0_.own_points, f32[8,128]{1,0:T(8,128)S(1)} %collective-permute-done.refs_1_.far_points, ...), custom_call_target="tpu_custom_call" | custom-call | flops 15728640 | tf_op jit(solution)/shard_map/pallas_call | solution.py:386
  16.8 2.1 %collective-permute-done.5.theirs = bf16[512,128]{1,0:T(8,128)(2,1)S(1)} collective-permute-done((bf16[512,128]{1,0:T(8,128)(2,1)S(1)}, bf16[512,128]{1,0:T(8,128)(2,1)S(1)}, u32[]{:S(2)}, u32[]{:S(2)}) %collective-permute-start.5) | collective-permute-done | bytes 131104 | tf_op jit(solution)/shard_map/ppermute | solution.py:316
  18.8 0.5 %shard_map.77 = (bf16[512,128]{1,0:T(8,128)(2,1)S(1)}, bf16[512,128]{1,0:T(8,128)(2,1)S(1)}, bf16[256,128]{1,0:T(8,128)(2,1)S(1)}, bf16[256,128]{1,0:T(8,128)(2,1)S(1)}) custom-call(f32[512,128]{1,0:T(8,128)S(1)} %get-tuple-element.35.mine, bf16[512,128]{1,0:T(8,128)(2,1)S(1)} %collective-permute-done.5.theirs, ...), custom_call_target="tpu_custom_call" | custom-call | tf_op jit(solution)/shard_map/pallas_call | solution.py:396
  19.4 0.5 %collective-permute-start.8 = (bf16[256,128]{1,0:T(8,128)(2,1)S(1)}, bf16[256,128]{1,0:T(8,128)(2,1)S(1)}, u32[]{:S(2)}, u32[]{:S(2)}) collective-permute-start(bf16[256,128]{1,0:T(8,128)(2,1)S(1)} %get-tuple-element.46), channel_id=1, source_target_pairs={{0,1},{1,0},{2,3},{3,2},{4,5},{5,4},{6,7},{7,6},{8,9},{9,8},{10,11... | collective-permute-start | bytes 196616 | tf_op jit(solution)/shard_map/ppermute | solution.py:316
  19.8 0.1 collective-permute-start.6
  19.9 0.4 %shard_map.78.mine = f32[512,128]{1,0:T(8,128)S(1)} custom-call(bf16[512,128]{1,0:T(8,128)(2,1)S(1)} %get-tuple-element.39.held, bf16[512,128]{1,0:T(8,128)(2,1)S(1)} %get-tuple-element.40.held_turned, bf16[512,512]{1,0:T(8,128)(2,1)S(1)} %get-tuple-element.41.kernel_re, bf16[512,512]{1,0:T(8,128)(2,1)S(1)} %get-tuple-element.42.kernel_im), custom_call_target="tpu_custom_call" | custom-call | tf_op jit(solution)/shard_map/pallas_call | solution.py:401
  20.4 0.3 %collective-permute-done.8.theirs = bf16[256,128]{1,0:T(8,128)(2,1)S(1)} collective-permute-done((bf16[256,128]{1,0:T(8,128)(2,1)S(1)}, bf16[256,128]{1,0:T(8,128)(2,1)S(1)}, u32[]{:S(2)}, u32[]{:S(2)}) %collective-permute-start.8) | collective-permute-done | bytes 65568 | tf_op jit(solution)/shard_map/ppermute | solution.py:316
  20.8 2.7 %collective-permute-start.9 = (bf16[256,128]{1,0:T(8,128)(2,1)S(1)}, bf16[256,128]{1,0:T(8,128)(2,1)S(1)}, u32[]{:S(2)}, u32[]{:S(2)}) collective-permute-start(bf16[256,128]{1,0:T(8,128)(2,1)S(1)} %shard_map.80), channel_id=1, source_target_pairs={{4,0},{6,2},{0,4},{2,6},{12,8},{14,10},{8,12},{10,14},{13,1},{15,3... | collective-permute-start | bytes 196616 | tf_op jit(solution)/shard_map/ppermute | solution.py:316
  23.5 0.0 collective-permute-done.6.theirs
  23.5 0.9 %collective-permute-start.7 = (bf16[128,128]{1,0:T(8,128)(2,1)S(1)}, bf16[128,128]{1,0:T(8,128)(2,1)S(1)}, u32[]{:S(2)}, u32[]{:S(2)}) collective-permute-start(bf16[128,128]{1,0:T(8,128)(2,1)S(1)} %get-tuple-element.45), channel_id=1, source_target_pairs={{9,0},{8,1},{11,2},{10,3},{13,4},{12,5},{15,6},{14,7},{1,8},{0,9},... | collective-permute-start | bytes 98312 | tf_op jit(solution)/shard_map/ppermute | solution.py:316
  24.4 1.8 %collective-permute-done.9.refs_1_ = bf16[256,128]{1,0:T(8,128)(2,1)S(1)} collective-permute-done((bf16[256,128]{1,0:T(8,128)(2,1)S(1)}, bf16[256,128]{1,0:T(8,128)(2,1)S(1)}, u32[]{:S(2)}, u32[]{:S(2)}) %collective-permute-start.9) | collective-permute-done | bytes 65568 | tf_op jit(solution)/shard_map/ppermute | solution.py:316
  26.1 0.0 collective-permute-start.10
  26.1 1.7 %collective-permute-done.7.refs_0_ = bf16[128,128]{1,0:T(8,128)(2,1)S(1)} collective-permute-done((bf16[128,128]{1,0:T(8,128)(2,1)S(1)}, bf16[128,128]{1,0:T(8,128)(2,1)S(1)}, u32[]{:S(2)}, u32[]{:S(2)}) %collective-permute-start.7) | collective-permute-done | bytes 32800 | tf_op jit(solution)/shard_map/ppermute | solution.py:316
  27.8 0.0 collective-permute-done.10.refs_2_
  27.8 0.6 %shard_map.81 = f32[128,128]{1,0:T(8,128)} custom-call(f32[128,128]{1,0:T(8,128)S(1)} %get-tuple-element.44.kept, bf16[128,128]{1,0:T(8,128)(2,1)S(1)} %collective-permute-done.7.refs_0_, bf16[256,128]{1,0:T(8,128)(2,1)S(1)} %collective-permute-done.9.refs_1_, bf16[128,128]{1,0:T(8,128)(2,1)S(1)} %collective-permute-done.10.refs_2_), custom_call_target="tpu_custom_call" | custom-call | tf_op jit(solution)/shard_map/pallas_call | solution.py:418
  (9 shorter events, 0.1 us)
Async XLA Ops:
  0.9 8.2 %collective-permute-start.3 = (bf16[144,128]{1,0:T(8,128)(2,1)S(1)}, bf16[144,128]{1,0:T(8,128)(2,1)S(1)}, u32[]{:S(2)}, u32[]{:S(2)}) collective-permute-start(bf16[144,128]{1,0:T(8,128)(2,1)S(1)} %get-tuple-element.27), channel_id=1, source_target_pairs={{0,13},{1,12},{2,15},{3,14},{4,9},{5,8},{6,11},{7,10},{8,5},{9,4},... | collective-permute-start | bytes 110600 | tf_op jit(solution)/shard_map/ppermute | solution.py:316
  5.6 4.3 %collective-permute-start.2 = (bf16[144,128]{1,0:T(8,128)(2,1)S(1)}, bf16[144,128]{1,0:T(8,128)(2,1)S(1)}, u32[]{:S(2)}, u32[]{:S(2)}) collective-permute-start(bf16[144,128]{1,0:T(8,128)(2,1)S(1)} %get-tuple-element.27), channel_id=1, source_target_pairs={{0,9},{1,8},{2,11},{3,10},{4,13},{5,12},{6,15},{7,14},{8,1},{9,0},... | collective-permute-start | bytes 110600 | tf_op jit(solution)/shard_map/ppermute | solution.py:316
  5.6 4.3 %collective-permute-start.1 = (bf16[144,128]{1,0:T(8,128)(2,1)S(1)}, bf16[144,128]{1,0:T(8,128)(2,1)S(1)}, u32[]{:S(2)}, u32[]{:S(2)}) collective-permute-start(bf16[144,128]{1,0:T(8,128)(2,1)S(1)} %get-tuple-element.27), channel_id=1, source_target_pairs={{0,5},{1,4},{2,7},{3,6},{4,1},{5,0},{6,3},{7,2},{8,13},{9,12},{10,... | collective-permute-start | bytes 110600 | tf_op jit(solution)/shard_map/ppermute | solution.py:316
  5.7 3.4 %collective-permute-start = (f32[8,128]{1,0:T(8,128)S(1)}, f32[8,128]{1,0:T(8,128)S(1)}, u32[]{:S(2)}, u32[]{:S(2)}) collective-permute-start(f32[8,128]{1,0:T(8,128)S(1)} %get-tuple-element.26.refs_0_.own_points), channel_id=1, source_target_pairs={{0,3},{1,2},{2,1},{3,0},{4,7},{5,6},{6,5},{7,4},{8,11},{9,10},{10,... | collective-permute-start | bytes 12296 | tf_op jit(solution)/shard_map/ppermute | solution.py:316
  10.0 1.9 %collective-permute-start.4 = (bf16[4,144,128]{2,1,0:T(8,128)(2,1)S(1)}, bf16[4,144,128]{2,1,0:T(8,128)(2,1)S(1)}, u32[]{:S(2)}, u32[]{:S(2)}) collective-permute-start(bf16[4,144,128]{2,1,0:T(8,128)(2,1)S(1)} %pad_maximum_fusion.refs_2_), channel_id=1, source_target_pairs={{0,1},{1,0},{2,3},{3,2},{4,5},{5,4},{6,7},{7,6},{8,9},{9,8},{10,11... | collective-permute-start | bytes 442376 | tf_op jit(solution)/shard_map/ppermute | solution.py:316
  13.3 5.5 %collective-permute-start.5 = (bf16[512,128]{1,0:T(8,128)(2,1)S(1)}, bf16[512,128]{1,0:T(8,128)(2,1)S(1)}, u32[]{:S(2)}, u32[]{:S(2)}) collective-permute-start(bf16[512,128]{1,0:T(8,128)(2,1)S(1)} %get-tuple-element.36), channel_id=1, source_target_pairs={{0,3},{1,2},{2,1},{3,0},{4,7},{5,6},{6,5},{7,4},{8,11},{9,10},{10,... | collective-permute-start | bytes 393224 | tf_op jit(solution)/shard_map/ppermute | solution.py:316
  19.4 1.4 %collective-permute-start.8 = (bf16[256,128]{1,0:T(8,128)(2,1)S(1)}, bf16[256,128]{1,0:T(8,128)(2,1)S(1)}, u32[]{:S(2)}, u32[]{:S(2)}) collective-permute-start(bf16[256,128]{1,0:T(8,128)(2,1)S(1)} %get-tuple-element.46), channel_id=1, source_target_pairs={{0,1},{1,0},{2,3},{3,2},{4,5},{5,4},{6,7},{7,6},{8,9},{9,8},{10,11... | collective-permute-start | bytes 196616 | tf_op jit(solution)/shard_map/ppermute | solution.py:316
  19.8 3.7 %collective-permute-start.6 = (bf16[256,128]{1,0:T(8,128)(2,1)S(1)}, bf16[256,128]{1,0:T(8,128)(2,1)S(1)}, u32[]{:S(2)}, u32[]{:S(2)}) collective-permute-start(bf16[256,128]{1,0:T(8,128)(2,1)S(1)} %get-tuple-element.43), channel_id=1, source_target_pairs={{0,1},{1,0},{2,3},{3,2},{4,5},{5,4},{6,7},{7,6},{8,9},{9,8},{10,11... | collective-permute-start | bytes 196616 | tf_op jit(solution)/shard_map/ppermute | solution.py:316
  20.8 5.4 %collective-permute-start.9 = (bf16[256,128]{1,0:T(8,128)(2,1)S(1)}, bf16[256,128]{1,0:T(8,128)(2,1)S(1)}, u32[]{:S(2)}, u32[]{:S(2)}) collective-permute-start(bf16[256,128]{1,0:T(8,128)(2,1)S(1)} %shard_map.80), channel_id=1, source_target_pairs={{4,0},{6,2},{0,4},{2,6},{12,8},{14,10},{8,12},{10,14},{13,1},{15,3... | collective-permute-start | bytes 196616 | tf_op jit(solution)/shard_map/ppermute | solution.py:316
  23.5 4.3 %collective-permute-start.7 = (bf16[128,128]{1,0:T(8,128)(2,1)S(1)}, bf16[128,128]{1,0:T(8,128)(2,1)S(1)}, u32[]{:S(2)}, u32[]{:S(2)}) collective-permute-start(bf16[128,128]{1,0:T(8,128)(2,1)S(1)} %get-tuple-element.45), channel_id=1, source_target_pairs={{9,0},{8,1},{11,2},{10,3},{13,4},{12,5},{15,6},{14,7},{1,8},{0,9},... | collective-permute-start | bytes 98312 | tf_op jit(solution)/shard_map/ppermute | solution.py:316
  26.1 1.7 %collective-permute-start.10 = (bf16[128,128]{1,0:T(8,128)(2,1)S(1)}, bf16[128,128]{1,0:T(8,128)(2,1)S(1)}, u32[]{:S(2)}, u32[]{:S(2)}) collective-permute-start(bf16[128,128]{1,0:T(8,128)(2,1)S(1)} %slice.44), channel_id=1, source_target_pairs={{0,1},{1,0},{2,3},{3,2},{4,5},{5,4},{6,7},{7,6},{8,9},{9,8},{10,11... | collective-permute-start | bytes 98312 | tf_op jit(solution)/shard_map/ppermute | solution.py:316
